TPU v7x, 128 devices: a whole 4x4x4 slice. The times are simulated.
128 devices in a mesh: frame: 16 (over y, z), head: 8 (over x, core).
Axes of the slice: x: 4, y: 4, z: 4, core: 2. Of those that a mesh axis runs over, the one named last changes fastest.
Arguments:
- video_q: bfloat16 [16384, 3072], P(('frame', 'head'))
- video_k: bfloat16 [16384, 3072], P(('frame', 'head'))
- video_v: bfloat16 [16384, 3072], P(('frame', 'head')), may hold values from -6 to 6
- text_q: bfloat16 [256, 3072], P(None, 'head')
- text_k: bfloat16 [256, 3072], P(None, 'head'), may hold values from -6 to 6
- text_v: bfloat16 [256, 3072], P(None, 'head'), may hold values from -6 to 6
- block_mask: int32 [128, 128], replicated, may hold values from 0 to 1, as said below
- text_count: int32 [1], replicated, may hold values from 1 to 256
Outputs:
- video_out: bfloat16 [16384, 3072], P(('frame', 'head'))
- text_out: bfloat16 [256, 3072], P(None, 'head')
Inputs may be any that keep to these rules, and one draw needn't show every extreme that they name: block_mask is drawn at random with density falling with block distance; block_mask[i, j] is 1 where |i - j| <= 1 and 0 where |i - j| > 32; block_mask[0, 32] is 1.
All inputs are finite; a program needn't handle non-finite values.
Results may differ from a plain program's by a relative error of at most 0.0075.
Values may be sent and summed in bfloat16 or wider, within the bound.
No kernel may reach another device: no remote copies, remote signals or barrier semaphores. Data moves between devices by JAX's collectives and lax.ppermute only.
A program may use at most 64 MiB of HBM per device.

v0:
```python
import jax
import jax.numpy as jnp
from jax import lax
from jax.sharding import PartitionSpec as P

DH = 128
TEXT = 256
BLOCK = 128


neg_fill = -1e30


def as_sent(array):
    return jax.tree.map(lambda a: a.astype(jnp.bfloat16) if a.dtype == jnp.float32 else a, array)


def shifted(block, axis, distance):
    devices = range(lax.axis_size(axis))
    route = [((i - distance) % len(devices), i) for i in devices]
    return lax.ppermute(block, axis, route)


def combined_all(part, axis, combine):
    gathered = jax.tree.map(lambda a: lax.all_gather(a, axis), part)

    def take(source):
        return jax.tree.map(lambda a: lax.dynamic_index_in_dim(a, source, 0, False), gathered)

    return lax.fori_loop(
        1, lax.axis_size(axis), lambda source, state: combine(state, take(source)), take(0)
    )


def panel_update(state, queries, keys, values, keep):
    scale = DH ** (-0.5)

    def one_head(operands):
        query, key_h, value_h, run_max, run_sum, run_acc = operands
        scores = jnp.einsum("qd,kd->qk", query, key_h, preferred_element_type=jnp.float32) * scale
        scores = jnp.where(keep, scores, neg_fill)
        new_max = jnp.maximum(run_max, jnp.max(scores, axis=1))
        weights = jnp.where(keep, jnp.exp(scores - new_max[:, None]), 0.0)
        factor = jnp.exp(run_max - new_max)
        run_sum = run_sum * factor + jnp.sum(weights, axis=1)
        run_acc = run_acc * factor[:, None] + jnp.dot(
            weights.astype(jnp.bfloat16), value_h, preferred_element_type=jnp.float32
        )
        return (new_max, run_sum, run_acc)

    return lax.map(one_head, (queries, keys, values) + tuple(state))


def local(video_q, video_k, video_v, text_q, text_k, text_v, block_mask, text_count):
    heads_all = lax.axis_size("head")
    frames = lax.axis_size("frame")
    frame_id = lax.axis_index("frame")
    tok_dev, width = video_q.shape
    local_width = width // heads_all
    head_dev = local_width // DH
    group = tok_dev * heads_all
    blocks = group // BLOCK

    def to_heads(x):
        return x.reshape(tok_dev, heads_all, local_width)

    def split(x, rows):
        return x.reshape(rows, head_dev, DH).transpose(1, 0, 2)

    queries, keys, values = (
        lax.all_to_all(to_heads(video_q), "head", split_axis=1, concat_axis=0, tiled=True),
        lax.all_to_all(to_heads(video_k), "head", split_axis=1, concat_axis=0, tiled=True),
        lax.all_to_all(to_heads(video_v), "head", split_axis=1, concat_axis=0, tiled=True),
    )
    queries, keys, values = (split(queries, group), split(keys, group), split(values, group))
    text_query, text_keys, text_values = (
        split(text_q, TEXT),
        split(text_k, TEXT),
        split(text_v, TEXT),
    )
    live = jnp.arange(TEXT) < text_count[0]
    my_rows = lax.dynamic_slice_in_dim(block_mask, frame_id * blocks, blocks, 0)

    def keep_for(source):
        cols = lax.dynamic_slice_in_dim(my_rows, source * blocks, blocks, 1) > 0
        return jnp.repeat(jnp.repeat(cols, BLOCK, 0), BLOCK, 1) & True

    state = (
        jnp.full((head_dev, group), neg_fill, jnp.float32),
        jnp.zeros((head_dev, group), jnp.float32),
        jnp.zeros((head_dev, group, DH), jnp.float32),
    )
    state = panel_update(
        state, queries, text_keys, text_values, jnp.broadcast_to(live[None, :], (group, TEXT))
    )
    state = panel_update(state, queries, keys, values, keep_for(frame_id))

    def step_one(index, carry):
        panel, inner = carry
        panel = jax.tree.map(
            lambda part, own: part.astype(own.dtype), shifted(as_sent(panel), "frame", 1), panel
        )
        source = (frame_id - index) % frames
        inner = panel_update(inner, queries, panel[0], panel[1], keep_for(source))
        return (panel, inner)

    _, state = lax.fori_loop(1, frames, step_one, ((keys, values), state))
    video_local = (state[2] / state[1][:, :, None]).astype(jnp.bfloat16)
    video_local = video_local.transpose(1, 0, 2).reshape(group, local_width)
    video_out = lax.all_to_all(video_local, "head", split_axis=0, concat_axis=1, tiled=True)
    scale = DH ** (-0.5)

    def text_part(operands):
        query, key_h, value_h = operands
        scores = jnp.einsum("qd,kd->qk", query, key_h, preferred_element_type=jnp.float32) * scale
        top = jnp.max(scores, axis=1)
        weights = jnp.exp(scores - top[:, None])
        return (
            top,
            jnp.sum(weights, axis=1),
            jnp.dot(weights.astype(jnp.bfloat16), value_h, preferred_element_type=jnp.float32),
        )

    partial_text = lax.map(text_part, (text_query, keys, values))

    def combine(first, second):
        top = jnp.maximum(first[0], second[0])
        scale_a = jnp.exp(first[0] - top)
        scale_b = jnp.exp(second[0] - top)
        return (
            top,
            first[1] * scale_a + second[1] * scale_b,
            first[2] * scale_a[:, :, None] + second[2] * scale_b[:, :, None],
        )

    merged = combined_all(partial_text, "frame", combine)
    text_state = panel_update(
        merged, text_query, text_keys, text_values, jnp.broadcast_to(live[None, :], (TEXT, TEXT))
    )
    text_out = (text_state[2] / text_state[1][:, :, None]).astype(jnp.bfloat16)
    text_out = text_out.transpose(1, 0, 2).reshape(TEXT, local_width)
    return (video_out, text_out)


def solution(mesh):
    in_specs = (
        P(("frame", "head"), None),
        P(("frame", "head"), None),
        P(("frame", "head"), None),
        P(None, "head"),
        P(None, "head"),
        P(None, "head"),
        P(),
        P(),
    )
    out_specs = (P(("frame", "head"), None), P(None, "head"))
    return jax.shard_map(local, mesh=mesh, in_specs=in_specs, out_specs=out_specs, check_vma=False)
```

profile of v0, /device:TPU:8, one launch (start us, length us, event | category | flops | bytes accessed | tf_op | source)
XLA Modules:
  0.0 907.4 jit_solution(2085115832123817814)
XLA Ops:
  15.2 12.0 %all-to-all-done = bf16[128,8,384]{0,2,1:T(8,128)(2,1)S(1)} async-done(((bf16[128,8,384]{0,2,1:T(8,128)(2,1)}), bf16[128,8,384]{0,2,1:T(8,128)(2,1)S(1)}, u32[]{:S(2)}, u32[]{:S(2)}) %all-to-all-start) | async-done | bytes 786464 | tf_op jit(solution)/shard_map/all_to_all | solution.py:72
  70.5 14.8 %while.140 = (s32[]{:T(128)}, f32[3,1024]{1,0:T(4,128)S(1)}, f32[3,1024]{1,0:T(4,128)S(1)}, f32[3,1024,128]{2,1,0:T(8,128)S(1)}, f32[3,1024]{1,0:T(4,128)S(1)}, ...) while((s32[]{:T(128)}, f32[3,1024]{1,0:T(4,128)S(1)}, ...), condition=%wide.region_7.8_spmd.clone, body=%wide.region_4.7_spmd.clone.sunk | while | flops 546574336 | bytes 14518413 | solution.py:51
  85.2 714.5 %while.136 = (s32[]{:T(128)}, bf16[3,1024,128]{2,1,0:T(8,128)(2,1)}, bf16[3,1024,128]{2,1,0:T(8,128)(2,1)S(1)}, f32[3,1024]{1,0:T(4,128)S(1)}, f32[3,1024]{1,0:T...) while((s32[]{:T(128)}, bf16[3,1024,128]{2,1,0:T(8,128)(2,1)}, ...), condition=%wide.region_13.14_spmd, body=%wide.region_8.13_spmd.sunk | while | flops 546574400 | bytes 28158980 | solution.py:107
  90.1 30.2 %collective-permute-done = bf16[3,1024,128]{2,1,0:T(8,128)(2,1)S(1)} collective-permute-done((bf16[3,1024,128]{2,1,0:T(8,128)(2,1)}, bf16[3,1024,128]{2,1,0:T(8,128)(2,1)S(1)}, u32[]{:S(2)}, u32[]{:S(2)}) %collective-permute-start) | collective-permute-done | bytes 786464 | tf_op jit(solution)/shard_map/while/body/eval_jaxpr/ppermute | solution.py:21
  120.4 29.4 %collective-permute-done.1 = bf16[3,1024,128]{2,1,0:T(8,128)(2,1)S(1)} collective-permute-done((bf16[3,1024,128]{2,1,0:T(8,128)(2,1)}, bf16[3,1024,128]{2,1,0:T(8,128)(2,1)S(1)}, u32[]{:S(2)}, u32[]{:S(2)}) %collective-permute-start.1) | collective-permute-done | bytes 786464 | tf_op jit(solution)/shard_map/while/body/eval_jaxpr/ppermute | solution.py:21
  149.8 11.6 %while.142 = (s32[]{:T(128)}, f32[3,1024]{1,0:T(4,128)S(1)}, f32[3,1024]{1,0:T(4,128)S(1)}, f32[3,1024,128]{2,1,0:T(8,128)S(1)}, bf16[3,1024,128]{2,1,0:T(8,128)...) while((s32[]{:T(128)}, f32[3,1024]{1,0:T(4,128)S(1)}, ...), condition=%wide.region_12.12_spmd.clone.clone, body=%wide.region_9.11_spmd.clone.clone.sunk | while | flops 546574336 | bytes 15566969 | solution.py:51
  165.0 21.0 %collective-permute-done = bf16[3,1024,128]{2,1,0:T(8,128)(2,1)S(1)} collective-permute-done((bf16[3,1024,128]{2,1,0:T(8,128)(2,1)}, bf16[3,1024,128]{2,1,0:T(8,128)(2,1)S(1)}, u32[]{:S(2)}, u32[]{:S(2)}) %collective-permute-start) | collective-permute-done | bytes 786464 | tf_op jit(solution)/shard_map/while/body/eval_jaxpr/ppermute | solution.py:21
  186.0 14.7 %collective-permute-done.1 = bf16[3,1024,128]{2,1,0:T(8,128)(2,1)S(1)} collective-permute-done((bf16[3,1024,128]{2,1,0:T(8,128)(2,1)}, bf16[3,1024,128]{2,1,0:T(8,128)(2,1)S(1)}, u32[]{:S(2)}, u32[]{:S(2)}) %collective-permute-start.1) | collective-permute-done | bytes 786464 | tf_op jit(solution)/shard_map/while/body/eval_jaxpr/ppermute | solution.py:21
  200.7 11.6 %while.142 = (s32[]{:T(128)}, f32[3,1024]{1,0:T(4,128)S(1)}, f32[3,1024]{1,0:T(4,128)S(1)}, f32[3,1024,128]{2,1,0:T(8,128)S(1)}, bf16[3,1024,128]{2,1,0:T(8,128)...) while((s32[]{:T(128)}, f32[3,1024]{1,0:T(4,128)S(1)}, ...), condition=%wide.region_12.12_spmd.clone.clone, body=%wide.region_9.11_spmd.clone.clone.sunk | while | flops 546574336 | bytes 15566969 | solution.py:51
  214.3 22.6 %collective-permute-done = bf16[3,1024,128]{2,1,0:T(8,128)(2,1)S(1)} collective-permute-done((bf16[3,1024,128]{2,1,0:T(8,128)(2,1)}, bf16[3,1024,128]{2,1,0:T(8,128)(2,1)S(1)}, u32[]{:S(2)}, u32[]{:S(2)}) %collective-permute-start) | collective-permute-done | bytes 786464 | tf_op jit(solution)/shard_map/while/body/eval_jaxpr/ppermute | solution.py:21
  236.9 13.7 %collective-permute-done.1 = bf16[3,1024,128]{2,1,0:T(8,128)(2,1)S(1)} collective-permute-done((bf16[3,1024,128]{2,1,0:T(8,128)(2,1)}, bf16[3,1024,128]{2,1,0:T(8,128)(2,1)S(1)}, u32[]{:S(2)}, u32[]{:S(2)}) %collective-permute-start.1) | collective-permute-done | bytes 786464 | tf_op jit(solution)/shard_map/while/body/eval_jaxpr/ppermute | solution.py:21
  250.7 11.6 %while.142 = (s32[]{:T(128)}, f32[3,1024]{1,0:T(4,128)S(1)}, f32[3,1024]{1,0:T(4,128)S(1)}, f32[3,1024,128]{2,1,0:T(8,128)S(1)}, bf16[3,1024,128]{2,1,0:T(8,128)...) while((s32[]{:T(128)}, f32[3,1024]{1,0:T(4,128)S(1)}, ...), condition=%wide.region_12.12_spmd.clone.clone, body=%wide.region_9.11_spmd.clone.clone.sunk | while | flops 546574336 | bytes 15566969 | solution.py:51
  264.3 22.6 %collective-permute-done = bf16[3,1024,128]{2,1,0:T(8,128)(2,1)S(1)} collective-permute-done((bf16[3,1024,128]{2,1,0:T(8,128)(2,1)}, bf16[3,1024,128]{2,1,0:T(8,128)(2,1)S(1)}, u32[]{:S(2)}, u32[]{:S(2)}) %collective-permute-start) | collective-permute-done | bytes 786464 | tf_op jit(solution)/shard_map/while/body/eval_jaxpr/ppermute | solution.py:21
  286.9 12.8 %collective-permute-done.1 = bf16[3,1024,128]{2,1,0:T(8,128)(2,1)S(1)} collective-permute-done((bf16[3,1024,128]{2,1,0:T(8,128)(2,1)}, bf16[3,1024,128]{2,1,0:T(8,128)(2,1)S(1)}, u32[]{:S(2)}, u32[]{:S(2)}) %collective-permute-start.1) | collective-permute-done | bytes 786464 | tf_op jit(solution)/shard_map/while/body/eval_jaxpr/ppermute | solution.py:21
  299.7 11.6 %while.142 = (s32[]{:T(128)}, f32[3,1024]{1,0:T(4,128)S(1)}, f32[3,1024]{1,0:T(4,128)S(1)}, f32[3,1024,128]{2,1,0:T(8,128)S(1)}, bf16[3,1024,128]{2,1,0:T(8,128)...) while((s32[]{:T(128)}, f32[3,1024]{1,0:T(4,128)S(1)}, ...), condition=%wide.region_12.12_spmd.clone.clone, body=%wide.region_9.11_spmd.clone.clone.sunk | while | flops 546574336 | bytes 15566969 | solution.py:51
  313.3 22.6 %collective-permute-done = bf16[3,1024,128]{2,1,0:T(8,128)(2,1)S(1)} collective-permute-done((bf16[3,1024,128]{2,1,0:T(8,128)(2,1)}, bf16[3,1024,128]{2,1,0:T(8,128)(2,1)S(1)}, u32[]{:S(2)}, u32[]{:S(2)}) %collective-permute-start) | collective-permute-done | bytes 786464 | tf_op jit(solution)/shard_map/while/body/eval_jaxpr/ppermute | solution.py:21
  336.0 11.9 %collective-permute-done.1 = bf16[3,1024,128]{2,1,0:T(8,128)(2,1)S(1)} collective-permute-done((bf16[3,1024,128]{2,1,0:T(8,128)(2,1)}, bf16[3,1024,128]{2,1,0:T(8,128)(2,1)S(1)}, u32[]{:S(2)}, u32[]{:S(2)}) %collective-permute-start.1) | collective-permute-done | bytes 786464 | tf_op jit(solution)/shard_map/while/body/eval_jaxpr/ppermute | solution.py:21
  347.8 11.6 %while.142 = (s32[]{:T(128)}, f32[3,1024]{1,0:T(4,128)S(1)}, f32[3,1024]{1,0:T(4,128)S(1)}, f32[3,1024,128]{2,1,0:T(8,128)S(1)}, bf16[3,1024,128]{2,1,0:T(8,128)...) while((s32[]{:T(128)}, f32[3,1024]{1,0:T(4,128)S(1)}, ...), condition=%wide.region_12.12_spmd.clone.clone, body=%wide.region_9.11_spmd.clone.clone.sunk | while | flops 546574336 | bytes 15566969 | solution.py:51
  361.4 22.6 %collective-permute-done = bf16[3,1024,128]{2,1,0:T(8,128)(2,1)S(1)} collective-permute-done((bf16[3,1024,128]{2,1,0:T(8,128)(2,1)}, bf16[3,1024,128]{2,1,0:T(8,128)(2,1)S(1)}, u32[]{:S(2)}, u32[]{:S(2)}) %collective-permute-start) | collective-permute-done | bytes 786464 | tf_op jit(solution)/shard_map/while/body/eval_jaxpr/ppermute | solution.py:21
  384.1 10.9 %collective-permute-done.1 = bf16[3,1024,128]{2,1,0:T(8,128)(2,1)S(1)} collective-permute-done((bf16[3,1024,128]{2,1,0:T(8,128)(2,1)}, bf16[3,1024,128]{2,1,0:T(8,128)(2,1)S(1)}, u32[]{:S(2)}, u32[]{:S(2)}) %collective-permute-start.1) | collective-permute-done | bytes 786464 | tf_op jit(solution)/shard_map/while/body/eval_jaxpr/ppermute | solution.py:21
  395.0 11.6 %while.142 = (s32[]{:T(128)}, f32[3,1024]{1,0:T(4,128)S(1)}, f32[3,1024]{1,0:T(4,128)S(1)}, f32[3,1024,128]{2,1,0:T(8,128)S(1)}, bf16[3,1024,128]{2,1,0:T(8,128)...) while((s32[]{:T(128)}, f32[3,1024]{1,0:T(4,128)S(1)}, ...), condition=%wide.region_12.12_spmd.clone.clone, body=%wide.region_9.11_spmd.clone.clone.sunk | while | flops 546574336 | bytes 15566969 | solution.py:51
  408.6 22.6 %collective-permute-done = bf16[3,1024,128]{2,1,0:T(8,128)(2,1)S(1)} collective-permute-done((bf16[3,1024,128]{2,1,0:T(8,128)(2,1)}, bf16[3,1024,128]{2,1,0:T(8,128)(2,1)S(1)}, u32[]{:S(2)}, u32[]{:S(2)}) %collective-permute-start) | collective-permute-done | bytes 786464 | tf_op jit(solution)/shard_map/while/body/eval_jaxpr/ppermute | solution.py:21
  431.3 10.0 %collective-permute-done.1 = bf16[3,1024,128]{2,1,0:T(8,128)(2,1)S(1)} collective-permute-done((bf16[3,1024,128]{2,1,0:T(8,128)(2,1)}, bf16[3,1024,128]{2,1,0:T(8,128)(2,1)S(1)}, u32[]{:S(2)}, u32[]{:S(2)}) %collective-permute-start.1) | collective-permute-done | bytes 786464 | tf_op jit(solution)/shard_map/while/body/eval_jaxpr/ppermute | solution.py:21
  441.3 11.6 %while.142 = (s32[]{:T(128)}, f32[3,1024]{1,0:T(4,128)S(1)}, f32[3,1024]{1,0:T(4,128)S(1)}, f32[3,1024,128]{2,1,0:T(8,128)S(1)}, bf16[3,1024,128]{2,1,0:T(8,128)...) while((s32[]{:T(128)}, f32[3,1024]{1,0:T(4,128)S(1)}, ...), condition=%wide.region_12.12_spmd.clone.clone, body=%wide.region_9.11_spmd.clone.clone.sunk | while | flops 546574336 | bytes 15566969 | solution.py:51
  454.9 22.6 %collective-permute-done = bf16[3,1024,128]{2,1,0:T(8,128)(2,1)S(1)} collective-permute-done((bf16[3,1024,128]{2,1,0:T(8,128)(2,1)}, bf16[3,1024,128]{2,1,0:T(8,128)(2,1)S(1)}, u32[]{:S(2)}, u32[]{:S(2)}) %collective-permute-start) | collective-permute-done | bytes 786464 | tf_op jit(solution)/shard_map/while/body/eval_jaxpr/ppermute | solution.py:21
  477.6 9.1 %collective-permute-done.1 = bf16[3,1024,128]{2,1,0:T(8,128)(2,1)S(1)} collective-permute-done((bf16[3,1024,128]{2,1,0:T(8,128)(2,1)}, bf16[3,1024,128]{2,1,0:T(8,128)(2,1)S(1)}, u32[]{:S(2)}, u32[]{:S(2)}) %collective-permute-start.1) | collective-permute-done | bytes 786464 | tf_op jit(solution)/shard_map/while/body/eval_jaxpr/ppermute | solution.py:21
  486.7 11.6 %while.142 = (s32[]{:T(128)}, f32[3,1024]{1,0:T(4,128)S(1)}, f32[3,1024]{1,0:T(4,128)S(1)}, f32[3,1024,128]{2,1,0:T(8,128)S(1)}, bf16[3,1024,128]{2,1,0:T(8,128)...) while((s32[]{:T(128)}, f32[3,1024]{1,0:T(4,128)S(1)}, ...), condition=%wide.region_12.12_spmd.clone.clone, body=%wide.region_9.11_spmd.clone.clone.sunk | while | flops 546574336 | bytes 15566969 | solution.py:51
  500.3 22.6 %collective-permute-done = bf16[3,1024,128]{2,1,0:T(8,128)(2,1)S(1)} collective-permute-done((bf16[3,1024,128]{2,1,0:T(8,128)(2,1)}, bf16[3,1024,128]{2,1,0:T(8,128)(2,1)S(1)}, u32[]{:S(2)}, u32[]{:S(2)}) %collective-permute-start) | collective-permute-done | bytes 786464 | tf_op jit(solution)/shard_map/while/body/eval_jaxpr/ppermute | solution.py:21
  522.9 8.4 collective-permute-done.1
  531.3 11.6 %while.142 = (s32[]{:T(128)}, f32[3,1024]{1,0:T(4,128)S(1)}, f32[3,1024]{1,0:T(4,128)S(1)}, f32[3,1024,128]{2,1,0:T(8,128)S(1)}, bf16[3,1024,128]{2,1,0:T(8,128)...) while((s32[]{:T(128)}, f32[3,1024]{1,0:T(4,128)S(1)}, ...), condition=%wide.region_12.12_spmd.clone.clone, body=%wide.region_9.11_spmd.clone.clone.sunk | while | flops 546574336 | bytes 15566969 | solution.py:51
  544.9 22.7 %collective-permute-done = bf16[3,1024,128]{2,1,0:T(8,128)(2,1)S(1)} collective-permute-done((bf16[3,1024,128]{2,1,0:T(8,128)(2,1)}, bf16[3,1024,128]{2,1,0:T(8,128)(2,1)S(1)}, u32[]{:S(2)}, u32[]{:S(2)}) %collective-permute-start) | collective-permute-done | bytes 786464 | tf_op jit(solution)/shard_map/while/body/eval_jaxpr/ppermute | solution.py:21
  567.7 8.6 collective-permute-done.1
  576.3 11.6 %while.142 = (s32[]{:T(128)}, f32[3,1024]{1,0:T(4,128)S(1)}, f32[3,1024]{1,0:T(4,128)S(1)}, f32[3,1024,128]{2,1,0:T(8,128)S(1)}, bf16[3,1024,128]{2,1,0:T(8,128)...) while((s32[]{:T(128)}, f32[3,1024]{1,0:T(4,128)S(1)}, ...), condition=%wide.region_12.12_spmd.clone.clone, body=%wide.region_9.11_spmd.clone.clone.sunk | while | flops 546574336 | bytes 15566969 | solution.py:51
  589.9 22.0 %collective-permute-done = bf16[3,1024,128]{2,1,0:T(8,128)(2,1)S(1)} collective-permute-done((bf16[3,1024,128]{2,1,0:T(8,128)(2,1)}, bf16[3,1024,128]{2,1,0:T(8,128)(2,1)S(1)}, u32[]{:S(2)}, u32[]{:S(2)}) %collective-permute-start) | collective-permute-done | bytes 786464 | tf_op jit(solution)/shard_map/while/body/eval_jaxpr/ppermute | solution.py:21
  620.3 11.6 %while.142 = (s32[]{:T(128)}, f32[3,1024]{1,0:T(4,128)S(1)}, f32[3,1024]{1,0:T(4,128)S(1)}, f32[3,1024,128]{2,1,0:T(8,128)S(1)}, bf16[3,1024,128]{2,1,0:T(8,128)...) while((s32[]{:T(128)}, f32[3,1024]{1,0:T(4,128)S(1)}, ...), condition=%wide.region_12.12_spmd.clone.clone, body=%wide.region_9.11_spmd.clone.clone.sunk | while | flops 546574336 | bytes 15566969 | solution.py:51
  633.9 21.1 %collective-permute-done = bf16[3,1024,128]{2,1,0:T(8,128)(2,1)S(1)} collective-permute-done((bf16[3,1024,128]{2,1,0:T(8,128)(2,1)}, bf16[3,1024,128]{2,1,0:T(8,128)(2,1)S(1)}, u32[]{:S(2)}, u32[]{:S(2)}) %collective-permute-start) | collective-permute-done | bytes 786464 | tf_op jit(solution)/shard_map/while/body/eval_jaxpr/ppermute | solution.py:21
  655.0 8.4 collective-permute-done.1
  663.4 11.6 %while.142 = (s32[]{:T(128)}, f32[3,1024]{1,0:T(4,128)S(1)}, f32[3,1024]{1,0:T(4,128)S(1)}, f32[3,1024,128]{2,1,0:T(8,128)S(1)}, bf16[3,1024,128]{2,1,0:T(8,128)...) while((s32[]{:T(128)}, f32[3,1024]{1,0:T(4,128)S(1)}, ...), condition=%wide.region_12.12_spmd.clone.clone, body=%wide.region_9.11_spmd.clone.clone.sunk | while | flops 546574336 | bytes 15566969 | solution.py:51
  677.0 20.1 %collective-permute-done = bf16[3,1024,128]{2,1,0:T(8,128)(2,1)S(1)} collective-permute-done((bf16[3,1024,128]{2,1,0:T(8,128)(2,1)}, bf16[3,1024,128]{2,1,0:T(8,128)(2,1)S(1)}, u32[]{:S(2)}, u32[]{:S(2)}) %collective-permute-start) | collective-permute-done | bytes 786464 | tf_op jit(solution)/shard_map/while/body/eval_jaxpr/ppermute | solution.py:21
  705.6 11.6 %while.142 = (s32[]{:T(128)}, f32[3,1024]{1,0:T(4,128)S(1)}, f32[3,1024]{1,0:T(4,128)S(1)}, f32[3,1024,128]{2,1,0:T(8,128)S(1)}, bf16[3,1024,128]{2,1,0:T(8,128)...) while((s32[]{:T(128)}, f32[3,1024]{1,0:T(4,128)S(1)}, ...), condition=%wide.region_12.12_spmd.clone.clone, body=%wide.region_9.11_spmd.clone.clone.sunk | while | flops 546574336 | bytes 15566969 | solution.py:51
  719.2 19.2 %collective-permute-done = bf16[3,1024,128]{2,1,0:T(8,128)(2,1)S(1)} collective-permute-done((bf16[3,1024,128]{2,1,0:T(8,128)(2,1)}, bf16[3,1024,128]{2,1,0:T(8,128)(2,1)S(1)}, u32[]{:S(2)}, u32[]{:S(2)}) %collective-permute-start) | collective-permute-done | bytes 786464 | tf_op jit(solution)/shard_map/while/body/eval_jaxpr/ppermute | solution.py:21
  746.9 11.6 %while.142 = (s32[]{:T(128)}, f32[3,1024]{1,0:T(4,128)S(1)}, f32[3,1024]{1,0:T(4,128)S(1)}, f32[3,1024,128]{2,1,0:T(8,128)S(1)}, bf16[3,1024,128]{2,1,0:T(8,128)...) while((s32[]{:T(128)}, f32[3,1024]{1,0:T(4,128)S(1)}, ...), condition=%wide.region_12.12_spmd.clone.clone, body=%wide.region_9.11_spmd.clone.clone.sunk | while | flops 546574336 | bytes 15566969 | solution.py:51
  760.5 18.3 %collective-permute-done = bf16[3,1024,128]{2,1,0:T(8,128)(2,1)S(1)} collective-permute-done((bf16[3,1024,128]{2,1,0:T(8,128)(2,1)}, bf16[3,1024,128]{2,1,0:T(8,128)(2,1)S(1)}, u32[]{:S(2)}, u32[]{:S(2)}) %collective-permute-start) | collective-permute-done | bytes 786464 | tf_op jit(solution)/shard_map/while/body/eval_jaxpr/ppermute | solution.py:21
  787.2 11.6 %while.142 = (s32[]{:T(128)}, f32[3,1024]{1,0:T(4,128)S(1)}, f32[3,1024]{1,0:T(4,128)S(1)}, f32[3,1024,128]{2,1,0:T(8,128)S(1)}, bf16[3,1024,128]{2,1,0:T(8,128)...) while((s32[]{:T(128)}, f32[3,1024]{1,0:T(4,128)S(1)}, ...), condition=%wide.region_12.12_spmd.clone.clone, body=%wide.region_9.11_spmd.clone.clone.sunk | while | flops 546574336 | bytes 15566969 | solution.py:51
  801.7 11.2 %all-to-all-start.3 = ((bf16[8,128,384]{1,2,0:T(8,128)(2,1)}), bf16[8,128,384]{1,2,0:T(8,128)(2,1)S(1)}, u32[]{:S(2)}, u32[]{:S(2)}) async-start(bf16[8,128,384]{1,2,0:T(8,128)(2,1)} %copy.79), calls=%async_computation.3 | async-start | bytes 1572864 | tf_op jit(solution)/shard_map/all_to_all | solution.py:110
  812.9 35.1 %all-gather.4 = f32[16,3,256]{2,1,0:T(4,128)S(1)} all-gather(f32[1,3,256]{2,1,0:T(4,128)S(1)} %bitcast.328), channel_id=3, replica_groups=mesh['frame'=16,'head'=8] {'frame'}, dimensions={0}, use_global_device_ids=true | all-gather | bytes 52224 | tf_op jit(solution)/shard_map/all_gather | solution.py:25
  848.0 20.6 %all-gather.3 = f32[16,3,256]{2,1,0:T(4,128)S(1)} all-gather(f32[1,3,256]{2,1,0:T(4,128)S(1)} %bitcast.327), channel_id=2, replica_groups=mesh['frame'=16,'head'=8] {'frame'}, dimensions={0}, use_global_device_ids=true | all-gather | bytes 52224 | tf_op jit(solution)/shard_map/all_gather | solution.py:25
  870.8 21.1 %while.138 = (s32[]{:T(128)}, f32[3,256]{1,0:T(4,128)S(1)}, f32[3,256]{1,0:T(4,128)S(1)}, f32[3,256,128]{2,1,0:T(8,128)S(1)}, f32[16,3,256]{2,1,0:T(4,128)S(1)},...) while((s32[]{:T(128)}, f32[3,256]{1,0:T(4,128)S(1)}, ...), condition=%wide.region_19.20_spmd, body=%wide.region_18.19_spmd.sunk | while | flops 299525 | bytes 1210519 | solution.py:30
  (731 shorter events, 360.2 us)
Async XLA Ops:
  7.2 6.8 copy-start.5
  9.5 21.2 %copy-start.9 = (bf16[256,384]{1,0:T(8,128)(2,1)S(1)}, bf16[256,384]{1,0:T(8,128)(2,1)}, u32[]{:S(2)}) copy-start(bf16[256,384]{1,0:T(8,128)(2,1)} %param.25) | copy-start | bytes 589828
  9.5 17.6 %all-to-all-start = ((bf16[128,8,384]{0,2,1:T(8,128)(2,1)}), bf16[128,8,384]{0,2,1:T(8,128)(2,1)S(1)}, u32[]{:S(2)}, u32[]{:S(2)}) async-start(bf16[128,8,384]{0,2,1:T(8,128)(2,1)} %bitcast.10), calls=%async_computation | async-start | bytes 1572864 | tf_op jit(solution)/shard_map/all_to_all | solution.py:72
  14.0 17.0 %copy-start.10 = (bf16[256,384]{1,0:T(8,128)(2,1)S(1)}, bf16[256,384]{1,0:T(8,128)(2,1)}, u32[]{:S(2)}) copy-start(bf16[256,384]{1,0:T(8,128)(2,1)} %param.26) | copy-start | bytes 589828
  14.0 17.4 %copy-start.11 = (bf16[256,384]{1,0:T(8,128)(2,1)S(1)}, bf16[256,384]{1,0:T(8,128)(2,1)}, u32[]{:S(2)}) copy-start(bf16[256,384]{1,0:T(8,128)(2,1)} %param.27) | copy-start | bytes 589828
  15.2 17.2 %copy-start.6 = (bf16[128,3072]{1,0:T(8,128)(2,1)S(1)}, bf16[128,3072]{1,0:T(8,128)(2,1)}, u32[]{:S(2)}) copy-start(bf16[128,3072]{1,0:T(8,128)(2,1)} %param.22) | copy-start | bytes 2359300
  27.1 16.6 %all-to-all-start.1 = ((bf16[128,8,384]{0,2,1:T(8,128)(2,1)}), bf16[128,8,384]{0,2,1:T(8,128)(2,1)S(1)}, u32[]{:S(2)}, u32[]{:S(2)}) async-start(bf16[128,8,384]{0,2,1:T(8,128)(2,1)} %bitcast.14), calls=%async_computation.1 | async-start | bytes 1572864 | tf_op jit(solution)/shard_map/all_to_all | solution.py:73
  43.8 16.6 %all-to-all-start.2 = ((bf16[128,8,384]{0,2,1:T(8,128)(2,1)}), bf16[128,8,384]{0,2,1:T(8,128)(2,1)S(1)}, u32[]{:S(2)}, u32[]{:S(2)}) async-start(bf16[128,8,384]{0,2,1:T(8,128)(2,1)} %bitcast.18), calls=%async_computation.2 | async-start | bytes 1572864 | tf_op jit(solution)/shard_map/all_to_all | solution.py:71
  47.3 822.4 %all-gather.7.cloned.1.call-start = ((), (), s32[]{:S(2)}) async-start(), calls=%async_computation.4 | async-start | bytes 6684672 | tf_op jit(solution)/shard_map/all_gather | solution.py:25
  59.0 2.2 copy-start.3
  59.1 2.2 copy-start.12
  59.1 2.2 copy-start.14
  69.2 1.3 copy-start.2
  69.2 1.3 copy-start.4
  86.2 34.2 %collective-permute-start = (bf16[3,1024,128]{2,1,0:T(8,128)(2,1)}, bf16[3,1024,128]{2,1,0:T(8,128)(2,1)S(1)}, u32[]{:S(2)}, u32[]{:S(2)}) collective-permute-start(bf16[3,1024,128]{2,1,0:T(8,128)(2,1)} %get-tuple-element.1657), channel_id=1, source_target_pairs={{120,0},{0,8},{8,16},{16,24},{24,32},{32,40},{40,48},{48,56},{56,6... | collective-permute-start | bytes 2359304 | tf_op jit(solution)/shard_map/while/body/eval_jaxpr/ppermute | solution.py:21
  88.1 61.7 %collective-permute-start.1 = (bf16[3,1024,128]{2,1,0:T(8,128)(2,1)}, bf16[3,1024,128]{2,1,0:T(8,128)(2,1)S(1)}, u32[]{:S(2)}, u32[]{:S(2)}) collective-permute-start(bf16[3,1024,128]{2,1,0:T(8,128)(2,1)} %copy-done), channel_id=1, source_target_pairs={{120,0},{0,8},{8,16},{16,24},{24,32},{32,40},{40,48},{48,56},{56,6... | collective-permute-start | bytes 2359304 | tf_op jit(solution)/shard_map/while/body/eval_jaxpr/ppermute | solution.py:21
  163.2 22.8 %collective-permute-start = (bf16[3,1024,128]{2,1,0:T(8,128)(2,1)}, bf16[3,1024,128]{2,1,0:T(8,128)(2,1)S(1)}, u32[]{:S(2)}, u32[]{:S(2)}) collective-permute-start(bf16[3,1024,128]{2,1,0:T(8,128)(2,1)} %get-tuple-element.1657), channel_id=1, source_target_pairs={{120,0},{0,8},{8,16},{16,24},{24,32},{32,40},{40,48},{48,56},{56,6... | collective-permute-start | bytes 2359304 | tf_op jit(solution)/shard_map/while/body/eval_jaxpr/ppermute | solution.py:21
  163.2 37.4 %collective-permute-start.1 = (bf16[3,1024,128]{2,1,0:T(8,128)(2,1)}, bf16[3,1024,128]{2,1,0:T(8,128)(2,1)S(1)}, u32[]{:S(2)}, u32[]{:S(2)}) collective-permute-start(bf16[3,1024,128]{2,1,0:T(8,128)(2,1)} %copy-done), channel_id=1, source_target_pairs={{120,0},{0,8},{8,16},{16,24},{24,32},{32,40},{40,48},{48,56},{56,6... | collective-permute-start | bytes 2359304 | tf_op jit(solution)/shard_map/while/body/eval_jaxpr/ppermute | solution.py:21
  214.1 22.8 %collective-permute-start = (bf16[3,1024,128]{2,1,0:T(8,128)(2,1)}, bf16[3,1024,128]{2,1,0:T(8,128)(2,1)S(1)}, u32[]{:S(2)}, u32[]{:S(2)}) collective-permute-start(bf16[3,1024,128]{2,1,0:T(8,128)(2,1)} %get-tuple-element.1657), channel_id=1, source_target_pairs={{120,0},{0,8},{8,16},{16,24},{24,32},{32,40},{40,48},{48,56},{56,6... | collective-permute-start | bytes 2359304 | tf_op jit(solution)/shard_map/while/body/eval_jaxpr/ppermute | solution.py:21
  214.1 36.5 %collective-permute-start.1 = (bf16[3,1024,128]{2,1,0:T(8,128)(2,1)}, bf16[3,1024,128]{2,1,0:T(8,128)(2,1)S(1)}, u32[]{:S(2)}, u32[]{:S(2)}) collective-permute-start(bf16[3,1024,128]{2,1,0:T(8,128)(2,1)} %copy-done), channel_id=1, source_target_pairs={{120,0},{0,8},{8,16},{16,24},{24,32},{32,40},{40,48},{48,56},{56,6... | collective-permute-start | bytes 2359304 | tf_op jit(solution)/shard_map/while/body/eval_jaxpr/ppermute | solution.py:21
  264.1 22.8 %collective-permute-start = (bf16[3,1024,128]{2,1,0:T(8,128)(2,1)}, bf16[3,1024,128]{2,1,0:T(8,128)(2,1)S(1)}, u32[]{:S(2)}, u32[]{:S(2)}) collective-permute-start(bf16[3,1024,128]{2,1,0:T(8,128)(2,1)} %get-tuple-element.1657), channel_id=1, source_target_pairs={{120,0},{0,8},{8,16},{16,24},{24,32},{32,40},{40,48},{48,56},{56,6... | collective-permute-start | bytes 2359304 | tf_op jit(solution)/shard_map/while/body/eval_jaxpr/ppermute | solution.py:21
  264.1 35.6 %collective-permute-start.1 = (bf16[3,1024,128]{2,1,0:T(8,128)(2,1)}, bf16[3,1024,128]{2,1,0:T(8,128)(2,1)S(1)}, u32[]{:S(2)}, u32[]{:S(2)}) collective-permute-start(bf16[3,1024,128]{2,1,0:T(8,128)(2,1)} %copy-done), channel_id=1, source_target_pairs={{120,0},{0,8},{8,16},{16,24},{24,32},{32,40},{40,48},{48,56},{56,6... | collective-permute-start | bytes 2359304 | tf_op jit(solution)/shard_map/while/body/eval_jaxpr/ppermute | solution.py:21
  313.2 22.8 %collective-permute-start = (bf16[3,1024,128]{2,1,0:T(8,128)(2,1)}, bf16[3,1024,128]{2,1,0:T(8,128)(2,1)S(1)}, u32[]{:S(2)}, u32[]{:S(2)}) collective-permute-start(bf16[3,1024,128]{2,1,0:T(8,128)(2,1)} %get-tuple-element.1657), channel_id=1, source_target_pairs={{120,0},{0,8},{8,16},{16,24},{24,32},{32,40},{40,48},{48,56},{56,6... | collective-permute-start | bytes 2359304 | tf_op jit(solution)/shard_map/while/body/eval_jaxpr/ppermute | solution.py:21
  313.2 34.7 %collective-permute-start.1 = (bf16[3,1024,128]{2,1,0:T(8,128)(2,1)}, bf16[3,1024,128]{2,1,0:T(8,128)(2,1)S(1)}, u32[]{:S(2)}, u32[]{:S(2)}) collective-permute-start(bf16[3,1024,128]{2,1,0:T(8,128)(2,1)} %copy-done), channel_id=1, source_target_pairs={{120,0},{0,8},{8,16},{16,24},{24,32},{32,40},{40,48},{48,56},{56,6... | collective-permute-start | bytes 2359304 | tf_op jit(solution)/shard_map/while/body/eval_jaxpr/ppermute | solution.py:21
  361.3 22.8 %collective-permute-start = (bf16[3,1024,128]{2,1,0:T(8,128)(2,1)}, bf16[3,1024,128]{2,1,0:T(8,128)(2,1)S(1)}, u32[]{:S(2)}, u32[]{:S(2)}) collective-permute-start(bf16[3,1024,128]{2,1,0:T(8,128)(2,1)} %get-tuple-element.1657), channel_id=1, source_target_pairs={{120,0},{0,8},{8,16},{16,24},{24,32},{32,40},{40,48},{48,56},{56,6... | collective-permute-start | bytes 2359304 | tf_op jit(solution)/shard_map/while/body/eval_jaxpr/ppermute | solution.py:21
  361.3 33.7 %collective-permute-start.1 = (bf16[3,1024,128]{2,1,0:T(8,128)(2,1)}, bf16[3,1024,128]{2,1,0:T(8,128)(2,1)S(1)}, u32[]{:S(2)}, u32[]{:S(2)}) collective-permute-start(bf16[3,1024,128]{2,1,0:T(8,128)(2,1)} %copy-done), channel_id=1, source_target_pairs={{120,0},{0,8},{8,16},{16,24},{24,32},{32,40},{40,48},{48,56},{56,6... | collective-permute-start | bytes 2359304 | tf_op jit(solution)/shard_map/while/body/eval_jaxpr/ppermute | solution.py:21
  408.5 22.8 %collective-permute-start = (bf16[3,1024,128]{2,1,0:T(8,128)(2,1)}, bf16[3,1024,128]{2,1,0:T(8,128)(2,1)S(1)}, u32[]{:S(2)}, u32[]{:S(2)}) collective-permute-start(bf16[3,1024,128]{2,1,0:T(8,128)(2,1)} %get-tuple-element.1657), channel_id=1, source_target_pairs={{120,0},{0,8},{8,16},{16,24},{24,32},{32,40},{40,48},{48,56},{56,6... | collective-permute-start | bytes 2359304 | tf_op jit(solution)/shard_map/while/body/eval_jaxpr/ppermute | solution.py:21
  408.5 32.8 %collective-permute-start.1 = (bf16[3,1024,128]{2,1,0:T(8,128)(2,1)}, bf16[3,1024,128]{2,1,0:T(8,128)(2,1)S(1)}, u32[]{:S(2)}, u32[]{:S(2)}) collective-permute-start(bf16[3,1024,128]{2,1,0:T(8,128)(2,1)} %copy-done), channel_id=1, source_target_pairs={{120,0},{0,8},{8,16},{16,24},{24,32},{32,40},{40,48},{48,56},{56,6... | collective-permute-start | bytes 2359304 | tf_op jit(solution)/shard_map/while/body/eval_jaxpr/ppermute | solution.py:21
  454.8 22.8 %collective-permute-start = (bf16[3,1024,128]{2,1,0:T(8,128)(2,1)}, bf16[3,1024,128]{2,1,0:T(8,128)(2,1)S(1)}, u32[]{:S(2)}, u32[]{:S(2)}) collective-permute-start(bf16[3,1024,128]{2,1,0:T(8,128)(2,1)} %get-tuple-element.1657), channel_id=1, source_target_pairs={{120,0},{0,8},{8,16},{16,24},{24,32},{32,40},{40,48},{48,56},{56,6... | collective-permute-start | bytes 2359304 | tf_op jit(solution)/shard_map/while/body/eval_jaxpr/ppermute | solution.py:21
  454.8 31.9 %collective-permute-start.1 = (bf16[3,1024,128]{2,1,0:T(8,128)(2,1)}, bf16[3,1024,128]{2,1,0:T(8,128)(2,1)S(1)}, u32[]{:S(2)}, u32[]{:S(2)}) collective-permute-start(bf16[3,1024,128]{2,1,0:T(8,128)(2,1)} %copy-done), channel_id=1, source_target_pairs={{120,0},{0,8},{8,16},{16,24},{24,32},{32,40},{40,48},{48,56},{56,6... | collective-permute-start | bytes 2359304 | tf_op jit(solution)/shard_map/while/body/eval_jaxpr/ppermute | solution.py:21
  500.1 22.8 %collective-permute-start = (bf16[3,1024,128]{2,1,0:T(8,128)(2,1)}, bf16[3,1024,128]{2,1,0:T(8,128)(2,1)S(1)}, u32[]{:S(2)}, u32[]{:S(2)}) collective-permute-start(bf16[3,1024,128]{2,1,0:T(8,128)(2,1)} %get-tuple-element.1657), channel_id=1, source_target_pairs={{120,0},{0,8},{8,16},{16,24},{24,32},{32,40},{40,48},{48,56},{56,6... | collective-permute-start | bytes 2359304 | tf_op jit(solution)/shard_map/while/body/eval_jaxpr/ppermute | solution.py:21
  500.1 31.2 %collective-permute-start.1 = (bf16[3,1024,128]{2,1,0:T(8,128)(2,1)}, bf16[3,1024,128]{2,1,0:T(8,128)(2,1)S(1)}, u32[]{:S(2)}, u32[]{:S(2)}) collective-permute-start(bf16[3,1024,128]{2,1,0:T(8,128)(2,1)} %copy-done), channel_id=1, source_target_pairs={{120,0},{0,8},{8,16},{16,24},{24,32},{32,40},{40,48},{48,56},{56,6... | collective-permute-start | bytes 2359304 | tf_op jit(solution)/shard_map/while/body/eval_jaxpr/ppermute | solution.py:21
  544.8 22.9 %collective-permute-start = (bf16[3,1024,128]{2,1,0:T(8,128)(2,1)}, bf16[3,1024,128]{2,1,0:T(8,128)(2,1)S(1)}, u32[]{:S(2)}, u32[]{:S(2)}) collective-permute-start(bf16[3,1024,128]{2,1,0:T(8,128)(2,1)} %get-tuple-element.1657), channel_id=1, source_target_pairs={{120,0},{0,8},{8,16},{16,24},{24,32},{32,40},{40,48},{48,56},{56,6... | collective-permute-start | bytes 2359304 | tf_op jit(solution)/shard_map/while/body/eval_jaxpr/ppermute | solution.py:21
  544.8 31.5 %collective-permute-start.1 = (bf16[3,1024,128]{2,1,0:T(8,128)(2,1)}, bf16[3,1024,128]{2,1,0:T(8,128)(2,1)S(1)}, u32[]{:S(2)}, u32[]{:S(2)}) collective-permute-start(bf16[3,1024,128]{2,1,0:T(8,128)(2,1)} %copy-done), channel_id=1, source_target_pairs={{120,0},{0,8},{8,16},{16,24},{24,32},{32,40},{40,48},{48,56},{56,6... | collective-permute-start | bytes 2359304 | tf_op jit(solution)/shard_map/while/body/eval_jaxpr/ppermute | solution.py:21
  589.7 22.1 %collective-permute-start = (bf16[3,1024,128]{2,1,0:T(8,128)(2,1)}, bf16[3,1024,128]{2,1,0:T(8,128)(2,1)S(1)}, u32[]{:S(2)}, u32[]{:S(2)}) collective-permute-start(bf16[3,1024,128]{2,1,0:T(8,128)(2,1)} %get-tuple-element.1657), channel_id=1, source_target_pairs={{120,0},{0,8},{8,16},{16,24},{24,32},{32,40},{40,48},{48,56},{56,6... | collective-permute-start | bytes 2359304 | tf_op jit(solution)/shard_map/while/body/eval_jaxpr/ppermute | solution.py:21
  589.7 30.6 %collective-permute-start.1 = (bf16[3,1024,128]{2,1,0:T(8,128)(2,1)}, bf16[3,1024,128]{2,1,0:T(8,128)(2,1)S(1)}, u32[]{:S(2)}, u32[]{:S(2)}) collective-permute-start(bf16[3,1024,128]{2,1,0:T(8,128)(2,1)} %copy-done), channel_id=1, source_target_pairs={{120,0},{0,8},{8,16},{16,24},{24,32},{32,40},{40,48},{48,56},{56,6... | collective-permute-start | bytes 2359304 | tf_op jit(solution)/shard_map/while/body/eval_jaxpr/ppermute | solution.py:21
  633.8 21.2 %collective-permute-start = (bf16[3,1024,128]{2,1,0:T(8,128)(2,1)}, bf16[3,1024,128]{2,1,0:T(8,128)(2,1)S(1)}, u32[]{:S(2)}, u32[]{:S(2)}) collective-permute-start(bf16[3,1024,128]{2,1,0:T(8,128)(2,1)} %get-tuple-element.1657), channel_id=1, source_target_pairs={{120,0},{0,8},{8,16},{16,24},{24,32},{32,40},{40,48},{48,56},{56,6... | collective-permute-start | bytes 2359304 | tf_op jit(solution)/shard_map/while/body/eval_jaxpr/ppermute | solution.py:21
  633.8 29.7 %collective-permute-start.1 = (bf16[3,1024,128]{2,1,0:T(8,128)(2,1)}, bf16[3,1024,128]{2,1,0:T(8,128)(2,1)S(1)}, u32[]{:S(2)}, u32[]{:S(2)}) collective-permute-start(bf16[3,1024,128]{2,1,0:T(8,128)(2,1)} %copy-done), channel_id=1, source_target_pairs={{120,0},{0,8},{8,16},{16,24},{24,32},{32,40},{40,48},{48,56},{56,6... | collective-permute-start | bytes 2359304 | tf_op jit(solution)/shard_map/while/body/eval_jaxpr/ppermute | solution.py:21
  676.9 20.3 %collective-permute-start = (bf16[3,1024,128]{2,1,0:T(8,128)(2,1)}, bf16[3,1024,128]{2,1,0:T(8,128)(2,1)S(1)}, u32[]{:S(2)}, u32[]{:S(2)}) collective-permute-start(bf16[3,1024,128]{2,1,0:T(8,128)(2,1)} %get-tuple-element.1657), channel_id=1, source_target_pairs={{120,0},{0,8},{8,16},{16,24},{24,32},{32,40},{40,48},{48,56},{56,6... | collective-permute-start | bytes 2359304 | tf_op jit(solution)/shard_map/while/body/eval_jaxpr/ppermute | solution.py:21
  676.9 28.7 %collective-permute-start.1 = (bf16[3,1024,128]{2,1,0:T(8,128)(2,1)}, bf16[3,1024,128]{2,1,0:T(8,128)(2,1)S(1)}, u32[]{:S(2)}, u32[]{:S(2)}) collective-permute-start(bf16[3,1024,128]{2,1,0:T(8,128)(2,1)} %copy-done), channel_id=1, source_target_pairs={{120,0},{0,8},{8,16},{16,24},{24,32},{32,40},{40,48},{48,56},{56,6... | collective-permute-start | bytes 2359304 | tf_op jit(solution)/shard_map/while/body/eval_jaxpr/ppermute | solution.py:21
  719.1 19.4 %collective-permute-start = (bf16[3,1024,128]{2,1,0:T(8,128)(2,1)}, bf16[3,1024,128]{2,1,0:T(8,128)(2,1)S(1)}, u32[]{:S(2)}, u32[]{:S(2)}) collective-permute-start(bf16[3,1024,128]{2,1,0:T(8,128)(2,1)} %get-tuple-element.1657), channel_id=1, source_target_pairs={{120,0},{0,8},{8,16},{16,24},{24,32},{32,40},{40,48},{48,56},{56,6... | collective-permute-start | bytes 2359304 | tf_op jit(solution)/shard_map/while/body/eval_jaxpr/ppermute | solution.py:21
  719.1 27.8 %collective-permute-start.1 = (bf16[3,1024,128]{2,1,0:T(8,128)(2,1)}, bf16[3,1024,128]{2,1,0:T(8,128)(2,1)S(1)}, u32[]{:S(2)}, u32[]{:S(2)}) collective-permute-start(bf16[3,1024,128]{2,1,0:T(8,128)(2,1)} %copy-done), channel_id=1, source_target_pairs={{120,0},{0,8},{8,16},{16,24},{24,32},{32,40},{40,48},{48,56},{56,6... | collective-permute-start | bytes 2359304 | tf_op jit(solution)/shard_map/while/body/eval_jaxpr/ppermute | solution.py:21
  760.3 18.5 %collective-permute-start = (bf16[3,1024,128]{2,1,0:T(8,128)(2,1)}, bf16[3,1024,128]{2,1,0:T(8,128)(2,1)S(1)}, u32[]{:S(2)}, u32[]{:S(2)}) collective-permute-start(bf16[3,1024,128]{2,1,0:T(8,128)(2,1)} %get-tuple-element.1657), channel_id=1, source_target_pairs={{120,0},{0,8},{8,16},{16,24},{24,32},{32,40},{40,48},{48,56},{56,6... | collective-permute-start | bytes 2359304 | tf_op jit(solution)/shard_map/while/body/eval_jaxpr/ppermute | solution.py:21
  760.3 26.9 %collective-permute-start.1 = (bf16[3,1024,128]{2,1,0:T(8,128)(2,1)}, bf16[3,1024,128]{2,1,0:T(8,128)(2,1)S(1)}, u32[]{:S(2)}, u32[]{:S(2)}) collective-permute-start(bf16[3,1024,128]{2,1,0:T(8,128)(2,1)} %copy-done), channel_id=1, source_target_pairs={{120,0},{0,8},{8,16},{16,24},{24,32},{32,40},{40,48},{48,56},{56,6... | collective-permute-start | bytes 2359304 | tf_op jit(solution)/shard_map/while/body/eval_jaxpr/ppermute | solution.py:21
  800.5 12.4 %copy-start.15 = (f32[3,256]{1,0:T(4,128)S(1)}, f32[3,256]{1,0:T(4,128)}, u32[]{:S(2)}) copy-start(f32[3,256]{1,0:T(4,128)} %copy-done.14) | copy-start | bytes 9220
  800.5 47.5 %copy-start.13 = (f32[3,256]{1,0:T(4,128)S(1)}, f32[3,256]{1,0:T(4,128)}, u32[]{:S(2)}) copy-start(f32[3,256]{1,0:T(4,128)} %copy-done.12) | copy-start | bytes 9220
  801.7 66.9 %all-to-all-start.3 = ((bf16[8,128,384]{1,2,0:T(8,128)(2,1)}), bf16[8,128,384]{1,2,0:T(8,128)(2,1)S(1)}, u32[]{:S(2)}, u32[]{:S(2)}) async-start(bf16[8,128,384]{1,2,0:T(8,128)(2,1)} %copy.79), calls=%async_computation.3 | async-start | bytes 1572864 | tf_op jit(solution)/shard_map/all_to_all | solution.py:110
  870.8 21.1 %copy-start.8 = (pred[256]{0:T(512)(128)(4,1)S(1)}, pred[256]{0:T(512)(128)(4,1)}, u32[]{:S(2)}) copy-start(pred[256]{0:T(512)(128)(4,1)} %copy-done.7) | copy-start | bytes 772
  (17 other events, 16.1 us)
Sparse Core Ops, SparseCore 0:
  59.2 89.2 all-gather.6
where the time goes:
time: 914 us; the launch traced here: 907 us
  waiting for transfers between devices  525 us (57%)
  matrix products  140 us (15%)
  other arithmetic  79.4 us (9%)
  local copies, waits for them, and re-layouts  59 us (6%)
  blocking collectives  55.6 us (6%)
  starting transfers between devices  28.5 us (3%)
  between operations  15.1 us (2%)
    ppermute x30, waiting for transfers between devices, shifted(): return lax.ppermute(block, axis, route)  505 us
    dot_general x54, matrix products, one_head(): jnp.einsum('qd,kd->qk', query, key_h, preferred_element_type=jnp.float32)  87.7 us
    all_gather x2, blocking collectives, combined_all(): gathered = jax.tree.map(lambda a: lax.all_gather(a, axis), part)  55.6 us
    convert_element_type x48, other arithmetic, one_head(): weights.astype(jnp.bfloat16)  52.6 us
    dot_general x54, matrix products, one_head(): jnp.dot(weights.astype(jnp.bfloat16), value_h, preferred_element_type=jnp...  45.4 us
    while x60, local copies, waits for them, and re-layouts  27.6 us
    add x15, other arithmetic, combine(): first[2] * scale_a[:, :, None] + second[2] * scale_b[:, :, None]  20.3 us
  transfers between devices with their start and end apart: 35, of which 33 were waited for; matrix products, arithmetic and copies ran while one was open for 25% of the time, Pallas kernels for 0%

commit v1 on v0

v1 whole, which is shorter than its diff:
```python
import functools

import jax
import jax.numpy as jnp
import numpy as np
from jax import lax
from jax.experimental import pallas as pl
from jax.experimental.pallas import tpu as pltpu
from jax.sharding import Mesh, PartitionSpec as P

DH = 128
TEXT = 256
BLOCK = 128
SLAB = 32
HALF = 16
NTQ = 2
REC = 384
QREC = 256
OREC = 272
STEP = 4
UNROLL = 4
LOG2 = float(DH**-0.5 * np.log2(np.e))
neg_fill = -1e30
FLAG = 4096
FIRST_LEN = SLAB * STEP
REST_LEN = SLAB * (HALF + STEP) + 4 * STEP
HALO_LEN = HALF * (2 * HALF + STEP) + 4 * STEP

VM = pl.BlockSpec(memory_space=pltpu.VMEM)
SM = pl.BlockSpec(memory_space=pltpu.SMEM)
ANY = pl.BlockSpec(memory_space=pl.ANY)
PARAMS = pltpu.CompilerParams(vmem_limit_bytes=20 << 20)


def head_a(chip):
    z, x = chip // 4, chip % 4
    return 6 * x + 3 * (z // 2) + z % 2


def head_c(chip):
    z, x = chip // 4, chip % 4
    return 6 * x + 3 * (z // 2) + 2


def packed(vt, half):
    cols = vt[:, 64 * half : 64 * half + 64]
    return jnp.concatenate([cols[:64], cols[64:]], axis=1)


def prep_kv_kernel(k_hbm, v_hbm, out_ref, k_ref, v_ref, sems):
    third = 8 * DH
    copies = [
        [
            pltpu.make_async_copy(
                hbm.at[:, pl.ds(third * i, third)], ref.at[:, pl.ds(third * i, third)], sems.at[2 * i + j]
            )
            for j, (hbm, ref) in enumerate(((k_hbm, k_ref), (v_hbm, v_ref)))
        ]
        for i in range(3)
    ]
    for pair in copies:
        for copy in pair:
            copy.start()
    arrived = 0
    for x in range(4):
        while 8 * arrived < 6 * (x + 1):
            for copy in copies[arrived]:
                copy.wait()
            arrived += 1
        for z in range(4):
            chip = 4 * z + x
            a, c, half = head_a(chip) * DH, head_c(chip) * DH, z % 2
            out_ref[chip, 0:128] = k_ref[:, a : a + DH]
            out_ref[chip, 128:192] = k_ref[64 * half : 64 * half + 64, c : c + DH]
            out_ref[chip, 192:320] = v_ref[:, a : a + DH].T
            out_ref[chip, 320:384] = packed(v_ref[:, c : c + DH].T, half)


def prep_q_kernel(q_ref, out_ref):
    for chip in range(16):
        a, c = head_a(chip) * DH, head_c(chip) * DH
        out_ref[chip, 0:128] = q_ref[:, a : a + DH].T
        out_ref[chip, 128:256] = q_ref[:, c : c + DH].T


def lists_kernel(place_ref, mask_ref, first_ref, rest_ref, halo_a_ref, halo_b_ref, n_ref):
    y, c = place_ref[0], place_ref[1]

    def kept(q, j, dy):
        col = (y + dy) * SLAB + 2 * j + c
        inside = jnp.logical_and(col >= 0, col < 4 * SLAB)
        value = mask_ref[y * SLAB + q, jnp.clip(col, 0, 4 * SLAB - 1)]
        return jnp.where(inside, value, 0)

    def row_of(n):
        return jnp.where(n < HALF, 2 * n + c, 2 * (n - HALF) + 1 - c)

    def close(ref, start, pos, size):
        last = ref[jnp.maximum(pos - 1, 0)]
        for _ in range(size - 1):
            missing = (pos - start) % size != 0

            @pl.when(missing)
            def _():
                ref[pos] = last | FLAG

            pos = pos + jnp.where(missing, 1, 0)
        return pos

    def own(n, pos):
        row = row_of(n)
        count = jnp.int32(0)
        start = pos
        for j in range(HALF):
            hit = kept(row, j, 0)

            @pl.when(jnp.logical_and(hit > 0, count < STEP - 1))
            def _():
                first_ref[n * STEP + count] = n * 64 + j

            @pl.when(jnp.logical_and(hit > 0, count >= STEP - 1))
            def _():
                rest_ref[pos] = n * 64 + j

            pos = pos + jnp.where(jnp.logical_and(hit > 0, count >= STEP - 1), 1, 0)
            count = count + hit
        some = jnp.minimum(count, STEP - 1)
        last = jnp.where(some > 0, first_ref[n * STEP + jnp.maximum(some - 1, 0)], n * 64)
        for k in range(STEP):

            @pl.when(k >= some)
            def _():
                first_ref[n * STEP + k] = last | FLAG

        return close(rest_ref, start, pos, STEP)

    end = lax.fori_loop(0, SLAB, own, jnp.int32(0))
    n_ref[0] = end // STEP
    for k in range(4 * STEP):
        rest_ref[end + k] = FLAG
    for which, (ref, base) in enumerate(((halo_a_ref, HALF), (halo_b_ref, 0))):

        def far(n, pos):
            start = pos
            row = row_of(n + base)
            for dy, shift in ((-1, 0), (1, HALF)):
                for j in range(HALF):
                    hit = kept(row, j, dy)

                    @pl.when(hit > 0)
                    def _():
                        ref[pos] = n * 64 + shift + j

                    pos = pos + hit
            return close(ref, start, pos, STEP)

        end = lax.fori_loop(0, HALF, far, jnp.int32(0))
        n_ref[1 + which] = end // STEP
        for k in range(4 * STEP):
            ref[end + k] = FLAG
    n_ref[3] = 0


def fold(x, op):
    return op(x.reshape(-1, 8, DH), axis=0)


def slots(list_ref, t):
    codes = [list_ref[STEP * t + k] for k in range(STEP)]
    q = (codes[0] & (FLAG - 1)) >> 6
    gaps = [jnp.where(code >= FLAG, jnp.float32(1e30), jnp.float32(0)) for code in codes]
    return q, [code & 63 for code in codes], gaps


def wide_c(kv_ref, js):
    low, high = [], []
    for j in js:
        part = kv_ref[j, 320:384]
        low.append(part[:, :64])
        high.append(part[:, 64:])
    return jnp.concatenate([jnp.concatenate(low, axis=1), jnp.concatenate(high, axis=1)], axis=0)


def scores(kv_ref, q_ref, s_ref, t_ref, buf, q, js, live=None):
    for h, (low, size, row) in enumerate(((0, 128, 0), (512, 64, 128))):
        keys = jnp.concatenate([kv_ref[j, row : row + size] for j in js], axis=0)
        s = jnp.dot(keys, q_ref[q, 128 * h : 128 * h + 128], preferred_element_type=jnp.float32)
        if live is not None:
            rows = lax.broadcasted_iota(jnp.int32, (size, DH), 0)
            s = jnp.concatenate([jnp.where(rows < live[h], s[:size], neg_fill), s[size:]], axis=0)
        s_ref[buf, low : low + STEP * size] = s
        t_ref[buf, h] = jnp.broadcast_to(column_max(s), (8, DH))


def column_max(s):
    return jnp.max(fold(s, jnp.max), axis=0, keepdims=True)


def weights(parts, top, gaps):
    return [jnp.exp2((s - (top + gap)) * LOG2) for s, gap in zip(parts, gaps)]


def values_of(kv_ref, js, h):
    if h == 0:
        return jnp.concatenate([kv_ref[j, 192:320] for j in js], axis=1)
    return wide_c(kv_ref, js)


def parts_of(s_ref, buf, h):
    low, size = (0, 128) if h == 0 else (512, 64)
    return [s_ref[buf, low + size * k : low + size * (k + 1)] for k in range(STEP)]


def first_step(kv_ref, s_ref, t_ref, acc_ref, m_ref, l_ref, buf, q, js, gaps):
    for h in range(2):
        top = t_ref[buf, h]
        w = weights(parts_of(s_ref, buf, h), top[:1], gaps)
        m_ref[q, h] = top
        l_ref[q, h] = sum(fold(x, jnp.sum) for x in w)
        w = jnp.concatenate(w, axis=0).astype(jnp.bfloat16)
        acc_ref[q, h] = jnp.dot(values_of(kv_ref, js, h), w, preferred_element_type=jnp.float32)


def next_step(kv_ref, s_ref, t_ref, acc_ref, m_ref, l_ref, buf, q, js, gaps):
    for h in range(2):
        old = m_ref[q, h]
        new = jnp.maximum(old, t_ref[buf, h])
        factor = jnp.exp2((old - new) * LOG2)
        w = weights(parts_of(s_ref, buf, h), new[:1], gaps)
        m_ref[q, h] = new
        l_ref[q, h] = l_ref[q, h] * factor + sum(fold(x, jnp.sum) for x in w)
        w = jnp.concatenate(w, axis=0).astype(jnp.bfloat16)
        acc_ref[q, h] = acc_ref[q, h] * factor[:1] + jnp.dot(
            values_of(kv_ref, js, h), w, preferred_element_type=jnp.float32
        )


def run_list(kv_ref, q_ref, s_ref, t_ref, acc_ref, m_ref, l_ref, list_ref, steps):
    def score(t, buf):
        q, js, _ = slots(list_ref, t)
        scores(kv_ref, q_ref, s_ref, t_ref, buf, q, js)

    def step(t, buf):
        q, js, gaps = slots(list_ref, t)
        next_step(kv_ref, s_ref, t_ref, acc_ref, m_ref, l_ref, buf, q, js, gaps)

    score(0, 0)

    def body(i, carry):
        for k in range(UNROLL):
            score(UNROLL * i + k + 1, (k + 1) % 2)
            step(UNROLL * i + k, k % 2)
        return carry

    lax.fori_loop(0, steps // UNROLL, body, 0)

    def rest(i, carry):
        @pl.when(i % 2 == 0)
        def _():
            score(i + 1, 1)
            step(i, 0)

        @pl.when(i % 2 == 1)
        def _():
            score(i + 1, 0)
            step(i, 1)

        return carry

    lax.fori_loop(steps // UNROLL * UNROLL, steps, rest, 0)


def own_kernel(
    first_ref, rest_ref, n_ref, live_ref, kv_hbm, text_hbm, q_hbm, other_hbm,
    acc_ref, m_ref, l_ref, kv_ref, q_ref, s_ref, t_ref, sems,
):
    copies = [
        pltpu.make_async_copy(kv_hbm, kv_ref.at[pl.ds(0, HALF)], sems.at[0]),
        pltpu.make_async_copy(text_hbm, kv_ref.at[pl.ds(HALF, 1)], sems.at[1]),
        pltpu.make_async_copy(q_hbm, q_ref.at[pl.ds(0, HALF)], sems.at[2]),
        pltpu.make_async_copy(other_hbm, q_ref.at[pl.ds(HALF, HALF)], sems.at[3]),
    ]
    for copy in copies:
        copy.start()
    for copy in copies:
        copy.wait()

    def line(n):
        codes = [first_ref[STEP * n + k] for k in range(STEP - 1)]
        gaps = [jnp.float32(0)]
        gaps += [jnp.where(code >= FLAG, jnp.float32(1e30), jnp.float32(0)) for code in codes]
        return [jnp.int32(HALF)] + [code & 63 for code in codes], gaps

    def score(n, buf):
        live = (live_ref[0], live_ref[1])
        scores(kv_ref, q_ref, s_ref, t_ref, buf, n, line(n)[0], live)

    def step(n, buf):
        js, gaps = line(n)
        first_step(kv_ref, s_ref, t_ref, acc_ref, m_ref, l_ref, buf, n, js, gaps)

    score(0, 0)

    def body(i, carry):
        for k in range(UNROLL):
            score(jnp.minimum(UNROLL * i + k + 1, SLAB - 1), (k + 1) % 2)
            step(UNROLL * i + k, k % 2)
        return carry

    lax.fori_loop(0, SLAB // UNROLL, body, 0)
    run_list(kv_ref, q_ref, s_ref, t_ref, acc_ref, m_ref, l_ref, rest_ref, n_ref[0])


def text_kernel(live_ref, kv_ref, text_ref, q_ref, out_ref, s_ref, t_ref, acc_ref, m_ref, l_ref):
    none = [jnp.float32(0)] * STEP
    live = (live_ref[2], live_ref[3])

    def one(block, carry):
        for start in range(0, HALF, STEP):
            js = list(range(start, start + STEP))
            scores(kv_ref, q_ref, s_ref, t_ref, 0, block, js)
            step = next_step if start else first_step
            step(kv_ref, s_ref, t_ref, acc_ref, m_ref, l_ref, 0, block, js, none)
        for h, (low, size, row) in enumerate(((0, 128, 0), (512, 64, 128))):
            s = jnp.dot(
                text_ref[0, row : row + size],
                q_ref[block, 128 * h : 128 * h + 128],
                preferred_element_type=jnp.float32,
            )
            rows = lax.broadcasted_iota(jnp.int32, s.shape, 0)
            s = jnp.where(rows < live[h], s, neg_fill)
            old = m_ref[block, h]
            new = jnp.maximum(old, column_max(s))
            factor = jnp.exp2((old - new) * LOG2)
            w = jnp.exp2((s - new[:1]) * LOG2)
            total = row_sum(l_ref[block, h] * factor) + row_sum(fold(w, jnp.sum))
            v = text_ref[0, 192:320] if h == 0 else wide_c(text_ref, [0])
            acc = acc_ref[block, h] * factor[:1] + jnp.dot(
                v, w.astype(jnp.bfloat16), preferred_element_type=jnp.float32
            )
            put_text(out_ref, h * NTQ + block, new[:1], total, acc)
        return carry

    lax.fori_loop(0, NTQ, one, 0)


def row_sum(x):
    return jnp.sum(x, axis=0, keepdims=True)


def put_text(ref, at, top, total, acc):
    ref[at, 0:128] = acc.astype(jnp.bfloat16)
    ref[at, 128:144] = stat_rows([top, total])


def merged(blocks):
    stats = [stats_of(block[128:144], 2) for block in blocks]
    top = functools.reduce(jnp.maximum, [s[0] for s in stats])
    factors = [jnp.exp2((s[0] - top) * LOG2) for s in stats]
    total = sum(s[1] * f for s, f in zip(stats, factors))
    return top, total, sum(b[0:128].astype(jnp.float32) * f for b, f in zip(blocks, factors))


def merge_text_kernel(mine_ref, other_ref, out_ref):
    for block in range(NTQ):
        for head in range(3):
            at = (0 if head < 2 else NTQ) + block
            members = (head,) if head < 2 else (0, 1)
            blocks = [ref[i, at] for ref in (mine_ref, other_ref) for i in members]
            put_text(out_ref, head * NTQ + block, *merged(blocks))


def final_text_kernel(*refs):
    for block in range(NTQ):
        for head in range(3):
            _, total, acc = merged([ref[head * NTQ + block] for ref in refs[:-1]])
            out = (acc / total).astype(jnp.bfloat16).T
            refs[-1][128 * block : 128 * block + 128, head * DH : head * DH + DH] = out


def split3(x):
    rows = []
    for _ in range(3):
        part = x.astype(jnp.bfloat16)
        rows.append(part)
        x = x - part.astype(jnp.float32)
    return rows


def stat_rows(rows):
    parts = [part for row in rows for part in split3(row)]
    pad = jnp.zeros((16 - len(parts), DH), jnp.bfloat16)
    return jnp.concatenate(parts + [pad], axis=0)


def stats_of(block, count):
    x = block.astype(jnp.float32)
    return [x[3 * i : 3 * i + 1] + x[3 * i + 1 : 3 * i + 2] + x[3 * i + 2 : 3 * i + 3] for i in range(count)]


def halo_kernel(
    which, list_ref, n_ref, down_hbm, up_hbm, q_hbm, acc_hbm, m_hbm, l_hbm,
    *refs,
):
    if which == 0:
        out_ref, kv_ref, q_ref, s_ref, t_ref, acc_ref, m_ref, l_ref, sems = refs
    else:
        acc_ref, m_ref, l_ref, kv_ref, q_ref, s_ref, t_ref, sems = refs
    base = HALF if which == 0 else 0
    copies = [
        pltpu.make_async_copy(down_hbm, kv_ref.at[pl.ds(0, HALF)], sems.at[0]),
        pltpu.make_async_copy(up_hbm, kv_ref.at[pl.ds(HALF, HALF)], sems.at[1]),
        pltpu.make_async_copy(q_hbm, q_ref, sems.at[2]),
        pltpu.make_async_copy(acc_hbm.at[pl.ds(base, HALF)], acc_ref, sems.at[3]),
        pltpu.make_async_copy(m_hbm.at[pl.ds(base, HALF)], m_ref, sems.at[4]),
        pltpu.make_async_copy(l_hbm.at[pl.ds(base, HALF)], l_ref, sems.at[5]),
    ]
    for copy in copies:
        copy.start()
    for copy in copies:
        copy.wait()
    run_list(kv_ref, q_ref, s_ref, t_ref, acc_ref, m_ref, l_ref, list_ref, n_ref[1 + which])
    if which == 0:

        def finish(n, carry):
            rows = []
            for h in range(2):
                out_ref[n, 128 * h : 128 * h + 128] = acc_ref[n, h].astype(jnp.bfloat16)
                rows += [m_ref[n, h, 0:1], jnp.sum(l_ref[n, h], axis=0, keepdims=True)]
            out_ref[n, 256:272] = stat_rows(rows)
            return carry

        lax.fori_loop(0, HALF, finish, 0)


def merge_kernel(acc_ref, m_ref, l_ref, got_ref, out_ref):
    def one(n, carry):
        stats = stats_of(got_ref[n, 256:272], 4)
        for h in range(2):
            mine, ours = m_ref[n, h, 0:1], jnp.sum(l_ref[n, h], axis=0, keepdims=True)
            his, theirs = stats[2 * h], stats[2 * h + 1]
            top = jnp.maximum(mine, his)
            a, b = jnp.exp2((mine - top) * LOG2), jnp.exp2((his - top) * LOG2)
            total = ours * a + theirs * b
            acc = acc_ref[n, h] * a + got_ref[n, 128 * h : 128 * h + 128].astype(jnp.float32) * b
            if h == 0:
                out_ref[n, 0:128] = (acc / total).astype(jnp.bfloat16)
            else:
                out_ref[n, 128:256] = acc.astype(jnp.bfloat16)
                out_ref[n, 256:272] = stat_rows([top, total])
        return carry

    lax.fori_loop(0, HALF, one, 0)


def final_kernel(got_ref, out_ref):
    for x in range(4):
        for pair in range(2):
            first, second = 4 * (2 * pair) + x, 4 * (2 * pair + 1) + x
            col = (6 * x + 3 * pair) * DH
            out_ref[:, col : col + DH] = got_ref[first, 0:128].T
            out_ref[:, col + DH : col + 2 * DH] = got_ref[second, 0:128].T
            m1, l1 = stats_of(got_ref[first, 256:272], 2)
            m2, l2 = stats_of(got_ref[second, 256:272], 2)
            top = jnp.maximum(m1, m2)
            a, b = jnp.exp2((m1 - top) * LOG2), jnp.exp2((m2 - top) * LOG2)
            total = l1 * a + l2 * b
            acc = got_ref[first, 128:256].astype(jnp.float32) * a
            acc = (acc + got_ref[second, 128:256].astype(jnp.float32) * b) / total
            out_ref[:, col + 2 * DH : col + 3 * DH] = acc.astype(jnp.bfloat16).T


def ring(x, axis):
    routes = [[(i, (i + far) % 4) for i in range(4)] for far in (1, 2, 3)]
    return [x] + [lax.ppermute(x, axis, route) for route in routes]


def shape(dims, dtype=jnp.bfloat16):
    return jax.ShapeDtypeStruct(dims, dtype)


def state(n):
    return [shape((n, 2, 128, 128), jnp.float32)] + [shape((n, 2, 8, 128), jnp.float32)] * 2


def run_lists(place, block_mask):
    return pl.pallas_call(
        lists_kernel,
        out_shape=[shape((n,), jnp.int32) for n in (FIRST_LEN, REST_LEN, HALO_LEN, HALO_LEN, 4)],
        in_specs=[SM, SM],
        out_specs=[SM] * 5,
        compiler_params=PARAMS,
        cost_estimate=pl.CostEstimate(flops=8 * 10**9, bytes_accessed=10**5, transcendentals=0),
        name="lists",
    )(place, block_mask)


def run_own(first, rest, counts, live, kv, text_rec, q, q_other):
    return pl.pallas_call(
        own_kernel,
        out_shape=state(SLAB),
        in_specs=[SM] * 4 + [ANY] * 4,
        out_specs=[VM] * 3,
        scratch_shapes=[
            pltpu.VMEM((HALF + 1, REC, DH), jnp.bfloat16),
            pltpu.VMEM((SLAB, QREC, DH), jnp.bfloat16),
            pltpu.VMEM((2, 768, DH), jnp.float32),
            pltpu.VMEM((2, 2, 8, DH), jnp.float32),
            pltpu.SemaphoreType.DMA((4,)),
        ],
        compiler_params=PARAMS,
        cost_estimate=pl.CostEstimate(flops=10**8, bytes_accessed=10**6, transcendentals=0),
        name="own_keys",
    )(first, rest, counts, live, kv, text_rec, q, q_other)


def run_text(live, kv, text_rec, tq):
    scratch = [pltpu.VMEM((1, 768, DH), jnp.float32), pltpu.VMEM((1, 2, 8, DH), jnp.float32)]
    return pl.pallas_call(
        text_kernel,
        out_shape=shape((2 * NTQ, 144, DH)),
        in_specs=[SM] + [VM] * 3,
        out_specs=VM,
        scratch_shapes=scratch + [pltpu.VMEM(s.shape, jnp.float32) for s in state(NTQ)],
        compiler_params=PARAMS,
        cost_estimate=pl.CostEstimate(flops=10**7, bytes_accessed=10**5, transcendentals=0),
        name="text_keys",
    )(live, kv, text_rec, tq)


def run_halo(which, queries, table, counts, from_down, from_up, acc, m, l):
    scratch = [
        pltpu.VMEM((SLAB, REC, DH), jnp.bfloat16),
        pltpu.VMEM((HALF, QREC, DH), jnp.bfloat16),
        pltpu.VMEM((2, 768, DH), jnp.float32),
            pltpu.VMEM((2, 2, 8, DH), jnp.float32),
    ]
    if which == 0:
        out = shape((HALF, OREC, DH))
        scratch += [pltpu.VMEM(s.shape, jnp.float32) for s in state(HALF)]
    else:
        out = state(HALF)
    return pl.pallas_call(
        functools.partial(halo_kernel, which),
        out_shape=out,
        in_specs=[SM, SM] + [ANY] * 6,
        out_specs=VM if which == 0 else [VM] * 3,
        scratch_shapes=scratch + [pltpu.SemaphoreType.DMA((6,))],
        compiler_params=PARAMS,
        cost_estimate=pl.CostEstimate(flops=2 * 10**9, bytes_accessed=10**7, transcendentals=4 * 10**6),
        name="halo_keys",
    )(table, counts, from_down, from_up, queries, acc, m, l)


def local(video_q, video_k, video_v, text_q, text_k, text_v, block_mask, text_count):
    f32 = jnp.float32
    together = lax.optimization_barrier
    y, z, c = lax.axis_index("y"), lax.axis_index("z"), lax.axis_index("c")
    pair, member = z // 2, z % 2
    chips = ("z", "x")
    swap = [(0, 1), (1, 0)]

    kv_send = pl.pallas_call(
        prep_kv_kernel, out_shape=shape((16, REC, DH)), in_specs=[ANY] * 2, out_specs=VM,
        scratch_shapes=[pltpu.VMEM((BLOCK, 24 * DH), jnp.bfloat16)] * 2 + [pltpu.SemaphoreType.DMA((6,))],
        compiler_params=pltpu.CompilerParams(vmem_limit_bytes=60 << 20), name="prep_kv",
    )(video_k, video_v)
    kv = lax.all_to_all(kv_send, chips, 0, 0, tiled=True)

    text_q, text_k, text_v, block_mask, _ = together((text_q, text_k, text_v, block_mask, kv_send))
    text = jnp.stack([text_q, text_k, text_v])
    text = jnp.where(c == pair, text, lax.ppermute(text, "c", swap))
    head = lax.dynamic_slice_in_dim(text, member * DH, DH, 2)
    shared = text[:, :, 2 * DH :]
    tq = jnp.stack([head[0].T, shared[0].T])
    tq = tq.reshape(2, DH, NTQ, DH).transpose(2, 0, 1, 3).reshape(NTQ, QREC, DH)
    mine = lax.dynamic_slice_in_dim(head, c * BLOCK, BLOCK, 1)
    half = lax.dynamic_slice_in_dim(shared, c * BLOCK + member * 64, 64, 1)
    vt = half[2].T
    text_rec = jnp.concatenate(
        [mine[1], half[1], mine[2].T, jnp.concatenate([vt[:64], vt[64:]], axis=1)], axis=0
    )[None]
    live_a = jnp.clip(text_count[0] - c * BLOCK, 0, BLOCK)
    live_c = jnp.clip(text_count[0] - c * BLOCK - member * 64, 0, 64)
    lead = y == 0
    live = jnp.stack([live_a, live_c, jnp.where(lead, live_a, 0), jnp.where(lead, live_c, 0)])
    live = live.astype(jnp.int32)
    place = jnp.stack([y, c]).astype(jnp.int32)
    first, rest, halo_a, halo_b, counts = run_lists(place, block_mask)
    video_q, tq, text_rec, first, rest, halo_a, halo_b, counts = together(
        (video_q, tq, text_rec, first, rest, halo_a, halo_b, counts)
    )
    q_send = pl.pallas_call(
        prep_q_kernel, out_shape=shape((16, QREC, DH)), in_specs=[VM], out_specs=VM,
        compiler_params=PARAMS, name="prep_q",
    )(video_q)

    q_send, kv = together((q_send, kv))
    from_down = lax.ppermute(kv, "y", [(0, 1), (1, 2), (2, 3)])
    from_up = lax.ppermute(kv, "y", [(1, 0), (2, 1), (3, 2)])
    q = lax.all_to_all(q_send, chips, 0, 0, tiled=True)
    text_part = run_text(live, kv, text_rec, tq)
    q, text_part = together((q, text_part))
    q_other = lax.ppermute(q, "c", swap)
    text_ring = ring(text_part, "z")
    acc, m, l = run_own(first, rest, counts, live, kv, text_rec, q, q_other)
    acc, *text_ring = together((acc, *text_ring))
    parts = jnp.stack(text_ring)[(z - jnp.arange(4)) % 4]
    theirs = lax.ppermute(lax.dynamic_slice_in_dim(parts, 2 - 2 * c, 2, 0), "c", swap)
    heads = pl.pallas_call(
        merge_text_kernel, out_shape=shape((3 * NTQ, 144, DH)), in_specs=[VM, VM], out_specs=VM,
        compiler_params=PARAMS, name="merge_text",
    )(lax.dynamic_slice_in_dim(parts, 2 * c, 2, 0), theirs)

    partial = run_halo(0, q_other, halo_a, counts, from_down, from_up, acc, m, l)
    q, heads = together((q, heads))
    got = lax.ppermute(partial, "c", swap)
    acc2, m2, l2 = run_halo(1, q, halo_b, counts, from_down, from_up, acc, m, l)
    record = pl.pallas_call(
        merge_kernel, out_shape=shape((HALF, OREC, DH)), in_specs=[VM] * 4, out_specs=VM,
        compiler_params=PARAMS, name="merge_cores",
    )(acc2, m2, l2, got)
    back = lax.all_to_all(record, chips, 0, 0, tiled=True)
    heads, _ = together((heads, record))
    text_out = pl.pallas_call(
        final_text_kernel, out_shape=shape((TEXT, 3 * DH)), in_specs=[VM] * 4, out_specs=VM,
        compiler_params=PARAMS, name="final_text",
    )(*ring(heads, "y"))
    video_out = pl.pallas_call(
        final_kernel, out_shape=shape((BLOCK, 24 * DH)), in_specs=[VM], out_specs=VM,
        compiler_params=PARAMS, name="final",
    )(back)
    return video_out, text_out


def solution(mesh):
    grid = Mesh(mesh.devices.reshape(4, 4, 4, 2), ("y", "z", "x", "c"))
    video = P(("y", "z", "x", "c"), None)
    text = P(None, ("x", "c"))
    return jax.shard_map(
        local,
        mesh=grid,
        in_specs=(video, video, video, text, text, text, P(), P()),
        out_specs=(video, text),
        check_vma=False,
    )
```

time: 914 us -> 136 us (0.15)
  waiting for transfers between devices: 525 us -> 27.8 us
  matrix products: 140 us -> 0 us
  other arithmetic: 79.4 us -> 2.31 us
  Pallas kernels: 0 us -> 62.6 us
  blocking collectives: 55.6 us -> 0 us
  local copies, waits for them, and re-layouts: 59 us -> 9.45 us
  between operations: 15.1 us -> 1.77 us
    ppermute x30 -> x12, waiting for transfers between devices: 505 us -> 13.6 us  [the longest x6 9.77 us: ring(): return [x] + [lax.ppermute(x, axis, route) for route in routes]]
    dot_general x114 -> x0, matrix products: 140 us -> none  [the longest x54 87.7 us: one_head(): jnp.einsum('qd,kd->qk', query, key_h, preferred_element_type=jnp.float32)]
    pallas_call x0 -> x11, Pallas kernels: none -> 62.6 us  [the longest x1 19 us: run_own(): pl.pallas_call(own_kernel, out_shape=state(SLAB), in_specs=[SM] * 4 + [AN...]
    all_gather x2 -> x0, blocking collectives: 55.6 us -> none  [combined_all(): gathered = jax.tree.map(lambda a: lax.all_gather(a, axis), part)]
    convert_element_type x49 -> x0, other arithmetic: 52.6 us -> none  [the longest x48 52.6 us: one_head(): weights.astype(jnp.bfloat16)]
    while x63 -> x0, local copies, waits for them, and re-layouts: 30.4 us -> none
    add x84 -> x0, other arithmetic: 22.2 us -> none  [the longest x15 20.3 us: combine(): first[2] * scale_a[:, :, None] + second[2] * scale_b[:, :, None]]
    all_to_all x4 -> x3, waiting for transfers between devices: 19.9 us -> 14.2 us  [the longest x1 6.51 us: local(): q = lax.all_to_all(q_send, chips, 0, 0, tiled=True)]
  transfers between devices with their start and end apart: 35 -> 15, of which waited for: 33 -> 9; matrix products, arithmetic and copies ran while one was open for 25% -> 6% of each run, Pallas kernels for 0% -> 35%
where the time goes in v1:
time: 136 us; the launch traced here: 134 us
  Pallas kernels  62.6 us (46%)
  starting transfers between devices  29.6 us (22%)
  waiting for transfers between devices  27.8 us (20%)
  local copies, waits for them, and re-layouts  9.45 us (7%)
  other arithmetic  2.31 us (2%)
  between operations  1.77 us (1%)
    pallas_call x1, Pallas kernels, run_own(): pl.pallas_call(own_kernel, out_shape=state(SLAB), in_specs=[SM] * 4 + [AN...  19 us
    pallas_call x2, Pallas kernels, run_halo(): pl.pallas_call(functools.partial(halo_kernel, which), out_shape=out, in_s...  17.4 us
    pallas_call x1, Pallas kernels, run_lists(): pl.pallas_call(lists_kernel, out_shape=[shape((n,), jnp.int32) for n in (...  13.8 us
    ppermute x6, waiting for transfers between devices, ring(): return [x] + [lax.ppermute(x, axis, route) for route in routes]  9.77 us
    all_to_all x1, starting transfers between devices, local(): kv = lax.all_to_all(kv_send, chips, 0, 0, tiled=True)  8.02 us
    all_to_all x1, waiting for transfers between devices, local(): q = lax.all_to_all(q_send, chips, 0, 0, tiled=True)  6.51 us
    all_to_all x1, starting transfers between devices, local(): back = lax.all_to_all(record, chips, 0, 0, tiled=True)  6.05 us
    ppermute x6, starting transfers between devices, ring(): return [x] + [lax.ppermute(x, axis, route) for route in routes]  5.2 us
  transfers between devices with their start and end apart: 15, of which 9 were waited for; matrix products, arithmetic and copies ran while one was open for 6% of the time, Pallas kernels for 35%

profile of v1, /device:TPU:8, one launch (start us, length us, event | category | flops | bytes accessed | tf_op | source)
XLA Modules:
  0.0 133.5 jit_solution(5004330974451672414)
XLA Ops:
  0.6 3.0 %prep_kv.1 = bf16[16,384,128]{2,1,0:T(8,128)(2,1)} custom-call(bf16[128,3072]{1,0:T(8,128)(2,1)} %k_hbm.1, bf16[128,3072]{1,0:T(8,128)(2,1)} %v_hbm.1), custom_call_target="tpu_custom_call" | custom-call | tf_op jit(solution)/shard_map/prep_kv/pallas_call | solution.py:563
  3.7 8.0 %all-to-all-start = ((bf16[16,384,128]{2,1,0:T(8,128)(2,1)}), bf16[16,384,128]{2,1,0:T(8,128)(2,1)S(1)}, u32[]{:S(2)}, u32[]{:S(2)}) async-start(bf16[16,384,128]{2,1,0:T(8,128)(2,1)} %prep_kv.1), calls=%async_computation | async-start | bytes 3145728 | tf_op jit(solution)/shard_map/all_to_all | solution.py:568
  11.7 0.1 copy.10
  11.9 0.1 copy.11
  12.1 0.1 copy.12
  12.2 0.9 pad_maximum_fusion
  13.2 13.8 %lists.1 = (s32[128]{0:T(128)S(1)}, s32[656]{0:T(1024)S(1)}, s32[592]{0:T(1024)S(1)}, s32[592]{0:T(1024)S(1)}, s32[4]{0:T(128)S(1)}) custom-call(s32[2]{0:T(128)S(1)} %pad_add_fusion.place_ref, s32[128,128]{1,0:T(8,128)S(1)} %copy-done.4), custom_call_target="tpu_custom_call" | custom-call | flops 8000000000 | bytes 100000 | tf_op jit(solution)/shard_map/lists/pallas_call | solution.py:487
  27.1 0.1 broadcast_select_fusion
  27.2 0.8 copy-done.5
  28.0 0.1 dynamic-slice_bitcast_fusion.4
  28.1 0.1 copy.14
  28.2 0.1 dynamic-slice_bitcast_fusion.3
  28.4 0.1 copy.15
  28.4 0.9 dynamic-slice_bitcast_fusion
  29.4 0.2 maximum_bitcast_fusion
  29.6 0.1 maximum_bitcast_fusion.1.text_ref.text_hbm
  29.7 0.3 prep_q.1
  30.0 1.0 copy-done.2
  31.0 5.2 %all-to-all-done.kv_ref.kv_hbm = bf16[16,384,128]{2,1,0:T(8,128)(2,1)S(1)} async-done(((bf16[16,384,128]{2,1,0:T(8,128)(2,1)}), bf16[16,384,128]{2,1,0:T(8,128)(2,1)S(1)}, u32[]{:S(2)}, u32[]{:S(2)}) %all-to-all-start) | async-done | bytes 1572896 | tf_op jit(solution)/shard_map/all_to_all | solution.py:568
  36.2 3.7 %all-to-all-start.1 = ((bf16[16,256,128]{2,1,0:T(8,128)(2,1)}), bf16[16,256,128]{2,1,0:T(8,128)(2,1)S(1)}, u32[]{:S(2)}, u32[]{:S(2)}) async-start(bf16[16,256,128]{2,1,0:T(8,128)(2,1)} %copy-done.2), calls=%async_computation.1 | async-start | bytes 2097152 | tf_op jit(solution)/shard_map/all_to_all | solution.py:601
  39.8 2.4 %collective-permute-start.2 = (bf16[16,384,128]{2,1,0:T(8,128)(2,1)S(1)}, bf16[16,384,128]{2,1,0:T(8,128)(2,1)}, u32[]{:S(2)}, u32[]{:S(2)}) collective-permute-start(bf16[16,384,128]{2,1,0:T(8,128)(2,1)S(1)} %all-to-all-done.kv_ref.kv_hbm), channel_id=1, source_target_pairs={{32,0},{64,32},{96,64},{33,1},{65,33},{97,65},{34,2},{66,34},{98,6... | collective-permute-start | bytes 4718600 | tf_op jit(solution)/shard_map/ppermute | solution.py:600
  42.2 3.5 %collective-permute-start.1 = (bf16[16,384,128]{2,1,0:T(8,128)(2,1)S(1)}, bf16[16,384,128]{2,1,0:T(8,128)(2,1)}, u32[]{:S(2)}, u32[]{:S(2)}) collective-permute-start(bf16[16,384,128]{2,1,0:T(8,128)(2,1)S(1)} %all-to-all-done.kv_ref.kv_hbm), channel_id=1, source_target_pairs={{0,32},{32,64},{64,96},{1,33},{33,65},{65,97},{2,34},{34,66},{66,9... | collective-permute-start | bytes 4718600 | tf_op jit(solution)/shard_map/ppermute | solution.py:599
  46.5 3.6 %text_keys.1 = bf16[4,144,128]{2,1,0:T(8,128)(2,1)S(1)} custom-call(s32[4]{0:T(128)S(1)} %pad_add_fusion.1.live_ref, bf16[16,384,128]{2,1,0:T(8,128)(2,1)S(1)} %all-to-all-done.kv_ref.kv_hbm, bf16[1,384,128]{2,1,0:T(8,128)(2,1)S(1)} %maximum_bitcast_fusion.1.text_ref.text_hbm, bf16[2,256,128]{2,1,0:T(8,128)(2,1)S(1)} %bitcast.43), custom_call_target="tpu_custom_call" | custom-call | flops 10000000 | bytes 100000 | tf_op jit(solution)/shard_map/text_keys/pallas_call | solution.py:519
  50.1 6.5 %all-to-all-done.1.q_hbm = bf16[16,256,128]{2,1,0:T(8,128)(2,1)S(1)} async-done(((bf16[16,256,128]{2,1,0:T(8,128)(2,1)}), bf16[16,256,128]{2,1,0:T(8,128)(2,1)S(1)}, u32[]{:S(2)}, u32[]{:S(2)}) %all-to-all-start.1) | async-done | bytes 1048608 | tf_op jit(solution)/shard_map/all_to_all | solution.py:601
  56.6 0.6 collective-permute-start.6
  57.2 0.6 collective-permute-start.5
  57.7 1.5 %collective-permute-done.3.other_hbm.q_hbm = bf16[16,256,128]{2,1,0:T(8,128)(2,1)S(1)} collective-permute-done((bf16[16,256,128]{2,1,0:T(8,128)(2,1)S(1)}, bf16[16,256,128]{2,1,0:T(8,128)(2,1)S(1)}, u32[]{:S(2)}, u32[]{:S(2)}) %collective-permute-start.3) | collective-permute-done | bytes 1048608 | tf_op jit(solution)/shard_map/ppermute | solution.py:604
  59.3 19.0 %own_keys.1 = (f32[32,2,128,128]{3,2,1,0:T(8,128)S(1)}, f32[32,2,8,128]{3,2,1,0:T(8,128)S(1)}, f32[32,2,8,128]{3,2,1,0:T(8,128)S(1)}) custom-call(s32[128]{0:T(128)S(1)} %get-tuple-element.54.first_ref, s32[656]{0:T(1024)S(1)} %get-tuple-element.55.rest_ref, s32[4]{0:T(128)S(1)} %get-tuple-element.47.n_ref, s32[4]{0:T(128)S(1)} %pad_add_fusion.1.live_ref, ...), custom_call_target="tpu_custom_call" | custom-call | flops 100000000 | bytes 1000000 | tf_op jit(solution)/shard_map/own_keys/pallas_call | solution.py:499
  78.4 0.7 collective-permute-done.1.down_hbm
  79.2 8.5 %halo_keys.3 = bf16[16,272,128]{2,1,0:T(8,128)(2,1)S(1)} custom-call(s32[592]{0:T(1024)S(1)} %get-tuple-element.69.list_ref, s32[4]{0:T(128)S(1)} %get-tuple-element.47.n_ref, bf16[16,384,128]{2,1,0:T(8,128)(2,1)} %collective-permute-done.1.down_hbm, bf16[16,384,128]{2,1,0:T(8,128)(2,1)} %collective-permute-done.2.up_hbm, ...), custom_call_target="tpu_custom_call" | custom-call | flops 2000000000 | bytes 10000000 | tf_op jit(solution)/shard_map/halo_keys/pallas_call | solution.py:543
  87.6 0.7 collective-permute-start.8
  88.4 0.9 pad_maximum_fusion.1
  89.3 2.5 %gather_fusion = bf16[4,4,144,128]{3,2,1,0:T(8,128)(2,1)} fusion(bf16[4,4,144,128]{3,2,1,0:T(8,128)(2,1)} %pad_maximum_fusion.1, s32[1024]{0:T(1024)S(1)} %pad_clamp_fusion), kind=kCustom, calls=%fused_computation | custom fusion | bytes 1179664 | tf_op jit(solution)/shard_map/gather | solution.py:608
  91.8 1.1 constant_dynamic-slice_fusion
  92.9 0.1 collective-permute-start.7
  93.0 1.6 %collective-permute-done.7.other_ref = bf16[2,4,144,128]{3,2,1,0:T(8,128)(2,1)S(1)} collective-permute-done((bf16[2,4,144,128]{3,2,1,0:T(8,128)(2,1)S(1)}, bf16[2,4,144,128]{3,2,1,0:T(8,128)(2,1)S(1)}, u32[]{:S(2)}, u32[]{:S(2)}) %collective-permute-start.7) | collective-permute-done | bytes 294944 | tf_op jit(solution)/shard_map/ppermute | solution.py:609
  94.6 0.2 merge_text.1.refs_0_
  94.7 2.2 %copy-done.1 = f32[32,2,128,128]{3,2,1,0:T(8,128)S(1)} copy-done((f32[32,2,128,128]{3,2,1,0:T(8,128)S(1)}, f32[32,2,128,128]{3,2,1,0:T(8,128)}, u32[]{:S(2)}) %copy-start.1) | copy-done | bytes 4194328
  96.9 8.9 %halo_keys.2 = (f32[16,2,128,128]{3,2,1,0:T(8,128)S(1)}, f32[16,2,8,128]{3,2,1,0:T(8,128)S(1)}, f32[16,2,8,128]{3,2,1,0:T(8,128)S(1)}) custom-call(s32[592]{0:T(1024)S(1)} %get-tuple-element.46.list_ref, s32[4]{0:T(128)S(1)} %get-tuple-element.47.n_ref, bf16[16,384,128]{2,1,0:T(8,128)(2,1)} %collective-permute-done.1.down_hbm, ...), custom_call_target="tpu_custom_call" | custom-call | flops 2000000000 | bytes 10000000 | tf_op jit(solution)/shard_map/halo_keys/pallas_call | solution.py:543
  105.9 3.1 %merge_cores.1 = bf16[16,272,128]{2,1,0:T(8,128)(2,1)} custom-call(f32[16,2,128,128]{3,2,1,0:T(8,128)S(1)} %get-tuple-element.66.acc_ref, f32[16,2,8,128]{3,2,1,0:T(8,128)S(1)} %get-tuple-element.67.m_ref, f32[16,2,8,128]{3,2,1,0:T(8,128)S(1)} %get-tuple-element.68.l_ref, bf16[16,272,128]{2,1,0:T(8,128)(2,1)} %collective-permute-done.8.got_ref), custom_call_target="tpu_custom_call" | custom-call | tf_op jit(solution)/shard_map/merge_cores/pallas_call | solution.py:619
  109.0 6.0 %all-to-all-start.2 = ((bf16[16,272,128]{2,1,0:T(8,128)(2,1)}), bf16[16,272,128]{2,1,0:T(8,128)(2,1)S(1)}, u32[]{:S(2)}, u32[]{:S(2)}) async-start(bf16[16,272,128]{2,1,0:T(8,128)(2,1)} %merge_cores.1), calls=%async_computation.2 | async-start | bytes 2228224 | tf_op jit(solution)/shard_map/all_to_all | solution.py:623
  115.1 4.0 %collective-permute-start.10 = (bf16[6,144,128]{2,1,0:T(8,128)(2,1)S(1)}, bf16[6,144,128]{2,1,0:T(8,128)(2,1)S(1)}, u32[]{:S(2)}, u32[]{:S(2)}) collective-permute-start(bf16[6,144,128]{2,1,0:T(8,128)(2,1)S(1)} %merge_text.1.refs_0_), channel_id=1, source_target_pairs={{0,64},{32,96},{64,0},{96,32},{1,65},{33,97},{65,1},{97,33},{2,66}... | collective-permute-start | bytes 663560 | tf_op jit(solution)/shard_map/ppermute | solution.py:475
  119.1 4.0 %collective-permute-done.11.refs_3_ = bf16[6,144,128]{2,1,0:T(8,128)(2,1)S(1)} collective-permute-done((bf16[6,144,128]{2,1,0:T(8,128)(2,1)S(1)}, bf16[6,144,128]{2,1,0:T(8,128)(2,1)S(1)}, u32[]{:S(2)}, u32[]{:S(2)}) %collective-permute-start.11) | collective-permute-done | bytes 221216 | tf_op jit(solution)/shard_map/ppermute | solution.py:475
  123.1 5.0 %collective-permute-done.10.refs_2_ = bf16[6,144,128]{2,1,0:T(8,128)(2,1)S(1)} collective-permute-done((bf16[6,144,128]{2,1,0:T(8,128)(2,1)S(1)}, bf16[6,144,128]{2,1,0:T(8,128)(2,1)S(1)}, u32[]{:S(2)}, u32[]{:S(2)}) %collective-permute-start.10) | collective-permute-done | bytes 221216 | tf_op jit(solution)/shard_map/ppermute | solution.py:475
  128.1 0.7 collective-permute-done.9.refs_1_
  128.9 1.0 final_text.1
  129.8 2.5 %all-to-all-done.2.got_ref = bf16[16,272,128]{2,1,0:T(8,128)(2,1)S(1)} async-done(((bf16[16,272,128]{2,1,0:T(8,128)(2,1)}), bf16[16,272,128]{2,1,0:T(8,128)(2,1)S(1)}, u32[]{:S(2)}, u32[]{:S(2)}) %all-to-all-start.2) | async-done | bytes 1114144 | tf_op jit(solution)/shard_map/all_to_all | solution.py:623
  132.4 1.2 final.1
  (47 shorter events, 0.4 us)
Async XLA Ops:
  3.7 8.1 %copy-start.6 = (bf16[256,384]{1,0:T(8,128)(2,1)S(1)}, bf16[256,384]{1,0:T(8,128)(2,1)}, u32[]{:S(2)}) copy-start(bf16[256,384]{1,0:T(8,128)(2,1)} %param.11) | copy-start | bytes 589828
  3.7 8.2 %copy-start.7 = (bf16[256,384]{1,0:T(8,128)(2,1)S(1)}, bf16[256,384]{1,0:T(8,128)(2,1)}, u32[]{:S(2)}) copy-start(bf16[256,384]{1,0:T(8,128)(2,1)} %param.12) | copy-start | bytes 589828
  3.7 8.4 %copy-start.8 = (bf16[256,384]{1,0:T(8,128)(2,1)S(1)}, bf16[256,384]{1,0:T(8,128)(2,1)}, u32[]{:S(2)}) copy-start(bf16[256,384]{1,0:T(8,128)(2,1)} %param.13) | copy-start | bytes 589828
  3.7 32.5 %all-to-all-start = ((bf16[16,384,128]{2,1,0:T(8,128)(2,1)}), bf16[16,384,128]{2,1,0:T(8,128)(2,1)S(1)}, u32[]{:S(2)}, u32[]{:S(2)}) async-start(bf16[16,384,128]{2,1,0:T(8,128)(2,1)} %prep_kv.1), calls=%async_computation | async-start | bytes 3145728 | tf_op jit(solution)/shard_map/all_to_all | solution.py:568
  11.7 1.4 %copy-start.4 = (s32[128,128]{1,0:T(8,128)S(1)}, s32[128,128]{1,0:T(8,128)}, u32[]{:S(2)}) copy-start(s32[128,128]{1,0:T(8,128)} %mask_ref) | copy-start | bytes 196612
  13.1 14.0 %collective-permute-start = (bf16[3,256,384]{1,2,0:T(8,128)(2,1)}, bf16[3,256,384]{1,2,0:T(8,128)(2,1)}, u32[]{:S(2)}, u32[]{:S(2)}) collective-permute-start(bf16[3,256,384]{1,2,0:T(8,128)(2,1)} %pad_maximum_fusion), channel_id=1, source_target_pairs={{0,1},{1,0},{2,3},{3,2},{4,5},{5,4},{6,7},{7,6},{8,9},{9,8},{10,11... | collective-permute-start | bytes 1769480 | tf_op jit(solution)/shard_map/ppermute | solution.py:572
  27.1 2.6 %copy-start.3 = (bf16[128,3072]{1,0:T(8,128)(2,1)S(1)}, bf16[128,3072]{1,0:T(8,128)(2,1)}, u32[]{:S(2)}) copy-start(bf16[128,3072]{1,0:T(8,128)(2,1)} %q_ref) | copy-start | bytes 2359300
  27.2 0.8 copy-start.5
  30.0 1.0 copy-start.2
  36.2 20.4 %all-to-all-start.1 = ((bf16[16,256,128]{2,1,0:T(8,128)(2,1)}), bf16[16,256,128]{2,1,0:T(8,128)(2,1)S(1)}, u32[]{:S(2)}, u32[]{:S(2)}) async-start(bf16[16,256,128]{2,1,0:T(8,128)(2,1)} %copy-done.2), calls=%async_computation.1 | async-start | bytes 2097152 | tf_op jit(solution)/shard_map/all_to_all | solution.py:601
  39.8 38.5 %collective-permute-start.2 = (bf16[16,384,128]{2,1,0:T(8,128)(2,1)S(1)}, bf16[16,384,128]{2,1,0:T(8,128)(2,1)}, u32[]{:S(2)}, u32[]{:S(2)}) collective-permute-start(bf16[16,384,128]{2,1,0:T(8,128)(2,1)S(1)} %all-to-all-done.kv_ref.kv_hbm), channel_id=1, source_target_pairs={{32,0},{64,32},{96,64},{33,1},{65,33},{97,65},{34,2},{66,34},{98,6... | collective-permute-start | bytes 4718600 | tf_op jit(solution)/shard_map/ppermute | solution.py:600
  42.2 36.9 %collective-permute-start.1 = (bf16[16,384,128]{2,1,0:T(8,128)(2,1)S(1)}, bf16[16,384,128]{2,1,0:T(8,128)(2,1)}, u32[]{:S(2)}, u32[]{:S(2)}) collective-permute-start(bf16[16,384,128]{2,1,0:T(8,128)(2,1)S(1)} %all-to-all-done.kv_ref.kv_hbm), channel_id=1, source_target_pairs={{0,32},{32,64},{64,96},{1,33},{33,65},{65,97},{2,34},{34,66},{66,9... | collective-permute-start | bytes 4718600 | tf_op jit(solution)/shard_map/ppermute | solution.py:599
  56.6 2.7 %collective-permute-start.3 = (bf16[16,256,128]{2,1,0:T(8,128)(2,1)S(1)}, bf16[16,256,128]{2,1,0:T(8,128)(2,1)S(1)}, u32[]{:S(2)}, u32[]{:S(2)}) collective-permute-start(bf16[16,256,128]{2,1,0:T(8,128)(2,1)S(1)} %all-to-all-done.1.q_hbm), channel_id=1, source_target_pairs={{0,1},{1,0},{2,3},{3,2},{4,5},{5,4},{6,7},{7,6},{8,9},{9,8},{10,11... | collective-permute-start | bytes 3145736 | tf_op jit(solution)/shard_map/ppermute | solution.py:604
  56.6 21.7 %collective-permute-start.6 = (bf16[4,144,128]{2,1,0:T(8,128)(2,1)S(1)}, bf16[4,144,128]{2,1,0:T(8,128)(2,1)S(1)}, u32[]{:S(2)}, u32[]{:S(2)}) collective-permute-start(bf16[4,144,128]{2,1,0:T(8,128)(2,1)S(1)} %text_keys.1), channel_id=1, source_target_pairs={{0,24},{8,0},{16,8},{24,16},{1,25},{9,1},{17,9},{25,17},{2,26},{10... | collective-permute-start | bytes 442376 | tf_op jit(solution)/shard_map/ppermute | solution.py:475
  57.2 21.1 %collective-permute-start.5 = (bf16[4,144,128]{2,1,0:T(8,128)(2,1)S(1)}, bf16[4,144,128]{2,1,0:T(8,128)(2,1)S(1)}, u32[]{:S(2)}, u32[]{:S(2)}) collective-permute-start(bf16[4,144,128]{2,1,0:T(8,128)(2,1)S(1)} %text_keys.1), channel_id=1, source_target_pairs={{0,16},{8,24},{16,0},{24,8},{1,17},{9,25},{17,1},{25,9},{2,18},{10... | collective-permute-start | bytes 442376 | tf_op jit(solution)/shard_map/ppermute | solution.py:475
  59.3 19.1 %collective-permute-start.4 = (bf16[4,144,128]{2,1,0:T(8,128)(2,1)S(1)}, bf16[4,144,128]{2,1,0:T(8,128)(2,1)S(1)}, u32[]{:S(2)}, u32[]{:S(2)}) collective-permute-start(bf16[4,144,128]{2,1,0:T(8,128)(2,1)S(1)} %text_keys.1), channel_id=1, source_target_pairs={{0,8},{8,16},{16,24},{24,0},{1,9},{9,17},{17,25},{25,1},{2,10},{10... | collective-permute-start | bytes 442376 | tf_op jit(solution)/shard_map/ppermute | solution.py:475
  78.3 9.3 %copy-start = (f32[32,2,128,128]{3,2,1,0:T(8,128)}, f32[32,2,128,128]{3,2,1,0:T(8,128)S(1)}, u32[]{:S(2)}) copy-start(f32[32,2,128,128]{3,2,1,0:T(8,128)S(1)} %get-tuple-element.63.acc_hbm) | copy-start | bytes 12582916
  78.3 0.8 copy-start.9
  78.3 0.8 copy-start.11
  78.4 0.8 copy-start.13
  79.1 9.2 %copy-start.10 = (bf16[4,144,128]{2,1,0:T(8,128)(2,1)S(1)}, bf16[4,144,128]{2,1,0:T(8,128)(2,1)}, u32[]{:S(2)}) copy-start(bf16[4,144,128]{2,1,0:T(8,128)(2,1)} %copy-done.9) | copy-start | bytes 442372
  79.1 9.2 %copy-start.12 = (bf16[4,144,128]{2,1,0:T(8,128)(2,1)S(1)}, bf16[4,144,128]{2,1,0:T(8,128)(2,1)}, u32[]{:S(2)}) copy-start(bf16[4,144,128]{2,1,0:T(8,128)(2,1)} %copy-done.11) | copy-start | bytes 442372
  79.1 9.2 %copy-start.14 = (bf16[4,144,128]{2,1,0:T(8,128)(2,1)S(1)}, bf16[4,144,128]{2,1,0:T(8,128)(2,1)}, u32[]{:S(2)}) copy-start(bf16[4,144,128]{2,1,0:T(8,128)(2,1)} %copy-done.13) | copy-start | bytes 442372
  87.6 18.2 %collective-permute-start.8 = (bf16[16,272,128]{2,1,0:T(8,128)(2,1)S(1)}, bf16[16,272,128]{2,1,0:T(8,128)(2,1)}, u32[]{:S(2)}, u32[]{:S(2)}) collective-permute-start(bf16[16,272,128]{2,1,0:T(8,128)(2,1)S(1)} %halo_keys.3), channel_id=1, source_target_pairs={{0,1},{1,0},{2,3},{3,2},{4,5},{5,4},{6,7},{7,6},{8,9},{9,8},{10,11... | collective-permute-start | bytes 3342344 | tf_op jit(solution)/shard_map/ppermute | solution.py:617
  92.9 1.7 %collective-permute-start.7 = (bf16[2,4,144,128]{3,2,1,0:T(8,128)(2,1)S(1)}, bf16[2,4,144,128]{3,2,1,0:T(8,128)(2,1)S(1)}, u32[]{:S(2)}, u32[]{:S(2)}) collective-permute-start(bf16[2,4,144,128]{3,2,1,0:T(8,128)(2,1)S(1)} %get-tuple-element.72), channel_id=1, source_target_pairs={{0,1},{1,0},{2,3},{3,2},{4,5},{5,4},{6,7},{7,6},{8,9},{9,8},{10,11... | collective-permute-start | bytes 884744 | tf_op jit(solution)/shard_map/ppermute | solution.py:609
  94.7 2.2 %copy-start.1 = (f32[32,2,128,128]{3,2,1,0:T(8,128)S(1)}, f32[32,2,128,128]{3,2,1,0:T(8,128)}, u32[]{:S(2)}) copy-start(f32[32,2,128,128]{3,2,1,0:T(8,128)} %copy-done) | copy-start | bytes 12582916
  109.0 23.4 %all-to-all-start.2 = ((bf16[16,272,128]{2,1,0:T(8,128)(2,1)}), bf16[16,272,128]{2,1,0:T(8,128)(2,1)S(1)}, u32[]{:S(2)}, u32[]{:S(2)}) async-start(bf16[16,272,128]{2,1,0:T(8,128)(2,1)} %merge_cores.1), calls=%async_computation.2 | async-start | bytes 2228224 | tf_op jit(solution)/shard_map/all_to_all | solution.py:623
  115.0 8.1 %collective-permute-start.11 = (bf16[6,144,128]{2,1,0:T(8,128)(2,1)S(1)}, bf16[6,144,128]{2,1,0:T(8,128)(2,1)S(1)}, u32[]{:S(2)}, u32[]{:S(2)}) collective-permute-start(bf16[6,144,128]{2,1,0:T(8,128)(2,1)S(1)} %merge_text.1.refs_0_), channel_id=1, source_target_pairs={{0,96},{32,0},{64,32},{96,64},{1,97},{33,1},{65,33},{97,65},{2,98}... | collective-permute-start | bytes 663560 | tf_op jit(solution)/shard_map/ppermute | solution.py:475
  115.1 13.0 %collective-permute-start.10 = (bf16[6,144,128]{2,1,0:T(8,128)(2,1)S(1)}, bf16[6,144,128]{2,1,0:T(8,128)(2,1)S(1)}, u32[]{:S(2)}, u32[]{:S(2)}) collective-permute-start(bf16[6,144,128]{2,1,0:T(8,128)(2,1)S(1)} %merge_text.1.refs_0_), channel_id=1, source_target_pairs={{0,64},{32,96},{64,0},{96,32},{1,65},{33,97},{65,1},{97,33},{2,66}... | collective-permute-start | bytes 663560 | tf_op jit(solution)/shard_map/ppermute | solution.py:475
  119.1 9.8 %collective-permute-start.9 = (bf16[6,144,128]{2,1,0:T(8,128)(2,1)S(1)}, bf16[6,144,128]{2,1,0:T(8,128)(2,1)S(1)}, u32[]{:S(2)}, u32[]{:S(2)}) collective-permute-start(bf16[6,144,128]{2,1,0:T(8,128)(2,1)S(1)} %merge_text.1.refs_0_), channel_id=1, source_target_pairs={{0,32},{32,64},{64,96},{96,0},{1,33},{33,65},{65,97},{97,1},{2,34}... | collective-permute-start | bytes 663560 | tf_op jit(solution)/shard_map/ppermute | solution.py:475

commit v2 on v1

--- a/solution.py
+++ b/solution.py
@@ -23,8 +23,9 @@
 neg_fill = -1e30
 FLAG = 4096
 FIRST_LEN = SLAB * STEP
-REST_LEN = SLAB * (HALF + STEP) + 4 * STEP
-HALO_LEN = HALF * (2 * HALF + STEP) + 4 * STEP
+PAD = (UNROLL + 2) * STEP
+REST_LEN = SLAB * (HALF + STEP) + PAD
+HALO_LEN = HALF * (2 * HALF + STEP) + PAD
 
 VM = pl.BlockSpec(memory_space=pltpu.VMEM)
 SM = pl.BlockSpec(memory_space=pltpu.SMEM)
@@ -136,8 +137,8 @@
 
     end = lax.fori_loop(0, SLAB, own, jnp.int32(0))
     n_ref[0] = end // STEP
-    for k in range(4 * STEP):
-        rest_ref[end + k] = FLAG
+    for k in range(PAD):
+        rest_ref[end + k] = FLAG | SLAB * 64
     for which, (ref, base) in enumerate(((halo_a_ref, HALF), (halo_b_ref, 0))):
 
         def far(n, pos):
@@ -156,8 +157,8 @@
 
         end = lax.fori_loop(0, HALF, far, jnp.int32(0))
         n_ref[1 + which] = end // STEP
-        for k in range(4 * STEP):
-            ref[end + k] = FLAG
+        for k in range(PAD):
+            ref[end + k] = FLAG | HALF * 64
     n_ref[3] = 0
 
 
@@ -181,23 +182,25 @@
     return jnp.concatenate([jnp.concatenate(low, axis=1), jnp.concatenate(high, axis=1)], axis=0)
 
 
-def scores(kv_ref, q_ref, s_ref, t_ref, buf, q, js, live=None):
+class Work:
+    def __init__(self, kv, q, s, p, top, factor, acc, m, l):
+        self.kv, self.q, self.s, self.p, self.top, self.factor = kv, q, s, p, top, factor
+        self.acc, self.m, self.l = acc, m, l
+
+
+def scores(work, buf, q, js, live=None):
     for h, (low, size, row) in enumerate(((0, 128, 0), (512, 64, 128))):
-        keys = jnp.concatenate([kv_ref[j, row : row + size] for j in js], axis=0)
-        s = jnp.dot(keys, q_ref[q, 128 * h : 128 * h + 128], preferred_element_type=jnp.float32)
+        keys = jnp.concatenate([work.kv[j, row : row + size] for j in js], axis=0)
+        s = jnp.dot(keys, work.q[q, 128 * h : 128 * h + 128], preferred_element_type=jnp.float32)
         if live is not None:
             rows = lax.broadcasted_iota(jnp.int32, (size, DH), 0)
             s = jnp.concatenate([jnp.where(rows < live[h], s[:size], neg_fill), s[size:]], axis=0)
-        s_ref[buf, low : low + STEP * size] = s
-        t_ref[buf, h] = jnp.broadcast_to(column_max(s), (8, DH))
+        work.s[buf, low : low + STEP * size] = s
+        work.top[buf, h] = jnp.broadcast_to(column_max(s), (8, DH))
 
 
 def column_max(s):
     return jnp.max(fold(s, jnp.max), axis=0, keepdims=True)
-
-
-def weights(parts, top, gaps):
-    return [jnp.exp2((s - (top + gap)) * LOG2) for s, gap in zip(parts, gaps)]
 
 
 def values_of(kv_ref, js, h):
@@ -206,73 +209,67 @@
     return wide_c(kv_ref, js)
 
 
-def parts_of(s_ref, buf, h):
-    low, size = (0, 128) if h == 0 else (512, 64)
-    return [s_ref[buf, low + size * k : low + size * (k + 1)] for k in range(STEP)]
-
-
-def first_step(kv_ref, s_ref, t_ref, acc_ref, m_ref, l_ref, buf, q, js, gaps):
+def soften(work, buf, q, gaps, first=False):
     for h in range(2):
-        top = t_ref[buf, h]
-        w = weights(parts_of(s_ref, buf, h), top[:1], gaps)
-        m_ref[q, h] = top
-        l_ref[q, h] = sum(fold(x, jnp.sum) for x in w)
-        w = jnp.concatenate(w, axis=0).astype(jnp.bfloat16)
-        acc_ref[q, h] = jnp.dot(values_of(kv_ref, js, h), w, preferred_element_type=jnp.float32)
-
-
-def next_step(kv_ref, s_ref, t_ref, acc_ref, m_ref, l_ref, buf, q, js, gaps):
-    for h in range(2):
-        old = m_ref[q, h]
-        new = jnp.maximum(old, t_ref[buf, h])
-        factor = jnp.exp2((old - new) * LOG2)
-        w = weights(parts_of(s_ref, buf, h), new[:1], gaps)
-        m_ref[q, h] = new
-        l_ref[q, h] = l_ref[q, h] * factor + sum(fold(x, jnp.sum) for x in w)
-        w = jnp.concatenate(w, axis=0).astype(jnp.bfloat16)
-        acc_ref[q, h] = acc_ref[q, h] * factor[:1] + jnp.dot(
-            values_of(kv_ref, js, h), w, preferred_element_type=jnp.float32
-        )
-
-
-def run_list(kv_ref, q_ref, s_ref, t_ref, acc_ref, m_ref, l_ref, list_ref, steps):
+        top = work.top[buf, h]
+        if not first:
+            old = work.m[q, h]
+            top = jnp.maximum(old, top)
+            factor = jnp.exp2((old - top) * LOG2)
+            work.factor[buf, h] = factor
+        low, size = (0, 128) if h == 0 else (512, 64)
+        sums = []
+        for k, gap in enumerate(gaps):
+            rows = slice(low + size * k, low + size * (k + 1))
+            w = jnp.exp2((work.s[buf, rows] - (top[:1] + gap)) * LOG2)
+            sums.append(fold(w, jnp.sum))
+            work.p[buf, rows] = w.astype(jnp.bfloat16)
+        total = sum(sums)
+        work.m[q, h] = top
+        work.l[q, h] = total if first else work.l[q, h] * factor + total
+
+
+def gather(work, buf, q, js, first=False):
+    for h, rows in enumerate((slice(0, 512), slice(512, 768))):
+        out = jnp.dot(values_of(work.kv, js, h), work.p[buf, rows], preferred_element_type=jnp.float32)
+        work.acc[q, h] = out if first else work.acc[q, h] * work.factor[buf, h, 0:1] + out
+
+
+def pipelined(score, soft, add, rounds):
+    score(0, 0)
+    score(1, 1)
+    soft(0, 0)
+
+    def body(i, carry):
+        for k in range(UNROLL):
+            t = UNROLL * i + k
+            score(t + 2, k % 2)
+            add(t, k % 2)
+            soft(t + 1, (k + 1) % 2)
+        return carry
+
+    lax.fori_loop(0, rounds, body, 0)
+
+
+def run_list(work, list_ref, steps):
     def score(t, buf):
         q, js, _ = slots(list_ref, t)
-        scores(kv_ref, q_ref, s_ref, t_ref, buf, q, js)
-
-    def step(t, buf):
-        q, js, gaps = slots(list_ref, t)
-        next_step(kv_ref, s_ref, t_ref, acc_ref, m_ref, l_ref, buf, q, js, gaps)
-
-    score(0, 0)
-
-    def body(i, carry):
-        for k in range(UNROLL):
-            score(UNROLL * i + k + 1, (k + 1) % 2)
-            step(UNROLL * i + k, k % 2)
-        return carry
-
-    lax.fori_loop(0, steps // UNROLL, body, 0)
-
-    def rest(i, carry):
-        @pl.when(i % 2 == 0)
-        def _():
-            score(i + 1, 1)
-            step(i, 0)
-
-        @pl.when(i % 2 == 1)
-        def _():
-            score(i + 1, 0)
-            step(i, 1)
-
-        return carry
-
-    lax.fori_loop(steps // UNROLL * UNROLL, steps, rest, 0)
+        scores(work, buf, q, js)
+
+    def soft(t, buf):
+        q, _, gaps = slots(list_ref, t)
+        soften(work, buf, q, gaps)
+
+    def add(t, buf):
+        q, js, _ = slots(list_ref, t)
+        gather(work, buf, q, js)
+
+    pipelined(score, soft, add, (steps + UNROLL - 1) // UNROLL)
 
 
 def own_kernel(
     first_ref, rest_ref, n_ref, live_ref, kv_hbm, text_hbm, q_hbm, other_hbm,
-    acc_ref, m_ref, l_ref, kv_ref, q_ref, s_ref, t_ref, sems,
+    acc_ref, m_ref, l_ref, kv_ref, q_ref, s_ref, p_ref, t_ref, f_ref, sems,
 ):
     copies = [
         pltpu.make_async_copy(kv_hbm, kv_ref.at[pl.ds(0, HALF)], sems.at[0]),
@@ -280,6 +277,7 @@
         pltpu.make_async_copy(q_hbm, q_ref.at[pl.ds(0, HALF)], sems.at[2]),
         pltpu.make_async_copy(other_hbm, q_ref.at[pl.ds(HALF, HALF)], sems.at[3]),
     ]
+    work = Work(kv_ref, q_ref, s_ref, p_ref, t_ref, f_ref, acc_ref, m_ref, l_ref)
     for copy in copies:
         copy.start()
     for copy in copies:
@@ -292,35 +290,36 @@
         return [jnp.int32(HALF)] + [code & 63 for code in codes], gaps
 
     def score(n, buf):
-        live = (live_ref[0], live_ref[1])
-        scores(kv_ref, q_ref, s_ref, t_ref, buf, n, line(n)[0], live)
-
-    def step(n, buf):
-        js, gaps = line(n)
-        first_step(kv_ref, s_ref, t_ref, acc_ref, m_ref, l_ref, buf, n, js, gaps)
-
-    score(0, 0)
-
-    def body(i, carry):
-        for k in range(UNROLL):
-            score(jnp.minimum(UNROLL * i + k + 1, SLAB - 1), (k + 1) % 2)
-            step(UNROLL * i + k, k % 2)
-        return carry
-
-    lax.fori_loop(0, SLAB // UNROLL, body, 0)
-    run_list(kv_ref, q_ref, s_ref, t_ref, acc_ref, m_ref, l_ref, rest_ref, n_ref[0])
-
-
-def text_kernel(live_ref, kv_ref, text_ref, q_ref, out_ref, s_ref, t_ref, acc_ref, m_ref, l_ref):
+        n = jnp.minimum(n, SLAB - 1)
+        scores(work, buf, n, line(n)[0], (live_ref[0], live_ref[1]))
+
+    def soft(n, buf):
+        n = jnp.minimum(n, SLAB - 1)
+        soften(work, buf, n, line(n)[1], True)
+
+    def add(n, buf):
+        gather(work, buf, n, line(n)[0], True)
+
+    pipelined(score, soft, add, SLAB // UNROLL)
+    run_list(work, rest_ref, n_ref[0])
+
+
+def text_kernel(
+    live_ref, kv_ref, text_ref, q_ref, out_ref, s_ref, p_ref, t_ref, f_ref, acc_ref, m_ref, l_ref
+):
     none = [jnp.float32(0)] * STEP
     live = (live_ref[2], live_ref[3])
-
-    def one(block, carry):
-        for start in range(0, HALF, STEP):
-            js = list(range(start, start + STEP))
-            scores(kv_ref, q_ref, s_ref, t_ref, 0, block, js)
-            step = next_step if start else first_step
-            step(kv_ref, s_ref, t_ref, acc_ref, m_ref, l_ref, 0, block, js, none)
+    work = Work(kv_ref, q_ref, s_ref, p_ref, t_ref, f_ref, acc_ref, m_ref, l_ref)
+
+    for start in range(0, HALF, STEP):
+        js = list(range(start, start + STEP))
+        for block in range(NTQ):
+            scores(work, block, block, js)
+        for block in range(NTQ):
+            soften(work, block, block, none, start == 0)
+        for block in range(NTQ):
+            gather(work, block, block, js, start == 0)
+    for block in range(NTQ):
         for h, (low, size, row) in enumerate(((0, 128, 0), (512, 64, 128))):
             s = jnp.dot(
                 text_ref[0, row : row + size],
@@ -339,9 +338,6 @@
                 v, w.astype(jnp.bfloat16), preferred_element_type=jnp.float32
             )
             put_text(out_ref, h * NTQ + block, new[:1], total, acc)
-        return carry
-
-    lax.fori_loop(0, NTQ, one, 0)
 
 
 def row_sum(x):
@@ -361,12 +357,18 @@
     return top, total, sum(b[0:128].astype(jnp.float32) * f for b, f in zip(blocks, factors))
 
 
-def merge_text_kernel(mine_ref, other_ref, out_ref):
+def merge_text_kernel(member_ref, here_ref, there_ref, out_ref):
+    first = member_ref[0] == 0
+    rows = 2 * NTQ
     for block in range(NTQ):
         for head in range(3):
             at = (0 if head < 2 else NTQ) + block
-            members = (head,) if head < 2 else (0, 1)
-            blocks = [ref[i, at] for ref in (mine_ref, other_ref) for i in members]
+            pairs = [(here_ref[core * rows + at], there_ref[core * rows + at]) for core in range(2)]
+            if head == 2:
+                blocks = [part for both in pairs for part in both]
+            else:
+                ours = first if head == 0 else jnp.logical_not(first)
+                blocks = [jnp.where(ours, *both) for both in pairs]
             put_text(out_ref, head * NTQ + block, *merged(blocks))
 
 
@@ -403,23 +405,24 @@
     *refs,
 ):
     if which == 0:
-        out_ref, kv_ref, q_ref, s_ref, t_ref, acc_ref, m_ref, l_ref, sems = refs
+        out_ref, kv_ref, q_ref, s_ref, p_ref, t_ref, f_ref, acc_ref, m_ref, l_ref, sems = refs
     else:
-        acc_ref, m_ref, l_ref, kv_ref, q_ref, s_ref, t_ref, sems = refs
+        acc_ref, m_ref, l_ref, kv_ref, q_ref, s_ref, p_ref, t_ref, f_ref, sems = refs
     base = HALF if which == 0 else 0
     copies = [
         pltpu.make_async_copy(down_hbm, kv_ref.at[pl.ds(0, HALF)], sems.at[0]),
         pltpu.make_async_copy(up_hbm, kv_ref.at[pl.ds(HALF, HALF)], sems.at[1]),
-        pltpu.make_async_copy(q_hbm, q_ref, sems.at[2]),
-        pltpu.make_async_copy(acc_hbm.at[pl.ds(base, HALF)], acc_ref, sems.at[3]),
-        pltpu.make_async_copy(m_hbm.at[pl.ds(base, HALF)], m_ref, sems.at[4]),
-        pltpu.make_async_copy(l_hbm.at[pl.ds(base, HALF)], l_ref, sems.at[5]),
+        pltpu.make_async_copy(q_hbm, q_ref.at[pl.ds(0, HALF)], sems.at[2]),
+        pltpu.make_async_copy(acc_hbm.at[pl.ds(base, HALF)], acc_ref.at[pl.ds(0, HALF)], sems.at[3]),
+        pltpu.make_async_copy(m_hbm.at[pl.ds(base, HALF)], m_ref.at[pl.ds(0, HALF)], sems.at[4]),
+        pltpu.make_async_copy(l_hbm.at[pl.ds(base, HALF)], l_ref.at[pl.ds(0, HALF)], sems.at[5]),
     ]
     for copy in copies:
         copy.start()
     for copy in copies:
         copy.wait()
-    run_list(kv_ref, q_ref, s_ref, t_ref, acc_ref, m_ref, l_ref, list_ref, n_ref[1 + which])
+    work = Work(kv_ref, q_ref, s_ref, p_ref, t_ref, f_ref, acc_ref, m_ref, l_ref)
+    run_list(work, list_ref, n_ref[1 + which])
     if which == 0:
 
         def finish(n, carry):
@@ -498,13 +501,15 @@
 def run_own(first, rest, counts, live, kv, text_rec, q, q_other):
     return pl.pallas_call(
         own_kernel,
-        out_shape=state(SLAB),
+        out_shape=state(SLAB + 1),
         in_specs=[SM] * 4 + [ANY] * 4,
         out_specs=[VM] * 3,
         scratch_shapes=[
             pltpu.VMEM((HALF + 1, REC, DH), jnp.bfloat16),
-            pltpu.VMEM((SLAB, QREC, DH), jnp.bfloat16),
+            pltpu.VMEM((SLAB + 1, QREC, DH), jnp.bfloat16),
             pltpu.VMEM((2, 768, DH), jnp.float32),
+            pltpu.VMEM((2, 768, DH), jnp.bfloat16),
+            pltpu.VMEM((2, 2, 8, DH), jnp.float32),
             pltpu.VMEM((2, 2, 8, DH), jnp.float32),
             pltpu.SemaphoreType.DMA((4,)),
         ],
@@ -515,7 +520,8 @@
 
 
 def run_text(live, kv, text_rec, tq):
-    scratch = [pltpu.VMEM((1, 768, DH), jnp.float32), pltpu.VMEM((1, 2, 8, DH), jnp.float32)]
+    scratch = [pltpu.VMEM((NTQ, 768, DH), jnp.float32), pltpu.VMEM((NTQ, 768, DH), jnp.bfloat16)]
+    scratch += [pltpu.VMEM((NTQ, 2, 8, DH), jnp.float32)] * 2
     return pl.pallas_call(
         text_kernel,
         out_shape=shape((2 * NTQ, 144, DH)),
@@ -531,15 +537,17 @@
 def run_halo(which, queries, table, counts, from_down, from_up, acc, m, l):
     scratch = [
         pltpu.VMEM((SLAB, REC, DH), jnp.bfloat16),
-        pltpu.VMEM((HALF, QREC, DH), jnp.bfloat16),
+        pltpu.VMEM((HALF + 1, QREC, DH), jnp.bfloat16),
         pltpu.VMEM((2, 768, DH), jnp.float32),
-            pltpu.VMEM((2, 2, 8, DH), jnp.float32),
+        pltpu.VMEM((2, 768, DH), jnp.bfloat16),
+        pltpu.VMEM((2, 2, 8, DH), jnp.float32),
+        pltpu.VMEM((2, 2, 8, DH), jnp.float32),
     ]
     if which == 0:
         out = shape((HALF, OREC, DH))
-        scratch += [pltpu.VMEM(s.shape, jnp.float32) for s in state(HALF)]
+        scratch += [pltpu.VMEM(s.shape, jnp.float32) for s in state(HALF + 1)]
     else:
-        out = state(HALF)
+        out = state(HALF + 1)
     return pl.pallas_call(
         functools.partial(halo_kernel, which),
         out_shape=out,
@@ -600,22 +608,24 @@
     from_up = lax.ppermute(kv, "y", [(1, 0), (2, 1), (3, 2)])
     q = lax.all_to_all(q_send, chips, 0, 0, tiled=True)
     text_part = run_text(live, kv, text_rec, tq)
-    q, text_part = together((q, text_part))
+    here = jnp.concatenate([text_part, lax.ppermute(text_part, "c", swap)])
+    q, here = together((q, here))
     q_other = lax.ppermute(q, "c", swap)
-    text_ring = ring(text_part, "z")
+    there = lax.ppermute(here, "z", [(0, 1), (1, 0), (2, 3), (3, 2)])
     acc, m, l = run_own(first, rest, counts, live, kv, text_rec, q, q_other)
-    acc, *text_ring = together((acc, *text_ring))
-    parts = jnp.stack(text_ring)[(z - jnp.arange(4)) % 4]
-    theirs = lax.ppermute(lax.dynamic_slice_in_dim(parts, 2 - 2 * c, 2, 0), "c", swap)
+    acc, there = together((acc, there))
     heads = pl.pallas_call(
-        merge_text_kernel, out_shape=shape((3 * NTQ, 144, DH)), in_specs=[VM, VM], out_specs=VM,
+        merge_text_kernel, out_shape=shape((3 * NTQ, 144, DH)), in_specs=[SM, VM, VM], out_specs=VM,
         compiler_params=PARAMS, name="merge_text",
-    )(lax.dynamic_slice_in_dim(parts, 2 * c, 2, 0), theirs)
+    )(member.astype(jnp.int32)[None], here, there)
+    acc, heads = together((acc, heads))
+    far = lax.ppermute(heads, "z", [(0, 2), (1, 3), (2, 0), (3, 1)])
+    heads = jnp.where(c == pair, heads, far)
 
     partial = run_halo(0, q_other, halo_a, counts, from_down, from_up, acc, m, l)
-    q, heads = together((q, heads))
     got = lax.ppermute(partial, "c", swap)
     acc2, m2, l2 = run_halo(1, q, halo_b, counts, from_down, from_up, acc, m, l)
+    got, heads = together((got, heads))
     record = pl.pallas_call(
         merge_kernel, out_shape=shape((HALF, OREC, DH)), in_specs=[VM] * 4, out_specs=VM,
         compiler_params=PARAMS, name="merge_cores",

time: 136 us -> 129 us (0.949); the launches traced: 134 us -> 128 us
  local copies, waits for them, and re-layouts: 9.45 us -> 4.65 us
  Pallas kernels: 62.6 us -> 58.8 us
  waiting for transfers between devices: 27.8 us -> 30.6 us
    ppermute x1 -> x3, starting transfers between devices: 0.1 us -> 3.31 us  [the longest x1 3.22 us: local(): far = lax.ppermute(heads, 'z', [(0, 2), (1, 3), (2, 0), (3, 1)])]
    all_to_all x1, waiting for transfers between devices: 2.55 us -> 5.72 us  [local(): back = lax.all_to_all(record, chips, 0, 0, tiled=True)]
    ppermute x6 -> x3, starting transfers between devices: 5.2 us -> 2.09 us  [ring(): return [x] + [lax.ppermute(x, axis, route) for route in routes]]
    unnamed x30 -> x12, local copies, waits for them, and re-layouts: 4.02 us -> 0.98 us
    ppermute x1, waiting for transfers between devices: 0.01 us -> 2.62 us  [local(): from_up = lax.ppermute(kv, 'y', [(1, 0), (2, 1), (3, 2)])]
    gather x1 -> x0, local copies, waits for them, and re-layouts: 2.52 us -> none  [local(): parts = jnp.stack(text_ring)[(z - jnp.arange(4)) % 4]]
    all_to_all x1, waiting for transfers between devices: 5.17 us -> 3.33 us  [local(): kv = lax.all_to_all(kv_send, chips, 0, 0, tiled=True)]
    all_to_all x1, waiting for transfers between devices: 6.51 us -> 5.01 us  [local(): q = lax.all_to_all(q_send, chips, 0, 0, tiled=True)]
  transfers between devices with their start and end apart: 15 -> 14, of which waited for: 9 -> 9; matrix products, arithmetic and copies ran while one was open for 6% -> 5% of each run, Pallas kernels for 35% -> 34%
where the time goes in v2:
time: 129 us; the launch traced here: 128 us
  Pallas kernels  58.8 us (46%)
  waiting for transfers between devices  30.6 us (24%)
  starting transfers between devices  30.5 us (24%)
  local copies, waits for them, and re-layouts  4.65 us (4%)
  other arithmetic  2.27 us (2%)
  between operations  1.66 us (1%)
    pallas_call x1, Pallas kernels, run_own(): pl.pallas_call(own_kernel, out_shape=state(SLAB + 1), in_specs=[SM] * 4 +...  18.1 us
    pallas_call x2, Pallas kernels, run_halo(): pl.pallas_call(functools.partial(halo_kernel, which), out_shape=out, in_s...  16.7 us
    pallas_call x1, Pallas kernels, run_lists(): pl.pallas_call(lists_kernel, out_shape=[shape((n,), jnp.int32) for n in (...  13.9 us
    ppermute x3, waiting for transfers between devices, ring(): return [x] + [lax.ppermute(x, axis, route) for route in routes]  9.92 us
    all_to_all x1, starting transfers between devices, local(): kv = lax.all_to_all(kv_send, chips, 0, 0, tiled=True)  8.02 us
    all_to_all x1, waiting for transfers between devices, local(): back = lax.all_to_all(record, chips, 0, 0, tiled=True)  5.72 us
    all_to_all x1, starting transfers between devices, local(): q = lax.all_to_all(q_send, chips, 0, 0, tiled=True)  5.02 us
    all_to_all x1, waiting for transfers between devices, local(): q = lax.all_to_all(q_send, chips, 0, 0, tiled=True)  5.01 us
  transfers between devices with their start and end apart: 14, of which 9 were waited for; matrix products, arithmetic and copies ran while one was open for 5% of the time, Pallas kernels for 34%

profile of v2, /device:TPU:8, one launch (start us, length us, event | category | flops | bytes accessed | tf_op | source)
XLA Modules:
  0.0 128.5 jit_solution(3882576001809281504)
XLA Ops:
  0.6 3.0 %prep_kv.1 = bf16[16,384,128]{2,1,0:T(8,128)(2,1)} custom-call(bf16[128,3072]{1,0:T(8,128)(2,1)} %k_hbm.1, bf16[128,3072]{1,0:T(8,128)(2,1)} %v_hbm.1), custom_call_target="tpu_custom_call" | custom-call | tf_op jit(solution)/shard_map/prep_kv/pallas_call | solution.py:571
  3.7 0.0 copy-start.3
  3.7 0.0 copy-start.4
  3.7 8.0 %all-to-all-start = ((bf16[16,384,128]{2,1,0:T(8,128)(2,1)}), bf16[16,384,128]{2,1,0:T(8,128)(2,1)S(1)}, u32[]{:S(2)}, u32[]{:S(2)}) async-start(bf16[16,384,128]{2,1,0:T(8,128)(2,1)} %prep_kv.1), calls=%async_computation | async-start | bytes 3145728 | tf_op jit(solution)/shard_map/all_to_all | solution.py:576
  11.7 0.1 copy.10
  11.9 0.1 copy.11
  12.1 0.1 copy.12
  12.2 0.9 pad_maximum_fusion
  13.1 0.1 pad_add_fusion.place_ref
  13.2 13.9 %lists.1 = (s32[128]{0:T(128)S(1)}, s32[664]{0:T(1024)S(1)}, s32[600]{0:T(1024)S(1)}, s32[600]{0:T(1024)S(1)}, s32[4]{0:T(128)S(1)}) custom-call(s32[2]{0:T(128)S(1)} %pad_add_fusion.place_ref, s32[128,128]{1,0:T(8,128)S(1)} %copy-done.2), custom_call_target="tpu_custom_call" | custom-call | flops 8000000000 | bytes 100000 | tf_op jit(solution)/shard_map/lists/pallas_call | solution.py:490
  27.1 0.9 broadcast_select_fusion
  28.0 0.9 slice.38
  29.0 0.1 dynamic-slice_bitcast_fusion.3
  29.1 0.1 copy.15
  29.2 1.0 dynamic-slice_bitcast_fusion.4
  30.2 0.1 copy.14
  30.3 0.9 dynamic-slice_bitcast_fusion
  31.3 0.2 maximum_bitcast_fusion
  31.5 0.1 maximum_bitcast_fusion.1.text_ref.text_hbm
  31.6 0.3 prep_q.1
  31.9 0.9 copy-done
  32.9 3.3 %all-to-all-done.kv_ref.kv_hbm = bf16[16,384,128]{2,1,0:T(8,128)(2,1)S(1)} async-done(((bf16[16,384,128]{2,1,0:T(8,128)(2,1)}), bf16[16,384,128]{2,1,0:T(8,128)(2,1)S(1)}, u32[]{:S(2)}, u32[]{:S(2)}) %all-to-all-start) | async-done | bytes 1572896 | tf_op jit(solution)/shard_map/all_to_all | solution.py:576
  36.2 5.0 %all-to-all-start.1 = ((bf16[16,256,128]{2,1,0:T(8,128)(2,1)}), bf16[16,256,128]{2,1,0:T(8,128)(2,1)S(1)}, u32[]{:S(2)}, u32[]{:S(2)}) async-start(bf16[16,256,128]{2,1,0:T(8,128)(2,1)} %copy-done), calls=%async_computation.1 | async-start | bytes 2097152 | tf_op jit(solution)/shard_map/all_to_all | solution.py:609
  41.2 3.5 %collective-permute-start.1 = (bf16[16,384,128]{2,1,0:T(8,128)(2,1)S(1)}, bf16[16,384,128]{2,1,0:T(8,128)(2,1)}, u32[]{:S(2)}, u32[]{:S(2)}) collective-permute-start(bf16[16,384,128]{2,1,0:T(8,128)(2,1)S(1)} %all-to-all-done.kv_ref.kv_hbm), channel_id=1, source_target_pairs={{0,32},{32,64},{64,96},{1,33},{33,65},{65,97},{2,34},{34,66},{66,9... | collective-permute-start | bytes 4718600 | tf_op jit(solution)/shard_map/ppermute | solution.py:607
  44.7 3.5 %collective-permute-start.2 = (bf16[16,384,128]{2,1,0:T(8,128)(2,1)S(1)}, bf16[16,384,128]{2,1,0:T(8,128)(2,1)}, u32[]{:S(2)}, u32[]{:S(2)}) collective-permute-start(bf16[16,384,128]{2,1,0:T(8,128)(2,1)S(1)} %all-to-all-done.kv_ref.kv_hbm), channel_id=1, source_target_pairs={{32,0},{64,32},{96,64},{33,1},{65,33},{97,65},{34,2},{66,34},{98,6... | collective-permute-start | bytes 4718600 | tf_op jit(solution)/shard_map/ppermute | solution.py:608
  48.9 0.1 pad_add_fusion.1.live_ref
  49.0 2.6 %text_keys.1 = bf16[4,144,128]{2,1,0:T(8,128)(2,1)S(1)} custom-call(s32[4]{0:T(128)S(1)} %pad_add_fusion.1.live_ref, bf16[16,384,128]{2,1,0:T(8,128)(2,1)S(1)} %all-to-all-done.kv_ref.kv_hbm, bf16[1,384,128]{2,1,0:T(8,128)(2,1)S(1)} %maximum_bitcast_fusion.1.text_ref.text_hbm, bf16[2,256,128]{2,1,0:T(8,128)(2,1)S(1)} %bitcast.37), custom_call_target="tpu_custom_call" | custom-call | flops 10000000 | bytes 100000 | tf_op jit(solution)/shard_map/text_keys/pallas_call | solution.py:525
  51.6 0.1 collective-permute-start.3
  51.7 1.4 %collective-permute-done.3 = bf16[4,144,128]{2,1,0:T(8,128)(2,1)S(1)} collective-permute-done((bf16[4,144,128]{2,1,0:T(8,128)(2,1)S(1)}, bf16[4,144,128]{2,1,0:T(8,128)(2,1)S(1)}, u32[]{:S(2)}, u32[]{:S(2)}) %collective-permute-start.3) | collective-permute-done | bytes 147488 | tf_op jit(solution)/shard_map/ppermute | solution.py:611
  53.1 5.0 %all-to-all-done.1.q_hbm = bf16[16,256,128]{2,1,0:T(8,128)(2,1)S(1)} async-done(((bf16[16,256,128]{2,1,0:T(8,128)(2,1)}), bf16[16,256,128]{2,1,0:T(8,128)(2,1)S(1)}, u32[]{:S(2)}, u32[]{:S(2)}) %all-to-all-start.1) | async-done | bytes 1048608 | tf_op jit(solution)/shard_map/all_to_all | solution.py:609
  58.1 2.7 %collective-permute-done.4.other_hbm.q_hbm = bf16[16,256,128]{2,1,0:T(8,128)(2,1)S(1)} collective-permute-done((bf16[16,256,128]{2,1,0:T(8,128)(2,1)S(1)}, bf16[16,256,128]{2,1,0:T(8,128)(2,1)S(1)}, u32[]{:S(2)}, u32[]{:S(2)}) %collective-permute-start.4) | collective-permute-done | bytes 1048608 | tf_op jit(solution)/shard_map/ppermute | solution.py:613
  60.7 18.1 %own_keys.1 = (f32[33,2,128,128]{3,2,1,0:T(8,128)S(1)}, f32[33,2,8,128]{3,2,1,0:T(8,128)S(1)}, f32[33,2,8,128]{3,2,1,0:T(8,128)S(1)}) custom-call(s32[128]{0:T(128)S(1)} %get-tuple-element.53.first_ref, s32[664]{0:T(1024)S(1)} %get-tuple-element.54.rest_ref, s32[4]{0:T(128)S(1)} %get-tuple-element.46.n_ref, s32[4]{0:T(128)S(1)} %pad_add_fusion.1.live_ref, ...), custom_call_target="tpu_custom_call" | custom-call | flops 100000000 | bytes 1000000 | tf_op jit(solution)/shard_map/own_keys/pallas_call | solution.py:502
  78.9 0.2 merge_text.1
  79.1 2.6 %collective-permute-done.2.up_hbm = bf16[16,384,128]{2,1,0:T(8,128)(2,1)} collective-permute-done((bf16[16,384,128]{2,1,0:T(8,128)(2,1)S(1)}, bf16[16,384,128]{2,1,0:T(8,128)(2,1)}, u32[]{:S(2)}, u32[]{:S(2)}) %collective-permute-start.2) | collective-permute-done | bytes 1572896 | tf_op jit(solution)/shard_map/ppermute | solution.py:608
  81.7 8.6 %halo_keys.3 = bf16[16,272,128]{2,1,0:T(8,128)(2,1)S(1)} custom-call(s32[600]{0:T(1024)S(1)} %get-tuple-element.65.list_ref, s32[4]{0:T(128)S(1)} %get-tuple-element.46.n_ref, bf16[16,384,128]{2,1,0:T(8,128)(2,1)} %collective-permute-done.1.down_hbm, bf16[16,384,128]{2,1,0:T(8,128)(2,1)} %collective-permute-done.2.up_hbm, ...), custom_call_target="tpu_custom_call" | custom-call | flops 2000000000 | bytes 10000000 | tf_op jit(solution)/shard_map/halo_keys/pallas_call | solution.py:551
  90.3 0.1 collective-permute-start.6
  90.4 3.2 %collective-permute-start.7 = (bf16[6,144,128]{2,1,0:T(8,128)(2,1)S(1)}, bf16[6,144,128]{2,1,0:T(8,128)(2,1)S(1)}, u32[]{:S(2)}, u32[]{:S(2)}) collective-permute-start(bf16[6,144,128]{2,1,0:T(8,128)(2,1)S(1)} %merge_text.1), channel_id=1, source_target_pairs={{0,16},{8,24},{16,0},{24,8},{1,17},{9,25},{17,1},{25,9},{2,18},{10... | collective-permute-start | bytes 663560 | tf_op jit(solution)/shard_map/ppermute | solution.py:622
  93.6 8.1 %halo_keys.2 = (f32[17,2,128,128]{3,2,1,0:T(8,128)S(1)}, f32[17,2,8,128]{3,2,1,0:T(8,128)S(1)}, f32[17,2,8,128]{3,2,1,0:T(8,128)S(1)}) custom-call(s32[600]{0:T(1024)S(1)} %get-tuple-element.45.list_ref, s32[4]{0:T(128)S(1)} %get-tuple-element.46.n_ref, bf16[16,384,128]{2,1,0:T(8,128)(2,1)} %collective-permute-done.1.down_hbm, ...), custom_call_target="tpu_custom_call" | custom-call | flops 2000000000 | bytes 10000000 | tf_op jit(solution)/shard_map/halo_keys/pallas_call | solution.py:551
  101.8 1.8 %merge_cores.1 = bf16[16,272,128]{2,1,0:T(8,128)(2,1)} custom-call(f32[17,2,128,128]{3,2,1,0:T(8,128)S(1)} %get-tuple-element.62.acc_ref, f32[17,2,8,128]{3,2,1,0:T(8,128)S(1)} %get-tuple-element.63.m_ref, f32[17,2,8,128]{3,2,1,0:T(8,128)S(1)} %get-tuple-element.64.l_ref, bf16[16,272,128]{2,1,0:T(8,128)(2,1)S(1)} %collective-permute-done.6.got_ref), custom_call_target="tpu_custom_call" | custom-call | tf_op jit(solution)/shard_map/merge_cores/pallas_call | solution.py:629
  103.7 4.9 %all-to-all-start.2 = ((bf16[16,272,128]{2,1,0:T(8,128)(2,1)}), bf16[16,272,128]{2,1,0:T(8,128)(2,1)S(1)}, u32[]{:S(2)}, u32[]{:S(2)}) async-start(bf16[16,272,128]{2,1,0:T(8,128)(2,1)} %merge_cores.1), calls=%async_computation.2 | async-start | bytes 2228224 | tf_op jit(solution)/shard_map/all_to_all | solution.py:633
  108.6 0.1 collective-permute-start.10
  108.7 2.0 %collective-permute-start.8 = (bf16[6,144,128]{2,1,0:T(8,128)(2,1)S(1)}, bf16[6,144,128]{2,1,0:T(8,128)(2,1)S(1)}, u32[]{:S(2)}, u32[]{:S(2)}) collective-permute-start(bf16[6,144,128]{2,1,0:T(8,128)(2,1)S(1)} %broadcast_select_fusion.1.refs_0_), channel_id=1, source_target_pairs={{0,32},{32,64},{64,96},{96,0},{1,33},{33,65},{65,97},{97,1},{2,34}... | collective-permute-start | bytes 663560 | tf_op jit(solution)/shard_map/ppermute | solution.py:478
  110.7 6.2 %collective-permute-done.10.refs_3_ = bf16[6,144,128]{2,1,0:T(8,128)(2,1)S(1)} collective-permute-done((bf16[6,144,128]{2,1,0:T(8,128)(2,1)S(1)}, bf16[6,144,128]{2,1,0:T(8,128)(2,1)S(1)}, u32[]{:S(2)}, u32[]{:S(2)}) %collective-permute-start.10) | collective-permute-done | bytes 221216 | tf_op jit(solution)/shard_map/ppermute | solution.py:478
  117.0 0.1 collective-permute-done.8.refs_1_
  117.1 3.6 %collective-permute-done.9.refs_2_ = bf16[6,144,128]{2,1,0:T(8,128)(2,1)S(1)} collective-permute-done((bf16[6,144,128]{2,1,0:T(8,128)(2,1)S(1)}, bf16[6,144,128]{2,1,0:T(8,128)(2,1)S(1)}, u32[]{:S(2)}, u32[]{:S(2)}) %collective-permute-start.9) | collective-permute-done | bytes 221216 | tf_op jit(solution)/shard_map/ppermute | solution.py:478
  120.6 1.0 final_text.1
  121.6 5.7 %all-to-all-done.2.got_ref = bf16[16,272,128]{2,1,0:T(8,128)(2,1)S(1)} async-done(((bf16[16,272,128]{2,1,0:T(8,128)(2,1)}), bf16[16,272,128]{2,1,0:T(8,128)(2,1)S(1)}, u32[]{:S(2)}, u32[]{:S(2)}) %all-to-all-start.2) | async-done | bytes 1114144 | tf_op jit(solution)/shard_map/all_to_all | solution.py:633
  127.3 1.2 final.1
  (24 shorter events, 0.2 us)
Async XLA Ops:
  3.7 8.1 %copy-start.3 = (bf16[256,384]{1,0:T(8,128)(2,1)S(1)}, bf16[256,384]{1,0:T(8,128)(2,1)}, u32[]{:S(2)}) copy-start(bf16[256,384]{1,0:T(8,128)(2,1)} %param.11) | copy-start | bytes 589828
  3.7 8.2 %copy-start.4 = (bf16[256,384]{1,0:T(8,128)(2,1)S(1)}, bf16[256,384]{1,0:T(8,128)(2,1)}, u32[]{:S(2)}) copy-start(bf16[256,384]{1,0:T(8,128)(2,1)} %param.12) | copy-start | bytes 589828
  3.7 8.4 %copy-start.5 = (bf16[256,384]{1,0:T(8,128)(2,1)S(1)}, bf16[256,384]{1,0:T(8,128)(2,1)}, u32[]{:S(2)}) copy-start(bf16[256,384]{1,0:T(8,128)(2,1)} %param.13) | copy-start | bytes 589828
  3.7 32.5 %all-to-all-start = ((bf16[16,384,128]{2,1,0:T(8,128)(2,1)}), bf16[16,384,128]{2,1,0:T(8,128)(2,1)S(1)}, u32[]{:S(2)}, u32[]{:S(2)}) async-start(bf16[16,384,128]{2,1,0:T(8,128)(2,1)} %prep_kv.1), calls=%async_computation | async-start | bytes 3145728 | tf_op jit(solution)/shard_map/all_to_all | solution.py:576
  11.7 1.4 %copy-start.2 = (s32[128,128]{1,0:T(8,128)S(1)}, s32[128,128]{1,0:T(8,128)}, u32[]{:S(2)}) copy-start(s32[128,128]{1,0:T(8,128)} %mask_ref) | copy-start | bytes 196612
  13.1 14.0 %collective-permute-start = (bf16[3,256,384]{1,2,0:T(8,128)(2,1)}, bf16[3,256,384]{1,2,0:T(8,128)(2,1)}, u32[]{:S(2)}, u32[]{:S(2)}) collective-permute-start(bf16[3,256,384]{1,2,0:T(8,128)(2,1)} %pad_maximum_fusion), channel_id=1, source_target_pairs={{0,1},{1,0},{2,3},{3,2},{4,5},{5,4},{6,7},{7,6},{8,9},{9,8},{10,11... | collective-permute-start | bytes 1769480 | tf_op jit(solution)/shard_map/ppermute | solution.py:580
  27.1 4.5 %copy-start.1 = (bf16[128,3072]{1,0:T(8,128)(2,1)S(1)}, bf16[128,3072]{1,0:T(8,128)(2,1)}, u32[]{:S(2)}) copy-start(bf16[128,3072]{1,0:T(8,128)(2,1)} %q_ref) | copy-start | bytes 2359300
  31.9 1.0 copy-start
  36.2 21.9 %all-to-all-start.1 = ((bf16[16,256,128]{2,1,0:T(8,128)(2,1)}), bf16[16,256,128]{2,1,0:T(8,128)(2,1)S(1)}, u32[]{:S(2)}, u32[]{:S(2)}) async-start(bf16[16,256,128]{2,1,0:T(8,128)(2,1)} %copy-done), calls=%async_computation.1 | async-start | bytes 2097152 | tf_op jit(solution)/shard_map/all_to_all | solution.py:609
  41.2 37.8 %collective-permute-start.1 = (bf16[16,384,128]{2,1,0:T(8,128)(2,1)S(1)}, bf16[16,384,128]{2,1,0:T(8,128)(2,1)}, u32[]{:S(2)}, u32[]{:S(2)}) collective-permute-start(bf16[16,384,128]{2,1,0:T(8,128)(2,1)S(1)} %all-to-all-done.kv_ref.kv_hbm), channel_id=1, source_target_pairs={{0,32},{32,64},{64,96},{1,33},{33,65},{65,97},{2,34},{34,66},{66,9... | collective-permute-start | bytes 4718600 | tf_op jit(solution)/shard_map/ppermute | solution.py:607
  44.7 37.0 %collective-permute-start.2 = (bf16[16,384,128]{2,1,0:T(8,128)(2,1)S(1)}, bf16[16,384,128]{2,1,0:T(8,128)(2,1)}, u32[]{:S(2)}, u32[]{:S(2)}) collective-permute-start(bf16[16,384,128]{2,1,0:T(8,128)(2,1)S(1)} %all-to-all-done.kv_ref.kv_hbm), channel_id=1, source_target_pairs={{32,0},{64,32},{96,64},{33,1},{65,33},{97,65},{34,2},{66,34},{98,6... | collective-permute-start | bytes 4718600 | tf_op jit(solution)/shard_map/ppermute | solution.py:608
  51.6 1.5 %collective-permute-start.3 = (bf16[4,144,128]{2,1,0:T(8,128)(2,1)S(1)}, bf16[4,144,128]{2,1,0:T(8,128)(2,1)S(1)}, u32[]{:S(2)}, u32[]{:S(2)}) collective-permute-start(bf16[4,144,128]{2,1,0:T(8,128)(2,1)S(1)} %text_keys.1), channel_id=1, source_target_pairs={{0,1},{1,0},{2,3},{3,2},{4,5},{5,4},{6,7},{7,6},{8,9},{9,8},{10,11... | collective-permute-start | bytes 442376 | tf_op jit(solution)/shard_map/ppermute | solution.py:611
  58.1 2.7 %collective-permute-start.4 = (bf16[16,256,128]{2,1,0:T(8,128)(2,1)S(1)}, bf16[16,256,128]{2,1,0:T(8,128)(2,1)S(1)}, u32[]{:S(2)}, u32[]{:S(2)}) collective-permute-start(bf16[16,256,128]{2,1,0:T(8,128)(2,1)S(1)} %all-to-all-done.1.q_hbm), channel_id=1, source_target_pairs={{0,1},{1,0},{2,3},{3,2},{4,5},{5,4},{6,7},{7,6},{8,9},{9,8},{10,11... | collective-permute-start | bytes 3145736 | tf_op jit(solution)/shard_map/ppermute | solution.py:613
  58.1 20.8 %collective-permute-start.5 = (bf16[8,144,128]{2,1,0:T(8,128)(2,1)S(1)}, bf16[8,144,128]{2,1,0:T(8,128)(2,1)S(1)}, u32[]{:S(2)}, u32[]{:S(2)}) collective-permute-start(bf16[8,144,128]{2,1,0:T(8,128)(2,1)S(1)} %pad_maximum_fusion.1.here_ref), channel_id=1, source_target_pairs={{0,8},{8,0},{16,24},{24,16},{1,9},{9,1},{17,25},{25,17},{2,10},{10... | collective-permute-start | bytes 884744 | tf_op jit(solution)/shard_map/ppermute | solution.py:614
  90.3 11.5 %collective-permute-start.6 = (bf16[16,272,128]{2,1,0:T(8,128)(2,1)S(1)}, bf16[16,272,128]{2,1,0:T(8,128)(2,1)S(1)}, u32[]{:S(2)}, u32[]{:S(2)}) collective-permute-start(bf16[16,272,128]{2,1,0:T(8,128)(2,1)S(1)} %halo_keys.3), channel_id=1, source_target_pairs={{0,1},{1,0},{2,3},{3,2},{4,5},{5,4},{6,7},{7,6},{8,9},{9,8},{10,11... | collective-permute-start | bytes 3342344 | tf_op jit(solution)/shard_map/ppermute | solution.py:626
  90.4 11.4 %collective-permute-start.7 = (bf16[6,144,128]{2,1,0:T(8,128)(2,1)S(1)}, bf16[6,144,128]{2,1,0:T(8,128)(2,1)S(1)}, u32[]{:S(2)}, u32[]{:S(2)}) collective-permute-start(bf16[6,144,128]{2,1,0:T(8,128)(2,1)S(1)} %merge_text.1), channel_id=1, source_target_pairs={{0,16},{8,24},{16,0},{24,8},{1,17},{9,25},{17,1},{25,9},{2,18},{10... | collective-permute-start | bytes 663560 | tf_op jit(solution)/shard_map/ppermute | solution.py:622
  103.7 23.7 %all-to-all-start.2 = ((bf16[16,272,128]{2,1,0:T(8,128)(2,1)}), bf16[16,272,128]{2,1,0:T(8,128)(2,1)S(1)}, u32[]{:S(2)}, u32[]{:S(2)}) async-start(bf16[16,272,128]{2,1,0:T(8,128)(2,1)} %merge_cores.1), calls=%async_computation.2 | async-start | bytes 2228224 | tf_op jit(solution)/shard_map/all_to_all | solution.py:633
  108.6 8.3 %collective-permute-start.10 = (bf16[6,144,128]{2,1,0:T(8,128)(2,1)S(1)}, bf16[6,144,128]{2,1,0:T(8,128)(2,1)S(1)}, u32[]{:S(2)}, u32[]{:S(2)}) collective-permute-start(bf16[6,144,128]{2,1,0:T(8,128)(2,1)S(1)} %broadcast_select_fusion.1.refs_0_), channel_id=1, source_target_pairs={{0,96},{32,0},{64,32},{96,64},{1,97},{33,1},{65,33},{97,65},{2,98}... | collective-permute-start | bytes 663560 | tf_op jit(solution)/shard_map/ppermute | solution.py:478
  108.7 8.4 %collective-permute-start.8 = (bf16[6,144,128]{2,1,0:T(8,128)(2,1)S(1)}, bf16[6,144,128]{2,1,0:T(8,128)(2,1)S(1)}, u32[]{:S(2)}, u32[]{:S(2)}) collective-permute-start(bf16[6,144,128]{2,1,0:T(8,128)(2,1)S(1)} %broadcast_select_fusion.1.refs_0_), channel_id=1, source_target_pairs={{0,32},{32,64},{64,96},{96,0},{1,33},{33,65},{65,97},{97,1},{2,34}... | collective-permute-start | bytes 663560 | tf_op jit(solution)/shard_map/ppermute | solution.py:478
  110.7 9.9 %collective-permute-start.9 = (bf16[6,144,128]{2,1,0:T(8,128)(2,1)S(1)}, bf16[6,144,128]{2,1,0:T(8,128)(2,1)S(1)}, u32[]{:S(2)}, u32[]{:S(2)}) collective-permute-start(bf16[6,144,128]{2,1,0:T(8,128)(2,1)S(1)} %broadcast_select_fusion.1.refs_0_), channel_id=1, source_target_pairs={{0,64},{32,96},{64,0},{96,32},{1,65},{33,97},{65,1},{97,33},{2,66}... | collective-permute-start | bytes 663560 | tf_op jit(solution)/shard_map/ppermute | solution.py:478

commit v3 on v2

--- a/solution.py
+++ b/solution.py
@@ -18,7 +18,7 @@
 QREC = 256
 OREC = 272
 STEP = 4
-UNROLL = 4
+UNROLL = 8
 LOG2 = float(DH**-0.5 * np.log2(np.e))
 neg_fill = -1e30
 FLAG = 4096
@@ -235,14 +235,14 @@
         work.acc[q, h] = out if first else work.acc[q, h] * work.factor[buf, h, 0:1] + out
 
 
-def pipelined(score, soft, add, rounds):
+def pipelined(score, soft, add, rounds, unroll=UNROLL):
     score(0, 0)
     score(1, 1)
     soft(0, 0)
 
     def body(i, carry):
-        for k in range(UNROLL):
-            t = UNROLL * i + k
+        for k in range(unroll):
+            t = unroll * i + k
             score(t + 2, k % 2)
             add(t, k % 2)
             soft(t + 1, (k + 1) % 2)
@@ -300,7 +300,7 @@
     def add(n, buf):
         gather(work, buf, n, line(n)[0], True)
 
-    pipelined(score, soft, add, SLAB // UNROLL)
+    pipelined(score, soft, add, SLAB // 16, 16)
     run_list(work, rest_ref, n_ref[0])
 
 

time: 129 us -> 129 us (level); the launches traced: 128 us -> 127 us
  Pallas kernels: 58.8 us -> 54.9 us
  starting transfers between devices: 30.5 us -> 32.4 us
    pallas_call x1, Pallas kernels: 18.1 us -> 15.5 us  [run_own(): pl.pallas_call(own_kernel, out_shape=state(SLAB + 1), in_specs=[SM] * 4 +...]
    ppermute x1, waiting for transfers between devices: 0.01 us -> 1.98 us  [local(): from_down = lax.ppermute(kv, 'y', [(0, 1), (1, 2), (2, 3)])]
    ppermute x3, starting transfers between devices: 2.09 us -> 3.8 us  [ring(): return [x] + [lax.ppermute(x, axis, route) for route in routes]]
    ppermute x3, waiting for transfers between devices: 9.92 us -> 8.37 us  [ring(): return [x] + [lax.ppermute(x, axis, route) for route in routes]]
    pallas_call x2, Pallas kernels: 16.7 us -> 15.4 us  [run_halo(): pl.pallas_call(functools.partial(halo_kernel, which), out_shape=out, in_s...]
  transfers between devices with their start and end apart: 14 -> 14, of which waited for: 9 -> 10; matrix products, arithmetic and copies ran while one was open for 5% -> 5% of each run, Pallas kernels for 34% -> 33%
where the time goes in v3:
time: 129 us; the launch traced here: 127 us
  Pallas kernels  54.9 us (43%)
  starting transfers between devices  32.4 us (25%)
  waiting for transfers between devices  31 us (24%)
  local copies, waits for them, and re-layouts  4.65 us (4%)
  other arithmetic  2.27 us (2%)
  between operations  1.65 us (1%)
    pallas_call x1, Pallas kernels, run_own(): pl.pallas_call(own_kernel, out_shape=state(SLAB + 1), in_specs=[SM] * 4 +...  15.5 us
    pallas_call x2, Pallas kernels, run_halo(): pl.pallas_call(functools.partial(halo_kernel, which), out_shape=out, in_s...  15.4 us
    pallas_call x1, Pallas kernels, run_lists(): pl.pallas_call(lists_kernel, out_shape=[shape((n,), jnp.int32) for n in (...  13.9 us
    ppermute x3, waiting for transfers between devices, ring(): return [x] + [lax.ppermute(x, axis, route) for route in routes]  8.37 us
    all_to_all x1, starting transfers between devices, local(): kv = lax.all_to_all(kv_send, chips, 0, 0, tiled=True)  8.02 us
    all_to_all x1, waiting for transfers between devices, local(): back = lax.all_to_all(record, chips, 0, 0, tiled=True)  5.06 us
    all_to_all x1, starting transfers between devices, local(): q = lax.all_to_all(q_send, chips, 0, 0, tiled=True)  5.03 us
    all_to_all x1, waiting for transfers between devices, local(): q = lax.all_to_all(q_send, chips, 0, 0, tiled=True)  5.02 us
  transfers between devices with their start and end apart: 14, of which 10 were waited for; matrix products, arithmetic and copies ran while one was open for 5% of the time, Pallas kernels for 33%

profile of v3, /device:TPU:8, one launch (start us, length us, event | category | flops | bytes accessed | tf_op | source)
XLA Modules:
  0.0 126.8 jit_solution(4404674483516063924)
XLA Ops:
  0.6 3.0 %prep_kv.1 = bf16[16,384,128]{2,1,0:T(8,128)(2,1)} custom-call(bf16[128,3072]{1,0:T(8,128)(2,1)} %k_hbm.1, bf16[128,3072]{1,0:T(8,128)(2,1)} %v_hbm.1), custom_call_target="tpu_custom_call" | custom-call | tf_op jit(solution)/shard_map/prep_kv/pallas_call | solution.py:571
  3.7 8.0 %all-to-all-start = ((bf16[16,384,128]{2,1,0:T(8,128)(2,1)}), bf16[16,384,128]{2,1,0:T(8,128)(2,1)S(1)}, u32[]{:S(2)}, u32[]{:S(2)}) async-start(bf16[16,384,128]{2,1,0:T(8,128)(2,1)} %prep_kv.1), calls=%async_computation | async-start | bytes 3145728 | tf_op jit(solution)/shard_map/all_to_all | solution.py:576
  11.7 0.1 copy.10
  11.9 0.1 copy.11
  12.1 0.1 copy.12
  12.2 0.9 pad_maximum_fusion
  13.1 0.1 pad_add_fusion.place_ref
  13.2 13.9 %lists.1 = (s32[128]{0:T(128)S(1)}, s32[680]{0:T(1024)S(1)}, s32[616]{0:T(1024)S(1)}, s32[616]{0:T(1024)S(1)}, s32[4]{0:T(128)S(1)}) custom-call(s32[2]{0:T(128)S(1)} %pad_add_fusion.place_ref, s32[128,128]{1,0:T(8,128)S(1)} %copy-done.2), custom_call_target="tpu_custom_call" | custom-call | flops 8000000000 | bytes 100000 | tf_op jit(solution)/shard_map/lists/pallas_call | solution.py:490
  27.1 0.9 broadcast_select_fusion
  28.0 0.9 slice.38
  29.0 0.1 dynamic-slice_bitcast_fusion.3
  29.1 0.1 copy.15
  29.2 1.0 dynamic-slice_bitcast_fusion.4
  30.2 0.1 copy.14
  30.3 0.9 dynamic-slice_bitcast_fusion
  31.3 0.2 maximum_bitcast_fusion
  31.5 0.1 maximum_bitcast_fusion.1.text_ref.text_hbm
  31.6 0.3 prep_q.1
  31.9 0.9 copy-done
  32.9 3.3 %all-to-all-done.kv_ref.kv_hbm = bf16[16,384,128]{2,1,0:T(8,128)(2,1)S(1)} async-done(((bf16[16,384,128]{2,1,0:T(8,128)(2,1)}), bf16[16,384,128]{2,1,0:T(8,128)(2,1)S(1)}, u32[]{:S(2)}, u32[]{:S(2)}) %all-to-all-start) | async-done | bytes 1572896 | tf_op jit(solution)/shard_map/all_to_all | solution.py:576
  36.2 5.0 %all-to-all-start.1 = ((bf16[16,256,128]{2,1,0:T(8,128)(2,1)}), bf16[16,256,128]{2,1,0:T(8,128)(2,1)S(1)}, u32[]{:S(2)}, u32[]{:S(2)}) async-start(bf16[16,256,128]{2,1,0:T(8,128)(2,1)} %copy-done), calls=%async_computation.1 | async-start | bytes 2097152 | tf_op jit(solution)/shard_map/all_to_all | solution.py:609
  41.2 3.5 %collective-permute-start.1 = (bf16[16,384,128]{2,1,0:T(8,128)(2,1)S(1)}, bf16[16,384,128]{2,1,0:T(8,128)(2,1)}, u32[]{:S(2)}, u32[]{:S(2)}) collective-permute-start(bf16[16,384,128]{2,1,0:T(8,128)(2,1)S(1)} %all-to-all-done.kv_ref.kv_hbm), channel_id=1, source_target_pairs={{0,32},{32,64},{64,96},{1,33},{33,65},{65,97},{2,34},{34,66},{66,9... | collective-permute-start | bytes 4718600 | tf_op jit(solution)/shard_map/ppermute | solution.py:607
  44.7 3.5 %collective-permute-start.2 = (bf16[16,384,128]{2,1,0:T(8,128)(2,1)S(1)}, bf16[16,384,128]{2,1,0:T(8,128)(2,1)}, u32[]{:S(2)}, u32[]{:S(2)}) collective-permute-start(bf16[16,384,128]{2,1,0:T(8,128)(2,1)S(1)} %all-to-all-done.kv_ref.kv_hbm), channel_id=1, source_target_pairs={{32,0},{64,32},{96,64},{33,1},{65,33},{97,65},{34,2},{66,34},{98,6... | collective-permute-start | bytes 4718600 | tf_op jit(solution)/shard_map/ppermute | solution.py:608
  48.9 0.1 pad_add_fusion.1.live_ref
  49.0 2.6 %text_keys.1 = bf16[4,144,128]{2,1,0:T(8,128)(2,1)S(1)} custom-call(s32[4]{0:T(128)S(1)} %pad_add_fusion.1.live_ref, bf16[16,384,128]{2,1,0:T(8,128)(2,1)S(1)} %all-to-all-done.kv_ref.kv_hbm, bf16[1,384,128]{2,1,0:T(8,128)(2,1)S(1)} %maximum_bitcast_fusion.1.text_ref.text_hbm, bf16[2,256,128]{2,1,0:T(8,128)(2,1)S(1)} %bitcast.37), custom_call_target="tpu_custom_call" | custom-call | flops 10000000 | bytes 100000 | tf_op jit(solution)/shard_map/text_keys/pallas_call | solution.py:525
  51.6 0.1 collective-permute-start.3
  51.7 1.4 %collective-permute-done.3 = bf16[4,144,128]{2,1,0:T(8,128)(2,1)S(1)} collective-permute-done((bf16[4,144,128]{2,1,0:T(8,128)(2,1)S(1)}, bf16[4,144,128]{2,1,0:T(8,128)(2,1)S(1)}, u32[]{:S(2)}, u32[]{:S(2)}) %collective-permute-start.3) | collective-permute-done | bytes 147488 | tf_op jit(solution)/shard_map/ppermute | solution.py:611
  53.1 5.0 %all-to-all-done.1.q_hbm = bf16[16,256,128]{2,1,0:T(8,128)(2,1)S(1)} async-done(((bf16[16,256,128]{2,1,0:T(8,128)(2,1)}), bf16[16,256,128]{2,1,0:T(8,128)(2,1)S(1)}, u32[]{:S(2)}, u32[]{:S(2)}) %all-to-all-start.1) | async-done | bytes 1048608 | tf_op jit(solution)/shard_map/all_to_all | solution.py:609
  58.1 2.7 %collective-permute-done.4.other_hbm.q_hbm = bf16[16,256,128]{2,1,0:T(8,128)(2,1)S(1)} collective-permute-done((bf16[16,256,128]{2,1,0:T(8,128)(2,1)S(1)}, bf16[16,256,128]{2,1,0:T(8,128)(2,1)S(1)}, u32[]{:S(2)}, u32[]{:S(2)}) %collective-permute-start.4) | collective-permute-done | bytes 1048608 | tf_op jit(solution)/shard_map/ppermute | solution.py:613
  60.7 15.5 %own_keys.1 = (f32[33,2,128,128]{3,2,1,0:T(8,128)S(1)}, f32[33,2,8,128]{3,2,1,0:T(8,128)S(1)}, f32[33,2,8,128]{3,2,1,0:T(8,128)S(1)}) custom-call(s32[128]{0:T(128)S(1)} %get-tuple-element.53.first_ref, s32[680]{0:T(1024)S(1)} %get-tuple-element.54.rest_ref, s32[4]{0:T(128)S(1)} %get-tuple-element.46.n_ref, s32[4]{0:T(128)S(1)} %pad_add_fusion.1.live_ref, ...), custom_call_target="tpu_custom_call" | custom-call | flops 100000000 | bytes 1000000 | tf_op jit(solution)/shard_map/own_keys/pallas_call | solution.py:502
  76.3 0.2 merge_text.1
  76.5 2.0 %collective-permute-done.1.down_hbm = bf16[16,384,128]{2,1,0:T(8,128)(2,1)} collective-permute-done((bf16[16,384,128]{2,1,0:T(8,128)(2,1)S(1)}, bf16[16,384,128]{2,1,0:T(8,128)(2,1)}, u32[]{:S(2)}, u32[]{:S(2)}) %collective-permute-start.1) | collective-permute-done | bytes 1572896 | tf_op jit(solution)/shard_map/ppermute | solution.py:607
  78.5 3.2 %collective-permute-done.2.up_hbm = bf16[16,384,128]{2,1,0:T(8,128)(2,1)} collective-permute-done((bf16[16,384,128]{2,1,0:T(8,128)(2,1)S(1)}, bf16[16,384,128]{2,1,0:T(8,128)(2,1)}, u32[]{:S(2)}, u32[]{:S(2)}) %collective-permute-start.2) | collective-permute-done | bytes 1572896 | tf_op jit(solution)/shard_map/ppermute | solution.py:608
  81.7 7.3 %halo_keys.3 = bf16[16,272,128]{2,1,0:T(8,128)(2,1)S(1)} custom-call(s32[616]{0:T(1024)S(1)} %get-tuple-element.65.list_ref, s32[4]{0:T(128)S(1)} %get-tuple-element.46.n_ref, bf16[16,384,128]{2,1,0:T(8,128)(2,1)} %collective-permute-done.1.down_hbm, bf16[16,384,128]{2,1,0:T(8,128)(2,1)} %collective-permute-done.2.up_hbm, ...), custom_call_target="tpu_custom_call" | custom-call | flops 2000000000 | bytes 10000000 | tf_op jit(solution)/shard_map/halo_keys/pallas_call | solution.py:551
  89.0 0.3 collective-permute-start.6
  89.3 3.2 %collective-permute-start.7 = (bf16[6,144,128]{2,1,0:T(8,128)(2,1)S(1)}, bf16[6,144,128]{2,1,0:T(8,128)(2,1)S(1)}, u32[]{:S(2)}, u32[]{:S(2)}) collective-permute-start(bf16[6,144,128]{2,1,0:T(8,128)(2,1)S(1)} %merge_text.1), channel_id=1, source_target_pairs={{0,16},{8,24},{16,0},{24,8},{1,17},{9,25},{17,1},{25,9},{2,18},{10... | collective-permute-start | bytes 663560 | tf_op jit(solution)/shard_map/ppermute | solution.py:622
  92.5 8.1 %halo_keys.2 = (f32[17,2,128,128]{3,2,1,0:T(8,128)S(1)}, f32[17,2,8,128]{3,2,1,0:T(8,128)S(1)}, f32[17,2,8,128]{3,2,1,0:T(8,128)S(1)}) custom-call(s32[616]{0:T(1024)S(1)} %get-tuple-element.45.list_ref, s32[4]{0:T(128)S(1)} %get-tuple-element.46.n_ref, bf16[16,384,128]{2,1,0:T(8,128)(2,1)} %collective-permute-done.1.down_hbm, ...), custom_call_target="tpu_custom_call" | custom-call | flops 2000000000 | bytes 10000000 | tf_op jit(solution)/shard_map/halo_keys/pallas_call | solution.py:551
  100.7 1.8 %merge_cores.1 = bf16[16,272,128]{2,1,0:T(8,128)(2,1)} custom-call(f32[17,2,128,128]{3,2,1,0:T(8,128)S(1)} %get-tuple-element.62.acc_ref, f32[17,2,8,128]{3,2,1,0:T(8,128)S(1)} %get-tuple-element.63.m_ref, f32[17,2,8,128]{3,2,1,0:T(8,128)S(1)} %get-tuple-element.64.l_ref, bf16[16,272,128]{2,1,0:T(8,128)(2,1)S(1)} %collective-permute-done.6.got_ref), custom_call_target="tpu_custom_call" | custom-call | tf_op jit(solution)/shard_map/merge_cores/pallas_call | solution.py:629
  102.5 4.9 %all-to-all-start.2 = ((bf16[16,272,128]{2,1,0:T(8,128)(2,1)}), bf16[16,272,128]{2,1,0:T(8,128)(2,1)S(1)}, u32[]{:S(2)}, u32[]{:S(2)}) async-start(bf16[16,272,128]{2,1,0:T(8,128)(2,1)} %merge_cores.1), calls=%async_computation.2 | async-start | bytes 2228224 | tf_op jit(solution)/shard_map/all_to_all | solution.py:633
  107.5 1.6 %collective-permute-start.10 = (bf16[6,144,128]{2,1,0:T(8,128)(2,1)S(1)}, bf16[6,144,128]{2,1,0:T(8,128)(2,1)S(1)}, u32[]{:S(2)}, u32[]{:S(2)}) collective-permute-start(bf16[6,144,128]{2,1,0:T(8,128)(2,1)S(1)} %broadcast_select_fusion.1.refs_0_), channel_id=1, source_target_pairs={{0,96},{32,0},{64,32},{96,64},{1,97},{33,1},{65,33},{97,65},{2,98}... | collective-permute-start | bytes 663560 | tf_op jit(solution)/shard_map/ppermute | solution.py:478
  109.1 0.4 collective-permute-start.8
  109.6 1.7 %collective-permute-start.9 = (bf16[6,144,128]{2,1,0:T(8,128)(2,1)S(1)}, bf16[6,144,128]{2,1,0:T(8,128)(2,1)S(1)}, u32[]{:S(2)}, u32[]{:S(2)}) collective-permute-start(bf16[6,144,128]{2,1,0:T(8,128)(2,1)S(1)} %broadcast_select_fusion.1.refs_0_), channel_id=1, source_target_pairs={{0,64},{32,96},{64,0},{96,32},{1,65},{33,97},{65,1},{97,33},{2,66}... | collective-permute-start | bytes 663560 | tf_op jit(solution)/shard_map/ppermute | solution.py:478
  111.3 3.9 %collective-permute-done.10.refs_3_ = bf16[6,144,128]{2,1,0:T(8,128)(2,1)S(1)} collective-permute-done((bf16[6,144,128]{2,1,0:T(8,128)(2,1)S(1)}, bf16[6,144,128]{2,1,0:T(8,128)(2,1)S(1)}, u32[]{:S(2)}, u32[]{:S(2)}) %collective-permute-start.10) | collective-permute-done | bytes 221216 | tf_op jit(solution)/shard_map/ppermute | solution.py:478
  115.2 2.3 %collective-permute-done.8.refs_1_ = bf16[6,144,128]{2,1,0:T(8,128)(2,1)S(1)} collective-permute-done((bf16[6,144,128]{2,1,0:T(8,128)(2,1)S(1)}, bf16[6,144,128]{2,1,0:T(8,128)(2,1)S(1)}, u32[]{:S(2)}, u32[]{:S(2)}) %collective-permute-start.8) | collective-permute-done | bytes 221216 | tf_op jit(solution)/shard_map/ppermute | solution.py:478
  117.5 2.2 %collective-permute-done.9.refs_2_ = bf16[6,144,128]{2,1,0:T(8,128)(2,1)S(1)} collective-permute-done((bf16[6,144,128]{2,1,0:T(8,128)(2,1)S(1)}, bf16[6,144,128]{2,1,0:T(8,128)(2,1)S(1)}, u32[]{:S(2)}, u32[]{:S(2)}) %collective-permute-start.9) | collective-permute-done | bytes 221216 | tf_op jit(solution)/shard_map/ppermute | solution.py:478
  119.7 1.0 final_text.1
  120.6 5.1 %all-to-all-done.2.got_ref = bf16[16,272,128]{2,1,0:T(8,128)(2,1)S(1)} async-done(((bf16[16,272,128]{2,1,0:T(8,128)(2,1)}), bf16[16,272,128]{2,1,0:T(8,128)(2,1)S(1)}, u32[]{:S(2)}, u32[]{:S(2)}) %all-to-all-start.2) | async-done | bytes 1114144 | tf_op jit(solution)/shard_map/all_to_all | solution.py:633
  125.7 1.2 final.1
  (24 shorter events, 0.2 us)
Async XLA Ops:
  3.7 8.1 %copy-start.3 = (bf16[256,384]{1,0:T(8,128)(2,1)S(1)}, bf16[256,384]{1,0:T(8,128)(2,1)}, u32[]{:S(2)}) copy-start(bf16[256,384]{1,0:T(8,128)(2,1)} %param.11) | copy-start | bytes 589828
  3.7 8.2 %copy-start.4 = (bf16[256,384]{1,0:T(8,128)(2,1)S(1)}, bf16[256,384]{1,0:T(8,128)(2,1)}, u32[]{:S(2)}) copy-start(bf16[256,384]{1,0:T(8,128)(2,1)} %param.12) | copy-start | bytes 589828
  3.7 8.4 %copy-start.5 = (bf16[256,384]{1,0:T(8,128)(2,1)S(1)}, bf16[256,384]{1,0:T(8,128)(2,1)}, u32[]{:S(2)}) copy-start(bf16[256,384]{1,0:T(8,128)(2,1)} %param.13) | copy-start | bytes 589828
  3.7 32.5 %all-to-all-start = ((bf16[16,384,128]{2,1,0:T(8,128)(2,1)}), bf16[16,384,128]{2,1,0:T(8,128)(2,1)S(1)}, u32[]{:S(2)}, u32[]{:S(2)}) async-start(bf16[16,384,128]{2,1,0:T(8,128)(2,1)} %prep_kv.1), calls=%async_computation | async-start | bytes 3145728 | tf_op jit(solution)/shard_map/all_to_all | solution.py:576
  11.7 1.4 %copy-start.2 = (s32[128,128]{1,0:T(8,128)S(1)}, s32[128,128]{1,0:T(8,128)}, u32[]{:S(2)}) copy-start(s32[128,128]{1,0:T(8,128)} %mask_ref) | copy-start | bytes 196612
  13.1 14.0 %collective-permute-start = (bf16[3,256,384]{1,2,0:T(8,128)(2,1)}, bf16[3,256,384]{1,2,0:T(8,128)(2,1)}, u32[]{:S(2)}, u32[]{:S(2)}) collective-permute-start(bf16[3,256,384]{1,2,0:T(8,128)(2,1)} %pad_maximum_fusion), channel_id=1, source_target_pairs={{0,1},{1,0},{2,3},{3,2},{4,5},{5,4},{6,7},{7,6},{8,9},{9,8},{10,11... | collective-permute-start | bytes 1769480 | tf_op jit(solution)/shard_map/ppermute | solution.py:580
  27.1 4.5 %copy-start.1 = (bf16[128,3072]{1,0:T(8,128)(2,1)S(1)}, bf16[128,3072]{1,0:T(8,128)(2,1)}, u32[]{:S(2)}) copy-start(bf16[128,3072]{1,0:T(8,128)(2,1)} %q_ref) | copy-start | bytes 2359300
  31.9 1.0 copy-start
  36.2 21.9 %all-to-all-start.1 = ((bf16[16,256,128]{2,1,0:T(8,128)(2,1)}), bf16[16,256,128]{2,1,0:T(8,128)(2,1)S(1)}, u32[]{:S(2)}, u32[]{:S(2)}) async-start(bf16[16,256,128]{2,1,0:T(8,128)(2,1)} %copy-done), calls=%async_computation.1 | async-start | bytes 2097152 | tf_op jit(solution)/shard_map/all_to_all | solution.py:609
  41.2 37.3 %collective-permute-start.1 = (bf16[16,384,128]{2,1,0:T(8,128)(2,1)S(1)}, bf16[16,384,128]{2,1,0:T(8,128)(2,1)}, u32[]{:S(2)}, u32[]{:S(2)}) collective-permute-start(bf16[16,384,128]{2,1,0:T(8,128)(2,1)S(1)} %all-to-all-done.kv_ref.kv_hbm), channel_id=1, source_target_pairs={{0,32},{32,64},{64,96},{1,33},{33,65},{65,97},{2,34},{34,66},{66,9... | collective-permute-start | bytes 4718600 | tf_op jit(solution)/shard_map/ppermute | solution.py:607
  44.7 37.0 %collective-permute-start.2 = (bf16[16,384,128]{2,1,0:T(8,128)(2,1)S(1)}, bf16[16,384,128]{2,1,0:T(8,128)(2,1)}, u32[]{:S(2)}, u32[]{:S(2)}) collective-permute-start(bf16[16,384,128]{2,1,0:T(8,128)(2,1)S(1)} %all-to-all-done.kv_ref.kv_hbm), channel_id=1, source_target_pairs={{32,0},{64,32},{96,64},{33,1},{65,33},{97,65},{34,2},{66,34},{98,6... | collective-permute-start | bytes 4718600 | tf_op jit(solution)/shard_map/ppermute | solution.py:608
  51.6 1.5 %collective-permute-start.3 = (bf16[4,144,128]{2,1,0:T(8,128)(2,1)S(1)}, bf16[4,144,128]{2,1,0:T(8,128)(2,1)S(1)}, u32[]{:S(2)}, u32[]{:S(2)}) collective-permute-start(bf16[4,144,128]{2,1,0:T(8,128)(2,1)S(1)} %text_keys.1), channel_id=1, source_target_pairs={{0,1},{1,0},{2,3},{3,2},{4,5},{5,4},{6,7},{7,6},{8,9},{9,8},{10,11... | collective-permute-start | bytes 442376 | tf_op jit(solution)/shard_map/ppermute | solution.py:611
  58.1 2.7 %collective-permute-start.4 = (bf16[16,256,128]{2,1,0:T(8,128)(2,1)S(1)}, bf16[16,256,128]{2,1,0:T(8,128)(2,1)S(1)}, u32[]{:S(2)}, u32[]{:S(2)}) collective-permute-start(bf16[16,256,128]{2,1,0:T(8,128)(2,1)S(1)} %all-to-all-done.1.q_hbm), channel_id=1, source_target_pairs={{0,1},{1,0},{2,3},{3,2},{4,5},{5,4},{6,7},{7,6},{8,9},{9,8},{10,11... | collective-permute-start | bytes 3145736 | tf_op jit(solution)/shard_map/ppermute | solution.py:613
  58.1 18.2 %collective-permute-start.5 = (bf16[8,144,128]{2,1,0:T(8,128)(2,1)S(1)}, bf16[8,144,128]{2,1,0:T(8,128)(2,1)S(1)}, u32[]{:S(2)}, u32[]{:S(2)}) collective-permute-start(bf16[8,144,128]{2,1,0:T(8,128)(2,1)S(1)} %pad_maximum_fusion.1.here_ref), channel_id=1, source_target_pairs={{0,8},{8,0},{16,24},{24,16},{1,9},{9,1},{17,25},{25,17},{2,10},{10... | collective-permute-start | bytes 884744 | tf_op jit(solution)/shard_map/ppermute | solution.py:614
  89.0 11.7 %collective-permute-start.6 = (bf16[16,272,128]{2,1,0:T(8,128)(2,1)S(1)}, bf16[16,272,128]{2,1,0:T(8,128)(2,1)S(1)}, u32[]{:S(2)}, u32[]{:S(2)}) collective-permute-start(bf16[16,272,128]{2,1,0:T(8,128)(2,1)S(1)} %halo_keys.3), channel_id=1, source_target_pairs={{0,1},{1,0},{2,3},{3,2},{4,5},{5,4},{6,7},{7,6},{8,9},{9,8},{10,11... | collective-permute-start | bytes 3342344 | tf_op jit(solution)/shard_map/ppermute | solution.py:626
  89.3 11.4 %collective-permute-start.7 = (bf16[6,144,128]{2,1,0:T(8,128)(2,1)S(1)}, bf16[6,144,128]{2,1,0:T(8,128)(2,1)S(1)}, u32[]{:S(2)}, u32[]{:S(2)}) collective-permute-start(bf16[6,144,128]{2,1,0:T(8,128)(2,1)S(1)} %merge_text.1), channel_id=1, source_target_pairs={{0,16},{8,24},{16,0},{24,8},{1,17},{9,25},{17,1},{25,9},{2,18},{10... | collective-permute-start | bytes 663560 | tf_op jit(solution)/shard_map/ppermute | solution.py:622
  102.5 23.1 %all-to-all-start.2 = ((bf16[16,272,128]{2,1,0:T(8,128)(2,1)}), bf16[16,272,128]{2,1,0:T(8,128)(2,1)S(1)}, u32[]{:S(2)}, u32[]{:S(2)}) async-start(bf16[16,272,128]{2,1,0:T(8,128)(2,1)} %merge_cores.1), calls=%async_computation.2 | async-start | bytes 2228224 | tf_op jit(solution)/shard_map/all_to_all | solution.py:633
  107.5 7.7 %collective-permute-start.10 = (bf16[6,144,128]{2,1,0:T(8,128)(2,1)S(1)}, bf16[6,144,128]{2,1,0:T(8,128)(2,1)S(1)}, u32[]{:S(2)}, u32[]{:S(2)}) collective-permute-start(bf16[6,144,128]{2,1,0:T(8,128)(2,1)S(1)} %broadcast_select_fusion.1.refs_0_), channel_id=1, source_target_pairs={{0,96},{32,0},{64,32},{96,64},{1,97},{33,1},{65,33},{97,65},{2,98}... | collective-permute-start | bytes 663560 | tf_op jit(solution)/shard_map/ppermute | solution.py:478
  109.1 8.4 %collective-permute-start.8 = (bf16[6,144,128]{2,1,0:T(8,128)(2,1)S(1)}, bf16[6,144,128]{2,1,0:T(8,128)(2,1)S(1)}, u32[]{:S(2)}, u32[]{:S(2)}) collective-permute-start(bf16[6,144,128]{2,1,0:T(8,128)(2,1)S(1)} %broadcast_select_fusion.1.refs_0_), channel_id=1, source_target_pairs={{0,32},{32,64},{64,96},{96,0},{1,33},{33,65},{65,97},{97,1},{2,34}... | collective-permute-start | bytes 663560 | tf_op jit(solution)/shard_map/ppermute | solution.py:478
  109.6 10.1 %collective-permute-start.9 = (bf16[6,144,128]{2,1,0:T(8,128)(2,1)S(1)}, bf16[6,144,128]{2,1,0:T(8,128)(2,1)S(1)}, u32[]{:S(2)}, u32[]{:S(2)}) collective-permute-start(bf16[6,144,128]{2,1,0:T(8,128)(2,1)S(1)} %broadcast_select_fusion.1.refs_0_), channel_id=1, source_target_pairs={{0,64},{32,96},{64,0},{96,32},{1,65},{33,97},{65,1},{97,33},{2,66}... | collective-permute-start | bytes 663560 | tf_op jit(solution)/shard_map/ppermute | solution.py:478

commit v4 on v3

--- a/solution.py
+++ b/solution.py
@@ -433,7 +433,7 @@
             out_ref[n, 256:272] = stat_rows(rows)
             return carry
 
-        lax.fori_loop(0, HALF, finish, 0)
+        lax.fori_loop(0, HALF, finish, 0, unroll=8)
 
 
 def merge_kernel(acc_ref, m_ref, l_ref, got_ref, out_ref):
@@ -453,7 +453,7 @@
                 out_ref[n, 256:272] = stat_rows([top, total])
         return carry
 
-    lax.fori_loop(0, HALF, one, 0)
+    lax.fori_loop(0, HALF, one, 0, unroll=8)
 
 
 def final_kernel(got_ref, out_ref):

time: 129 us -> 129 us (level)
    ppermute x3, waiting for transfers between devices: 8.37 us -> 9.96 us  [ring(): return [x] + [lax.ppermute(x, axis, route) for route in routes]]
  transfers between devices with their start and end apart: 14 -> 14, of which waited for: 10 -> 10; matrix products, arithmetic and copies ran while one was open for 5% -> 5% of each run, Pallas kernels for 33% -> 32%
where the time goes in v4:
time: 129 us; the launch traced here: 128 us
  Pallas kernels  54.3 us (42%)
  starting transfers between devices  32.7 us (25%)
  waiting for transfers between devices  32 us (25%)
  local copies, waits for them, and re-layouts  4.65 us (4%)
  other arithmetic  2.27 us (2%)
  between operations  1.66 us (1%)
    pallas_call x1, Pallas kernels, run_own(): pl.pallas_call(own_kernel, out_shape=state(SLAB + 1), in_specs=[SM] * 4 +...  15.5 us
    pallas_call x2, Pallas kernels, run_halo(): pl.pallas_call(functools.partial(halo_kernel, which), out_shape=out, in_s...  15.1 us
    pallas_call x1, Pallas kernels, run_lists(): pl.pallas_call(lists_kernel, out_shape=[shape((n,), jnp.int32) for n in (...  13.9 us
    ppermute x3, waiting for transfers between devices, ring(): return [x] + [lax.ppermute(x, axis, route) for route in routes]  9.96 us
    all_to_all x1, starting transfers between devices, local(): kv = lax.all_to_all(kv_send, chips, 0, 0, tiled=True)  8.02 us
    all_to_all x1, starting transfers between devices, local(): back = lax.all_to_all(record, chips, 0, 0, tiled=True)  6.23 us
    all_to_all x1, starting transfers between devices, local(): q = lax.all_to_all(q_send, chips, 0, 0, tiled=True)  5.03 us
    all_to_all x1, waiting for transfers between devices, local(): q = lax.all_to_all(q_send, chips, 0, 0, tiled=True)  5.02 us
  transfers between devices with their start and end apart: 14, of which 10 were waited for; matrix products, arithmetic and copies ran while one was open for 5% of the time, Pallas kernels for 32%

profile of v4, /device:TPU:8, one launch (start us, length us, event | category | flops | bytes accessed | tf_op | source)
XLA Modules:
  0.0 127.6 jit_solution(788455796555109453)
XLA Ops:
  0.6 3.0 %prep_kv.1 = bf16[16,384,128]{2,1,0:T(8,128)(2,1)} custom-call(bf16[128,3072]{1,0:T(8,128)(2,1)} %k_hbm.1, bf16[128,3072]{1,0:T(8,128)(2,1)} %v_hbm.1), custom_call_target="tpu_custom_call" | custom-call | tf_op jit(solution)/shard_map/prep_kv/pallas_call | solution.py:571
  3.7 8.0 %all-to-all-start = ((bf16[16,384,128]{2,1,0:T(8,128)(2,1)}), bf16[16,384,128]{2,1,0:T(8,128)(2,1)S(1)}, u32[]{:S(2)}, u32[]{:S(2)}) async-start(bf16[16,384,128]{2,1,0:T(8,128)(2,1)} %prep_kv.1), calls=%async_computation | async-start | bytes 3145728 | tf_op jit(solution)/shard_map/all_to_all | solution.py:576
  11.7 0.1 copy.10
  11.9 0.1 copy.11
  12.1 0.1 copy.12
  12.2 0.9 pad_maximum_fusion
  13.1 0.1 pad_add_fusion.place_ref
  13.2 13.9 %lists.1 = (s32[128]{0:T(128)S(1)}, s32[680]{0:T(1024)S(1)}, s32[616]{0:T(1024)S(1)}, s32[616]{0:T(1024)S(1)}, s32[4]{0:T(128)S(1)}) custom-call(s32[2]{0:T(128)S(1)} %pad_add_fusion.place_ref, s32[128,128]{1,0:T(8,128)S(1)} %copy-done.2), custom_call_target="tpu_custom_call" | custom-call | flops 8000000000 | bytes 100000 | tf_op jit(solution)/shard_map/lists/pallas_call | solution.py:490
  27.1 0.9 broadcast_select_fusion
  28.0 0.9 slice.38
  29.0 0.1 dynamic-slice_bitcast_fusion.3
  29.1 0.1 copy.15
  29.2 1.0 dynamic-slice_bitcast_fusion.4
  30.2 0.1 copy.14
  30.3 0.9 dynamic-slice_bitcast_fusion
  31.3 0.2 maximum_bitcast_fusion
  31.5 0.1 maximum_bitcast_fusion.1.text_ref.text_hbm
  31.6 0.3 prep_q.1
  31.9 0.9 copy-done
  32.9 3.3 %all-to-all-done.kv_ref.kv_hbm = bf16[16,384,128]{2,1,0:T(8,128)(2,1)S(1)} async-done(((bf16[16,384,128]{2,1,0:T(8,128)(2,1)}), bf16[16,384,128]{2,1,0:T(8,128)(2,1)S(1)}, u32[]{:S(2)}, u32[]{:S(2)}) %all-to-all-start) | async-done | bytes 1572896 | tf_op jit(solution)/shard_map/all_to_all | solution.py:576
  36.2 5.0 %all-to-all-start.1 = ((bf16[16,256,128]{2,1,0:T(8,128)(2,1)}), bf16[16,256,128]{2,1,0:T(8,128)(2,1)S(1)}, u32[]{:S(2)}, u32[]{:S(2)}) async-start(bf16[16,256,128]{2,1,0:T(8,128)(2,1)} %copy-done), calls=%async_computation.1 | async-start | bytes 2097152 | tf_op jit(solution)/shard_map/all_to_all | solution.py:609
  41.2 3.5 %collective-permute-start.1 = (bf16[16,384,128]{2,1,0:T(8,128)(2,1)S(1)}, bf16[16,384,128]{2,1,0:T(8,128)(2,1)}, u32[]{:S(2)}, u32[]{:S(2)}) collective-permute-start(bf16[16,384,128]{2,1,0:T(8,128)(2,1)S(1)} %all-to-all-done.kv_ref.kv_hbm), channel_id=1, source_target_pairs={{0,32},{32,64},{64,96},{1,33},{33,65},{65,97},{2,34},{34,66},{66,9... | collective-permute-start | bytes 4718600 | tf_op jit(solution)/shard_map/ppermute | solution.py:607
  44.7 3.5 %collective-permute-start.2 = (bf16[16,384,128]{2,1,0:T(8,128)(2,1)S(1)}, bf16[16,384,128]{2,1,0:T(8,128)(2,1)}, u32[]{:S(2)}, u32[]{:S(2)}) collective-permute-start(bf16[16,384,128]{2,1,0:T(8,128)(2,1)S(1)} %all-to-all-done.kv_ref.kv_hbm), channel_id=1, source_target_pairs={{32,0},{64,32},{96,64},{33,1},{65,33},{97,65},{34,2},{66,34},{98,6... | collective-permute-start | bytes 4718600 | tf_op jit(solution)/shard_map/ppermute | solution.py:608
  48.9 0.1 pad_add_fusion.1.live_ref
  49.0 2.6 %text_keys.1 = bf16[4,144,128]{2,1,0:T(8,128)(2,1)S(1)} custom-call(s32[4]{0:T(128)S(1)} %pad_add_fusion.1.live_ref, bf16[16,384,128]{2,1,0:T(8,128)(2,1)S(1)} %all-to-all-done.kv_ref.kv_hbm, bf16[1,384,128]{2,1,0:T(8,128)(2,1)S(1)} %maximum_bitcast_fusion.1.text_ref.text_hbm, bf16[2,256,128]{2,1,0:T(8,128)(2,1)S(1)} %bitcast.37), custom_call_target="tpu_custom_call" | custom-call | flops 10000000 | bytes 100000 | tf_op jit(solution)/shard_map/text_keys/pallas_call | solution.py:525
  51.6 0.1 collective-permute-start.3
  51.7 1.4 %collective-permute-done.3 = bf16[4,144,128]{2,1,0:T(8,128)(2,1)S(1)} collective-permute-done((bf16[4,144,128]{2,1,0:T(8,128)(2,1)S(1)}, bf16[4,144,128]{2,1,0:T(8,128)(2,1)S(1)}, u32[]{:S(2)}, u32[]{:S(2)}) %collective-permute-start.3) | collective-permute-done | bytes 147488 | tf_op jit(solution)/shard_map/ppermute | solution.py:611
  53.1 5.0 %all-to-all-done.1.q_hbm = bf16[16,256,128]{2,1,0:T(8,128)(2,1)S(1)} async-done(((bf16[16,256,128]{2,1,0:T(8,128)(2,1)}), bf16[16,256,128]{2,1,0:T(8,128)(2,1)S(1)}, u32[]{:S(2)}, u32[]{:S(2)}) %all-to-all-start.1) | async-done | bytes 1048608 | tf_op jit(solution)/shard_map/all_to_all | solution.py:609
  58.1 2.7 %collective-permute-done.4.other_hbm.q_hbm = bf16[16,256,128]{2,1,0:T(8,128)(2,1)S(1)} collective-permute-done((bf16[16,256,128]{2,1,0:T(8,128)(2,1)S(1)}, bf16[16,256,128]{2,1,0:T(8,128)(2,1)S(1)}, u32[]{:S(2)}, u32[]{:S(2)}) %collective-permute-start.4) | collective-permute-done | bytes 1048608 | tf_op jit(solution)/shard_map/ppermute | solution.py:613
  60.7 15.5 %own_keys.1 = (f32[33,2,128,128]{3,2,1,0:T(8,128)S(1)}, f32[33,2,8,128]{3,2,1,0:T(8,128)S(1)}, f32[33,2,8,128]{3,2,1,0:T(8,128)S(1)}) custom-call(s32[128]{0:T(128)S(1)} %get-tuple-element.53.first_ref, s32[680]{0:T(1024)S(1)} %get-tuple-element.54.rest_ref, s32[4]{0:T(128)S(1)} %get-tuple-element.46.n_ref, s32[4]{0:T(128)S(1)} %pad_add_fusion.1.live_ref, ...), custom_call_target="tpu_custom_call" | custom-call | flops 100000000 | bytes 1000000 | tf_op jit(solution)/shard_map/own_keys/pallas_call | solution.py:502
  76.3 0.2 merge_text.1
  76.5 2.0 %collective-permute-done.1.down_hbm = bf16[16,384,128]{2,1,0:T(8,128)(2,1)} collective-permute-done((bf16[16,384,128]{2,1,0:T(8,128)(2,1)S(1)}, bf16[16,384,128]{2,1,0:T(8,128)(2,1)}, u32[]{:S(2)}, u32[]{:S(2)}) %collective-permute-start.1) | collective-permute-done | bytes 1572896 | tf_op jit(solution)/shard_map/ppermute | solution.py:607
  78.5 3.2 %collective-permute-done.2.up_hbm = bf16[16,384,128]{2,1,0:T(8,128)(2,1)} collective-permute-done((bf16[16,384,128]{2,1,0:T(8,128)(2,1)S(1)}, bf16[16,384,128]{2,1,0:T(8,128)(2,1)}, u32[]{:S(2)}, u32[]{:S(2)}) %collective-permute-start.2) | collective-permute-done | bytes 1572896 | tf_op jit(solution)/shard_map/ppermute | solution.py:608
  81.7 8.3 %halo_keys.3 = bf16[16,272,128]{2,1,0:T(8,128)(2,1)S(1)} custom-call(s32[616]{0:T(1024)S(1)} %get-tuple-element.65.list_ref, s32[4]{0:T(128)S(1)} %get-tuple-element.46.n_ref, bf16[16,384,128]{2,1,0:T(8,128)(2,1)} %collective-permute-done.1.down_hbm, bf16[16,384,128]{2,1,0:T(8,128)(2,1)} %collective-permute-done.2.up_hbm, ...), custom_call_target="tpu_custom_call" | custom-call | flops 2000000000 | bytes 10000000 | tf_op jit(solution)/shard_map/halo_keys/pallas_call | solution.py:551
  90.0 0.3 collective-permute-start.6
  90.3 3.2 %collective-permute-start.7 = (bf16[6,144,128]{2,1,0:T(8,128)(2,1)S(1)}, bf16[6,144,128]{2,1,0:T(8,128)(2,1)S(1)}, u32[]{:S(2)}, u32[]{:S(2)}) collective-permute-start(bf16[6,144,128]{2,1,0:T(8,128)(2,1)S(1)} %merge_text.1), channel_id=1, source_target_pairs={{0,16},{8,24},{16,0},{24,8},{1,17},{9,25},{17,1},{25,9},{2,18},{10... | collective-permute-start | bytes 663560 | tf_op jit(solution)/shard_map/ppermute | solution.py:622
  93.5 6.8 %halo_keys.2 = (f32[17,2,128,128]{3,2,1,0:T(8,128)S(1)}, f32[17,2,8,128]{3,2,1,0:T(8,128)S(1)}, f32[17,2,8,128]{3,2,1,0:T(8,128)S(1)}) custom-call(s32[616]{0:T(1024)S(1)} %get-tuple-element.45.list_ref, s32[4]{0:T(128)S(1)} %get-tuple-element.46.n_ref, bf16[16,384,128]{2,1,0:T(8,128)(2,1)} %collective-permute-done.1.down_hbm, ...), custom_call_target="tpu_custom_call" | custom-call | flops 2000000000 | bytes 10000000 | tf_op jit(solution)/shard_map/halo_keys/pallas_call | solution.py:551
  100.4 1.6 %merge_cores.1 = bf16[16,272,128]{2,1,0:T(8,128)(2,1)} custom-call(f32[17,2,128,128]{3,2,1,0:T(8,128)S(1)} %get-tuple-element.62.acc_ref, f32[17,2,8,128]{3,2,1,0:T(8,128)S(1)} %get-tuple-element.63.m_ref, f32[17,2,8,128]{3,2,1,0:T(8,128)S(1)} %get-tuple-element.64.l_ref, bf16[16,272,128]{2,1,0:T(8,128)(2,1)S(1)} %collective-permute-done.6.got_ref), custom_call_target="tpu_custom_call" | custom-call | tf_op jit(solution)/shard_map/merge_cores/pallas_call | solution.py:629
  102.0 6.2 %all-to-all-start.2 = ((bf16[16,272,128]{2,1,0:T(8,128)(2,1)}), bf16[16,272,128]{2,1,0:T(8,128)(2,1)S(1)}, u32[]{:S(2)}, u32[]{:S(2)}) async-start(bf16[16,272,128]{2,1,0:T(8,128)(2,1)} %merge_cores.1), calls=%async_computation.2 | async-start | bytes 2228224 | tf_op jit(solution)/shard_map/all_to_all | solution.py:633
  108.2 0.1 collective-permute-start.10
  108.3 2.0 %collective-permute-start.8 = (bf16[6,144,128]{2,1,0:T(8,128)(2,1)S(1)}, bf16[6,144,128]{2,1,0:T(8,128)(2,1)S(1)}, u32[]{:S(2)}, u32[]{:S(2)}) collective-permute-start(bf16[6,144,128]{2,1,0:T(8,128)(2,1)S(1)} %broadcast_select_fusion.1.refs_0_), channel_id=1, source_target_pairs={{0,32},{32,64},{64,96},{96,0},{1,33},{33,65},{65,97},{97,1},{2,34}... | collective-permute-start | bytes 663560 | tf_op jit(solution)/shard_map/ppermute | solution.py:478
  110.3 0.7 collective-permute-start.9
  111.0 4.0 %collective-permute-done.10.refs_3_ = bf16[6,144,128]{2,1,0:T(8,128)(2,1)S(1)} collective-permute-done((bf16[6,144,128]{2,1,0:T(8,128)(2,1)S(1)}, bf16[6,144,128]{2,1,0:T(8,128)(2,1)S(1)}, u32[]{:S(2)}, u32[]{:S(2)}) %collective-permute-start.10) | collective-permute-done | bytes 221216 | tf_op jit(solution)/shard_map/ppermute | solution.py:478
  115.1 4.1 %collective-permute-done.8.refs_1_ = bf16[6,144,128]{2,1,0:T(8,128)(2,1)S(1)} collective-permute-done((bf16[6,144,128]{2,1,0:T(8,128)(2,1)S(1)}, bf16[6,144,128]{2,1,0:T(8,128)(2,1)S(1)}, u32[]{:S(2)}, u32[]{:S(2)}) %collective-permute-start.8) | collective-permute-done | bytes 221216 | tf_op jit(solution)/shard_map/ppermute | solution.py:478
  119.2 1.8 %collective-permute-done.9.refs_2_ = bf16[6,144,128]{2,1,0:T(8,128)(2,1)S(1)} collective-permute-done((bf16[6,144,128]{2,1,0:T(8,128)(2,1)S(1)}, bf16[6,144,128]{2,1,0:T(8,128)(2,1)S(1)}, u32[]{:S(2)}, u32[]{:S(2)}) %collective-permute-start.9) | collective-permute-done | bytes 221216 | tf_op jit(solution)/shard_map/ppermute | solution.py:478
  121.0 1.0 final_text.1
  122.0 4.5 %all-to-all-done.2.got_ref = bf16[16,272,128]{2,1,0:T(8,128)(2,1)S(1)} async-done(((bf16[16,272,128]{2,1,0:T(8,128)(2,1)}), bf16[16,272,128]{2,1,0:T(8,128)(2,1)S(1)}, u32[]{:S(2)}, u32[]{:S(2)}) %all-to-all-start.2) | async-done | bytes 1114144 | tf_op jit(solution)/shard_map/all_to_all | solution.py:633
  126.4 1.2 final.1
  (24 shorter events, 0.2 us)
Async XLA Ops:
  3.7 8.1 %copy-start.3 = (bf16[256,384]{1,0:T(8,128)(2,1)S(1)}, bf16[256,384]{1,0:T(8,128)(2,1)}, u32[]{:S(2)}) copy-start(bf16[256,384]{1,0:T(8,128)(2,1)} %param.11) | copy-start | bytes 589828
  3.7 8.2 %copy-start.4 = (bf16[256,384]{1,0:T(8,128)(2,1)S(1)}, bf16[256,384]{1,0:T(8,128)(2,1)}, u32[]{:S(2)}) copy-start(bf16[256,384]{1,0:T(8,128)(2,1)} %param.12) | copy-start | bytes 589828
  3.7 8.4 %copy-start.5 = (bf16[256,384]{1,0:T(8,128)(2,1)S(1)}, bf16[256,384]{1,0:T(8,128)(2,1)}, u32[]{:S(2)}) copy-start(bf16[256,384]{1,0:T(8,128)(2,1)} %param.13) | copy-start | bytes 589828
  3.7 32.5 %all-to-all-start = ((bf16[16,384,128]{2,1,0:T(8,128)(2,1)}), bf16[16,384,128]{2,1,0:T(8,128)(2,1)S(1)}, u32[]{:S(2)}, u32[]{:S(2)}) async-start(bf16[16,384,128]{2,1,0:T(8,128)(2,1)} %prep_kv.1), calls=%async_computation | async-start | bytes 3145728 | tf_op jit(solution)/shard_map/all_to_all | solution.py:576
  11.7 1.4 %copy-start.2 = (s32[128,128]{1,0:T(8,128)S(1)}, s32[128,128]{1,0:T(8,128)}, u32[]{:S(2)}) copy-start(s32[128,128]{1,0:T(8,128)} %mask_ref) | copy-start | bytes 196612
  13.1 14.0 %collective-permute-start = (bf16[3,256,384]{1,2,0:T(8,128)(2,1)}, bf16[3,256,384]{1,2,0:T(8,128)(2,1)}, u32[]{:S(2)}, u32[]{:S(2)}) collective-permute-start(bf16[3,256,384]{1,2,0:T(8,128)(2,1)} %pad_maximum_fusion), channel_id=1, source_target_pairs={{0,1},{1,0},{2,3},{3,2},{4,5},{5,4},{6,7},{7,6},{8,9},{9,8},{10,11... | collective-permute-start | bytes 1769480 | tf_op jit(solution)/shard_map/ppermute | solution.py:580
  27.1 4.5 %copy-start.1 = (bf16[128,3072]{1,0:T(8,128)(2,1)S(1)}, bf16[128,3072]{1,0:T(8,128)(2,1)}, u32[]{:S(2)}) copy-start(bf16[128,3072]{1,0:T(8,128)(2,1)} %q_ref) | copy-start | bytes 2359300
  31.9 1.0 copy-start
  36.2 21.9 %all-to-all-start.1 = ((bf16[16,256,128]{2,1,0:T(8,128)(2,1)}), bf16[16,256,128]{2,1,0:T(8,128)(2,1)S(1)}, u32[]{:S(2)}, u32[]{:S(2)}) async-start(bf16[16,256,128]{2,1,0:T(8,128)(2,1)} %copy-done), calls=%async_computation.1 | async-start | bytes 2097152 | tf_op jit(solution)/shard_map/all_to_all | solution.py:609
  41.2 37.3 %collective-permute-start.1 = (bf16[16,384,128]{2,1,0:T(8,128)(2,1)S(1)}, bf16[16,384,128]{2,1,0:T(8,128)(2,1)}, u32[]{:S(2)}, u32[]{:S(2)}) collective-permute-start(bf16[16,384,128]{2,1,0:T(8,128)(2,1)S(1)} %all-to-all-done.kv_ref.kv_hbm), channel_id=1, source_target_pairs={{0,32},{32,64},{64,96},{1,33},{33,65},{65,97},{2,34},{34,66},{66,9... | collective-permute-start | bytes 4718600 | tf_op jit(solution)/shard_map/ppermute | solution.py:607
  44.7 37.0 %collective-permute-start.2 = (bf16[16,384,128]{2,1,0:T(8,128)(2,1)S(1)}, bf16[16,384,128]{2,1,0:T(8,128)(2,1)}, u32[]{:S(2)}, u32[]{:S(2)}) collective-permute-start(bf16[16,384,128]{2,1,0:T(8,128)(2,1)S(1)} %all-to-all-done.kv_ref.kv_hbm), channel_id=1, source_target_pairs={{32,0},{64,32},{96,64},{33,1},{65,33},{97,65},{34,2},{66,34},{98,6... | collective-permute-start | bytes 4718600 | tf_op jit(solution)/shard_map/ppermute | solution.py:608
  51.6 1.5 %collective-permute-start.3 = (bf16[4,144,128]{2,1,0:T(8,128)(2,1)S(1)}, bf16[4,144,128]{2,1,0:T(8,128)(2,1)S(1)}, u32[]{:S(2)}, u32[]{:S(2)}) collective-permute-start(bf16[4,144,128]{2,1,0:T(8,128)(2,1)S(1)} %text_keys.1), channel_id=1, source_target_pairs={{0,1},{1,0},{2,3},{3,2},{4,5},{5,4},{6,7},{7,6},{8,9},{9,8},{10,11... | collective-permute-start | bytes 442376 | tf_op jit(solution)/shard_map/ppermute | solution.py:611
  58.1 2.7 %collective-permute-start.4 = (bf16[16,256,128]{2,1,0:T(8,128)(2,1)S(1)}, bf16[16,256,128]{2,1,0:T(8,128)(2,1)S(1)}, u32[]{:S(2)}, u32[]{:S(2)}) collective-permute-start(bf16[16,256,128]{2,1,0:T(8,128)(2,1)S(1)} %all-to-all-done.1.q_hbm), channel_id=1, source_target_pairs={{0,1},{1,0},{2,3},{3,2},{4,5},{5,4},{6,7},{7,6},{8,9},{9,8},{10,11... | collective-permute-start | bytes 3145736 | tf_op jit(solution)/shard_map/ppermute | solution.py:613
  58.1 18.2 %collective-permute-start.5 = (bf16[8,144,128]{2,1,0:T(8,128)(2,1)S(1)}, bf16[8,144,128]{2,1,0:T(8,128)(2,1)S(1)}, u32[]{:S(2)}, u32[]{:S(2)}) collective-permute-start(bf16[8,144,128]{2,1,0:T(8,128)(2,1)S(1)} %pad_maximum_fusion.1.here_ref), channel_id=1, source_target_pairs={{0,8},{8,0},{16,24},{24,16},{1,9},{9,1},{17,25},{25,17},{2,10},{10... | collective-permute-start | bytes 884744 | tf_op jit(solution)/shard_map/ppermute | solution.py:614
  90.0 10.3 %collective-permute-start.6 = (bf16[16,272,128]{2,1,0:T(8,128)(2,1)S(1)}, bf16[16,272,128]{2,1,0:T(8,128)(2,1)S(1)}, u32[]{:S(2)}, u32[]{:S(2)}) collective-permute-start(bf16[16,272,128]{2,1,0:T(8,128)(2,1)S(1)} %halo_keys.3), channel_id=1, source_target_pairs={{0,1},{1,0},{2,3},{3,2},{4,5},{5,4},{6,7},{7,6},{8,9},{9,8},{10,11... | collective-permute-start | bytes 3342344 | tf_op jit(solution)/shard_map/ppermute | solution.py:626
  90.3 10.0 %collective-permute-start.7 = (bf16[6,144,128]{2,1,0:T(8,128)(2,1)S(1)}, bf16[6,144,128]{2,1,0:T(8,128)(2,1)S(1)}, u32[]{:S(2)}, u32[]{:S(2)}) collective-permute-start(bf16[6,144,128]{2,1,0:T(8,128)(2,1)S(1)} %merge_text.1), channel_id=1, source_target_pairs={{0,16},{8,24},{16,0},{24,8},{1,17},{9,25},{17,1},{25,9},{2,18},{10... | collective-permute-start | bytes 663560 | tf_op jit(solution)/shard_map/ppermute | solution.py:622
  102.0 24.5 %all-to-all-start.2 = ((bf16[16,272,128]{2,1,0:T(8,128)(2,1)}), bf16[16,272,128]{2,1,0:T(8,128)(2,1)S(1)}, u32[]{:S(2)}, u32[]{:S(2)}) async-start(bf16[16,272,128]{2,1,0:T(8,128)(2,1)} %merge_cores.1), calls=%async_computation.2 | async-start | bytes 2228224 | tf_op jit(solution)/shard_map/all_to_all | solution.py:633
  108.2 6.9 %collective-permute-start.10 = (bf16[6,144,128]{2,1,0:T(8,128)(2,1)S(1)}, bf16[6,144,128]{2,1,0:T(8,128)(2,1)S(1)}, u32[]{:S(2)}, u32[]{:S(2)}) collective-permute-start(bf16[6,144,128]{2,1,0:T(8,128)(2,1)S(1)} %broadcast_select_fusion.1.refs_0_), channel_id=1, source_target_pairs={{0,96},{32,0},{64,32},{96,64},{1,97},{33,1},{65,33},{97,65},{2,98}... | collective-permute-start | bytes 663560 | tf_op jit(solution)/shard_map/ppermute | solution.py:478
  108.3 10.9 %collective-permute-start.8 = (bf16[6,144,128]{2,1,0:T(8,128)(2,1)S(1)}, bf16[6,144,128]{2,1,0:T(8,128)(2,1)S(1)}, u32[]{:S(2)}, u32[]{:S(2)}) collective-permute-start(bf16[6,144,128]{2,1,0:T(8,128)(2,1)S(1)} %broadcast_select_fusion.1.refs_0_), channel_id=1, source_target_pairs={{0,32},{32,64},{64,96},{96,0},{1,33},{33,65},{65,97},{97,1},{2,34}... | collective-permute-start | bytes 663560 | tf_op jit(solution)/shard_map/ppermute | solution.py:478
  110.3 10.7 %collective-permute-start.9 = (bf16[6,144,128]{2,1,0:T(8,128)(2,1)S(1)}, bf16[6,144,128]{2,1,0:T(8,128)(2,1)S(1)}, u32[]{:S(2)}, u32[]{:S(2)}) collective-permute-start(bf16[6,144,128]{2,1,0:T(8,128)(2,1)S(1)} %broadcast_select_fusion.1.refs_0_), channel_id=1, source_target_pairs={{0,64},{32,96},{64,0},{96,32},{1,65},{33,97},{65,1},{97,33},{2,66}... | collective-permute-start | bytes 663560 | tf_op jit(solution)/shard_map/ppermute | solution.py:478
